TPU v7x, 128 devices: a whole 4x4x4 slice. The times are simulated.
128 devices in a mesh: row: 16 (over x, y), col: 8 (over z, core).
Axes of the slice: x: 4, y: 4, z: 4, core: 2. Of those that a mesh axis runs over, the one named last changes fastest.
Arguments:
- tile_values: bfloat16 [128, 8, 4, 256, 256], P('row', 'col'), may hold values from 0 to 1, as said below
- tile_cols: int32 [128, 8, 4], P('row', 'col'), may hold values from 0 to 15, as said below
- row_counts: int32 [128, 8], P('row', 'col'), may hold values from 1 to 4, as said below
- start_basis: bfloat16 [64, 32768], P(None, ('row', 'col')), may hold values from -6 to 6
Outputs:
- embedding: float32 [64, 32768], P(None, ('row', 'col'))
- degrees: float32 [32768], P(('row', 'col'))
Inputs may be any that keep to these rules, and one draw needn't show every extreme that they name: `tile_values`: entries are positive. `tile_cols`: within one tile row and column class the numbers of the 4 slots are distinct. Over the 8 tile rows that one device stores in its column class, no number occurs in more than 2 slots, live or empty, and one number, the same on every device of that column class, occurs in 2 live slots. `row_counts`: some entry equals 4.
All inputs are finite; a program needn't handle non-finite values.
Results may differ from a plain program's by a relative error of at most 0.009.
Values may be sent and summed in bfloat16 or wider, within the bound.
No kernel may reach another device: no remote copies, remote signals or barrier semaphores. Data moves between devices by JAX's collectives and lax.ppermute only.
A program may use at most 64 MiB of HBM per device.

v0:
```python
import jax
import jax.numpy as jnp
from jax import lax
from jax.sharding import PartitionSpec as P

STEPS = 3


EPSILON = 1e-06
RESTART = 0.2


def local(tile_values, tile_cols, row_counts, start_basis):
    row_devices = lax.axis_size("row")
    col_devices = lax.axis_size("col")
    tiles = tile_values[:, 0]
    columns = tile_cols[:, 0]
    counts = row_counts[:, 0]
    slot_count = tiles.shape[1]
    tile_size = tiles.shape[2]
    total_cells = row_devices * col_devices * tile_size
    live_mask = jnp.arange(slot_count)[None, :] < counts[:, None]
    bucket_hot = (columns[:, :, None] == jnp.arange(row_devices)[None, None, :]) & live_mask[
        :, :, None
    ]
    arrived = (
        lax.all_to_all(tile_values, "col", split_axis=0, concat_axis=1, tiled=True),
        lax.all_to_all(
            tile_cols.astype(jnp.bfloat16), "col", split_axis=0, concat_axis=1, tiled=True
        ),
        lax.all_to_all(
            row_counts.astype(jnp.bfloat16), "col", split_axis=0, concat_axis=1, tiled=True
        ),
    )
    in_tiles = arrived[0][0]
    in_columns = arrived[1][0].astype(jnp.int32)
    in_counts = arrived[2][0].astype(jnp.int32)
    in_mask = (jnp.arange(slot_count)[None, :] < in_counts[:, None]).astype(jnp.bfloat16)
    in_panel = in_columns * col_devices + jnp.arange(col_devices, dtype=jnp.int32)[:, None]
    most = max(2, col_devices * slot_count // row_devices)
    flat_hot = bucket_hot.reshape(col_devices * slot_count, row_devices).astype(jnp.int32)
    earlier = jnp.cumsum(flat_hot, axis=0) - flat_hot
    placement = (flat_hot[:, :, None] == 1) & (
        earlier[:, :, None] == jnp.arange(most)[None, None, :]
    )
    flat_tiles = tiles.reshape(col_devices * slot_count, tile_size, tile_size)
    outgoing = jnp.einsum(
        "qbm,quv->bmuv",
        placement.astype(jnp.bfloat16),
        flat_tiles,
        preferred_element_type=jnp.float32,
    ).astype(jnp.bfloat16)
    source_row = jnp.repeat(jnp.arange(col_devices), slot_count).astype(jnp.float32)
    outgoing_rows = jnp.sum(
        placement.astype(jnp.float32) * source_row[:, None, None], axis=0
    ).astype(jnp.bfloat16)
    mirrored, mirror_rows = (
        lax.all_to_all(outgoing, "row", split_axis=0, concat_axis=0, tiled=True),
        lax.all_to_all(outgoing_rows, "row", split_axis=0, concat_axis=0, tiled=True),
    )
    mirror_panel = jnp.arange(row_devices, dtype=jnp.int32)[
        :, None
    ] * col_devices + mirror_rows.astype(jnp.int32)
    degrees = jnp.einsum("csuv,cs->u", in_tiles, in_mask, preferred_element_type=jnp.float32)
    degrees = degrees + jnp.sum(mirrored, axis=(0, 1, 2), dtype=jnp.float32)
    volume = lax.psum(jnp.sum(degrees), ("row", "col"))
    inv_root = 1.0 / jnp.sqrt(degrees + volume / total_cells)
    leading = jnp.sqrt(degrees / volume)
    start_wide = start_basis.astype(jnp.float32)
    current = start_basis
    for repeat in range(STEPS):
        weighted = (inv_root[None, :] * current.astype(jnp.float32)).astype(jnp.bfloat16)
        gathered = lax.all_gather(weighted[None], ("row", "col"), axis=0, tiled=True)
        picked = gathered[in_panel] * in_mask[:, :, None, None]
        result = jnp.einsum("cskv,csuv->ku", picked, in_tiles, preferred_element_type=jnp.float32)
        applied = inv_root[None, :] * (
            result
            + jnp.einsum(
                "rmku,rmuv->kv",
                gathered[mirror_panel],
                mirrored,
                preferred_element_type=jnp.float32,
            )
        )
        projection = lax.psum(
            jnp.sum(current.astype(jnp.float32) * leading[None, :], axis=1), ("row", "col")
        )
        residual = applied - projection[:, None] * leading[None, :]
        norms = lax.psum(jnp.sum(residual * residual, axis=1), ("row", "col"))
        scaled = residual / jnp.sqrt(norms / total_cells + EPSILON)[:, None]
        blend = (1.0 - RESTART) * scaled + RESTART * start_wide
        current = blend.astype(jnp.bfloat16) if repeat + 1 < STEPS else blend
    return (current, degrees)


def solution(mesh):
    placed = (
        P("row", "col", None, None, None),
        P("row", "col", None),
        P("row", "col"),
        P(None, ("row", "col")),
    )
    return jax.shard_map(
        local,
        mesh=mesh,
        in_specs=placed,
        out_specs=(P(None, ("row", "col")), P(("row", "col"))),
        check_vma=False,
    )
```

profile of v0, /device:TPU:1, one launch (start us, length us, event | category | flops | bytes accessed | tf_op | source)
XLA Modules:
  0.0 662.7 jit_solution(247240367015029430)
XLA Ops:
  7.9 11.2 %all_to_all.42 = bf16[8,1,1]{2,1,0:T(2,128)(2,1)S(1)} all-to-all(bf16[8,1,1]{2,1,0:T(2,128)(2,1)S(1)} %copy.65), channel_id=1, replica_groups=mesh['row'=16,'col'=8] {'col'}, dimensions={0} | all-to-all | bytes 32 | tf_op jit(solution)/shard_map/all_to_all | solution.py:31
  19.1 5.2 all-to-all-start
  25.1 4.7 fusion.15
  29.8 3.5 copy.70
  33.3 40.0 %all-to-all-done = bf16[8,1,4,256,256]{4,3,2,1,0:T(8,128)(2,1)} async-done(((bf16[8,1,4,256,256]{4,3,2,1,0:T(8,128)(2,1)}), bf16[8,1,4,256,256]{4,3,2,1,0:T(8,128)(2,1)}, u32[]{:S(2)}, u32[]{:S(2)}) %all-to-all-start) | async-done | bytes 4194336 | tf_op jit(solution)/shard_map/all_to_all | solution.py:27
  73.3 6.8 %all-to-all-start.2 = ((bf16[16,2,256,256]{3,2,1,0:T(8,128)(2,1)}), bf16[16,2,256,256]{3,2,1,0:T(8,128)(2,1)}, u32[]{:S(2)}, u32[]{:S(2)}) async-start(bf16[16,2,256,256]{3,2,1,0:T(8,128)(2,1)} %copy.70), calls=%async_computation.2 | async-start | bytes 8388608 | tf_op jit(solution)/shard_map/all_to_all | solution.py:58
  80.5 3.4 convert_reduce_fusion.1
  84.0 55.0 %all-to-all-done.2 = bf16[16,2,256,256]{3,2,1,0:T(8,128)(2,1)} async-done(((bf16[16,2,256,256]{3,2,1,0:T(8,128)(2,1)}), bf16[16,2,256,256]{3,2,1,0:T(8,128)(2,1)}, u32[]{:S(2)}, u32[]{:S(2)}) %all-to-all-start.2) | async-done | bytes 4194336 | tf_op jit(solution)/shard_map/all_to_all | solution.py:58
  139.0 3.3 convert_reduce_fusion
  142.9 69.2 %psum.49 = f32[]{:T(128)} all-reduce(f32[]{:T(128)} %get-tuple-element.6), channel_id=1, replica_groups=mesh['row'=16,'col'=8] {'row','col'}, use_global_device_ids=true, to_apply=%region_4.5 | all-reduce | flops 1 | bytes 8 | tf_op jit(solution)/shard_map/psum | solution.py:66
  214.9 4.2 all-to-all-start.3
  220.0 3.7 all-to-all-done.3
  223.7 4.7 all-to-all-start.4
  228.7 6.1 all-to-all-done.4
  235.1 63.9 %psum.50 = f32[64]{0:T(128)S(1)} all-reduce(f32[64]{0:T(128)S(1)} %get-tuple-element.8), channel_id=1, replica_groups=mesh['row'=16,'col'=8] {'row','col'}, use_global_device_ids=true, to_apply=%region_7.8 | all-reduce | flops 64 | bytes 512 | tf_op jit(solution)/shard_map/psum | solution.py:85
  299.1 2.8 gather_fusion
  301.9 2.8 gather_fusion.1
  304.7 3.6 fusion.27
  308.3 3.1 multiply_reduce_fusion.2
  311.4 62.7 %psum.51 = f32[64]{0:T(128)S(1)} all-reduce(f32[64]{0:T(128)S(1)} %get-tuple-element.16), channel_id=1, replica_groups=mesh['row'=16,'col'=8] {'row','col'}, use_global_device_ids=true, to_apply=%region_9.10 | all-reduce | flops 64 | bytes 512 | tf_op jit(solution)/shard_map/psum | solution.py:89
  375.0 64.8 %psum.52 = f32[64]{0:T(128)S(1)} all-reduce(f32[64]{0:T(128)S(1)} %get-tuple-element.4), channel_id=1, replica_groups=mesh['row'=16,'col'=8] {'row','col'}, use_global_device_ids=true, to_apply=%region_11.12 | all-reduce | flops 64 | bytes 512 | tf_op jit(solution)/shard_map/psum | solution.py:85
  439.8 2.8 gather_fusion.2
  442.6 2.8 gather_fusion.3
  445.4 3.6 fusion.30
  449.0 3.1 multiply_reduce_fusion.1
  452.1 62.7 %psum.53 = f32[64]{0:T(128)S(1)} all-reduce(f32[64]{0:T(128)S(1)} %get-tuple-element.18), channel_id=1, replica_groups=mesh['row'=16,'col'=8] {'row','col'}, use_global_device_ids=true, to_apply=%region_13.14 | all-reduce | flops 64 | bytes 512 | tf_op jit(solution)/shard_map/psum | solution.py:89
  515.6 64.8 %psum.54 = f32[64]{0:T(128)S(1)} all-reduce(f32[64]{0:T(128)S(1)} %get-tuple-element.2), channel_id=1, replica_groups=mesh['row'=16,'col'=8] {'row','col'}, use_global_device_ids=true, to_apply=%region_15.16 | all-reduce | flops 64 | bytes 512 | tf_op jit(solution)/shard_map/psum | solution.py:85
  580.4 2.8 gather_fusion.4
  583.2 2.8 gather_fusion.5
  586.0 3.6 fusion.33
  589.6 3.1 multiply_reduce_fusion
  592.7 62.7 %psum.55 = f32[64]{0:T(128)S(1)} all-reduce(f32[64]{0:T(128)S(1)} %get-tuple-element.20), channel_id=1, replica_groups=mesh['row'=16,'col'=8] {'row','col'}, use_global_device_ids=true, to_apply=%region_17.18 | all-reduce | flops 64 | bytes 512 | tf_op jit(solution)/shard_map/psum | solution.py:89
  (59 shorter events, 8.7 us)
Async XLA Ops:
  19.1 5.3 copy-start.1
  19.1 5.4 copy-start.3
  19.1 54.2 %all-to-all-start = ((bf16[8,1,4,256,256]{4,3,2,1,0:T(8,128)(2,1)}), bf16[8,1,4,256,256]{4,3,2,1,0:T(8,128)(2,1)}, u32[]{:S(2)}, u32[]{:S(2)}) async-start(bf16[8,1,4,256,256]{4,3,2,1,0:T(8,128)(2,1)} %param.4), calls=%async_computation | async-start | bytes 8388608 | tf_op jit(solution)/shard_map/all_to_all | solution.py:27
  73.3 65.7 %all-to-all-start.2 = ((bf16[16,2,256,256]{3,2,1,0:T(8,128)(2,1)}), bf16[16,2,256,256]{3,2,1,0:T(8,128)(2,1)}, u32[]{:S(2)}, u32[]{:S(2)}) async-start(bf16[16,2,256,256]{3,2,1,0:T(8,128)(2,1)} %copy.70), calls=%async_computation.2 | async-start | bytes 8388608 | tf_op jit(solution)/shard_map/all_to_all | solution.py:58
  80.1 219.0 %all-gather.7.cloned.1.call-start = ((), (), s32[]{:S(2)}) async-start(), calls=%async_computation.5 | async-start | bytes 4227072 | tf_op jit(solution)/shard_map/all_gather | solution.py:73
  80.5 133.0 %copy-start = (bf16[64,256]{1,0:T(8,128)(2,1)S(1)}, bf16[64,256]{1,0:T(8,128)(2,1)}, u32[]{:S(2)}) copy-start(bf16[64,256]{1,0:T(8,128)(2,1)} %param.7) | copy-start | bytes 98308
  142.9 165.4 %copy-start.2 = (f32[256]{0:T(256)}, f32[256]{0:T(256)S(1)}, u32[]{:S(2)}) copy-start(f32[256]{0:T(256)S(1)} %get-tuple-element.7) | copy-start | bytes 3076
  214.9 8.8 %all-to-all-start.3 = ((bf16[8,1,4]{2,1,0:T(2,128)(2,1)}), bf16[8,1,4]{2,1,0:T(2,128)(2,1)S(1)}, u32[]{:S(2)}, u32[]{:S(2)}) async-start(bf16[8,1,4]{2,1,0:T(2,128)(2,1)} %copy.71), calls=%async_computation.3 | async-start | bytes 8192 | tf_op jit(solution)/shard_map/all_to_all | solution.py:28
  223.7 11.1 %all-to-all-start.4 = ((bf16[16,1,2]{2,1,0:T(2,128)(2,1)}), bf16[16,1,2]{2,1,0:T(2,128)(2,1)S(1)}, u32[]{:S(2)}, u32[]{:S(2)}) async-start(bf16[16,1,2]{2,1,0:T(2,128)(2,1)} %copy.74), calls=%async_computation.4 | async-start | bytes 16384 | tf_op jit(solution)/shard_map/all_to_all | solution.py:59
  228.4 211.4 %all-gather.9.cloned.1.call-start = ((), (), s32[]{:S(2)}) async-start(), calls=%async_computation.6 | async-start | bytes 4227072 | tf_op jit(solution)/shard_map/all_gather | solution.py:73
  375.0 205.4 %all-gather.11.cloned.1.call-start = ((), (), s32[]{:S(2)}) async-start(), calls=%async_computation.7 | async-start | bytes 4227072 | tf_op jit(solution)/shard_map/all_gather | solution.py:73
Sparse Core Ops, SparseCore 0:
  214.3 64.7 all-gather.6
  375.1 64.4 all-gather.8
  515.8 64.3 all-gather.10
where the time goes:
time: 664 us; the launch traced here: 663 us
  blocking collectives  462 us (70%)
  waiting for transfers between devices  105 us (16%)
  matrix products  25.1 us (4%)
  local copies, waits for them, and re-layouts  22.8 us (3%)
  starting transfers between devices  21.1 us (3%)
  between operations  14.6 us (2%)
  other arithmetic  12.4 us (2%)
    psum x3, blocking collectives, local(): lax.psum(jnp.sum(current.astype(jnp.float32) * leading[None, :], axis=1),...  193 us
    psum x3, blocking collectives, local(): norms = lax.psum(jnp.sum(residual * residual, axis=1), ('row', 'col'))  188 us
    psum x1, blocking collectives, local(): volume = lax.psum(jnp.sum(degrees), ('row', 'col'))  69.2 us
    all_to_all x1, waiting for transfers between devices, local(): lax.all_to_all(outgoing, 'row', split_axis=0, concat_axis=0, tiled=True)  55 us
    all_to_all x1, waiting for transfers between devices, local(): lax.all_to_all(tile_values, 'col', split_axis=0, concat_axis=1, tiled=True)  40 us
  transfers between devices with their start and end apart: 7, of which 4 were waited for; matrix products, arithmetic and copies ran while one was open for 2% of the time, Pallas kernels for 0%

commit v1 on v0

v1 whole, which is shorter than its diff:
```python
import jax
import jax.numpy as jnp
from jax import lax
from jax.experimental import pallas as pl
from jax.experimental.pallas import tpu as pltpu
from jax.sharding import PartitionSpec as P

STEPS = 3
EPSILON = 1e-06
RESTART = 0.2

F32 = jnp.float32
BF16 = jnp.bfloat16
VMEM = pl.BlockSpec(memory_space=pltpu.VMEM)
SMEM = pl.BlockSpec(memory_space=pltpu.SMEM)
PARAMS = pltpu.CompilerParams(vmem_limit_bytes=40 * 1024 * 1024)
EXTRA = 16


def nn(a, b):
    return lax.dot_general(a, b, (((1,), (0,)), ((), ())), preferred_element_type=F32)


def nt(a, b):
    return lax.dot_general(a, b, (((1,), (1,)), ((), ())), preferred_element_type=F32)


def call(kernel, outs, ins, out_specs=None, scratch=(), flops=1e6, moved=1e6):
    return pl.pallas_call(
        kernel,
        out_shape=outs,
        in_specs=ins,
        out_specs=out_specs if out_specs is not None else jax.tree.map(lambda _: VMEM, outs),
        scratch_shapes=list(scratch),
        compiler_params=PARAMS,
        cost_estimate=pl.CostEstimate(
            flops=int(flops), bytes_accessed=int(moved), transcendentals=0
        ),
    )


def to_rows(first, second):
    cells = first.shape[0]
    lane = lax.broadcasted_iota(jnp.int32, (cells, 128), 1)
    wide = jnp.where(lane == 0, first, jnp.where(lane == 1, second, 0.0))
    wide = jnp.concatenate([wide, jnp.zeros((128 - cells, 128), F32)], axis=0)
    return wide.T[:8]


def to_columns(block, cells):
    wide = jnp.concatenate([block, jnp.zeros((120, 128), F32)], axis=0).T
    return wide[:cells, 0:1], wide[:cells, 1:2]


def degree_kernel(place, columns, counts, tiles, message, table, row_sums, col_sums, used):
    panels, slots, tile = tiles.shape[0], tiles.shape[1], tiles.shape[2]
    row_devices = message.shape[0]
    mine_row, mine_col = place[0], place[1]

    for b in range(row_devices):
        used[b] = 0
    for q in range(panels * slots):
        b = columns[q]
        table[2 * b + used[b]] = q
        used[b] = used[b] + 1

    ones = jnp.ones((16, tile), BF16)
    for i in range(panels):
        total = jnp.zeros((16, tile), F32)
        for s in range(slots):
            live = s < counts[i]
            weight = jnp.where(live, ones, jnp.zeros_like(ones))
            value = tiles[i, s]
            total = total + nt(weight, value)
            col_sums[i * slots + s] = nn(weight, value)[:8]
        row_sums[i : i + 1, :] = total[:1]
    rows = row_sums[...]
    everything = jnp.sum(jnp.sum(rows, axis=1, keepdims=True), axis=0, keepdims=True)
    for b in range(row_devices):
        part = col_sums[table[2 * b]] + col_sums[table[2 * b + 1]]
        at = lax.broadcasted_iota(jnp.int32, part.shape, 0)
        part = jnp.where(at == mine_col, part, 0.0) + jnp.where(b == mine_row, rows, 0.0)
        message[b, :, :tile] = part
        message[b, :, tile:] = jnp.broadcast_to(everything, (part.shape[0], 128))


def pack(values, dots, many, one):
    cells = values.shape[0]
    body = values.astype(BF16)
    high = dots.astype(BF16)
    low = (dots - high.astype(F32)).astype(BF16)
    tail = jnp.concatenate([high, low], axis=0)
    tail = jnp.concatenate([tail, jnp.zeros_like(tail)], axis=1)
    one[...] = body
    for b in range(many.shape[0]):
        many[b, :cells] = body
        many[b, cells:] = tail


def start_kernel(total_cells, parts, start, degrees, scales, many, one):
    tile = start.shape[1]
    sums = jnp.sum(parts[...], axis=0, keepdims=True)
    degree = sums[:, :tile]
    volume = 2.0 * sums[:, tile : tile + 1]
    inv_root = 1.0 / jnp.sqrt(degree + volume / total_cells)
    leading = jnp.sqrt(degree / volume)
    degrees[...] = degree
    scales[0:1, :] = inv_root
    scales[1:2, :] = leading
    wide = start[...].astype(F32)
    dot = jnp.sum(wide * leading, axis=1, keepdims=True)
    pack(wide * inv_root, to_rows(dot, jnp.zeros_like(dot)), many, one)


def backward_kernel(place, table, counts, tiles, own, pair, far1, far3, far2, out):
    slots = tiles.shape[1]
    zs = tiles.shape[0] // 2
    mine_col = place[1]
    z, core = mine_col // 2, mine_col % 2
    panels = tiles.shape[0]
    buffer = out[1]
    result = out[0]
    for k, source in ((0, None), (1, far1), (2, far2), (3, far3)):
        at = (z + zs - k) % zs
        same = own[...] if source is None else source[0]
        other = pair[...] if source is None else source[1]
        buffer[2 * at + core] = same
        buffer[2 * at + 1 - core] = other
    for b in range(result.shape[0]):
        total = None
        for m in range(2):
            q = table[2 * b + m]
            i = q // slots
            s = q % slots
            panel = buffer[i]
            panel = jnp.where(s < counts[i], panel, jnp.zeros_like(panel))
            part = nn(panel, tiles[i, s])
            total = part if total is None else total + part
        result[b] = total


def forward_kernel(place, columns, counts, tiles, gathered, keep, give):
    panels, slots = tiles.shape[0], tiles.shape[1]
    cells = gathered.shape[1] - EXTRA
    zs = panels // 2
    z, core = place[1] // 2, place[1] % 2
    dots = jnp.zeros((8, 128), F32)
    for b in range(gathered.shape[0]):
        tail = gathered[b, cells:, :128].astype(F32)
        dots = dots + tail[:8] + tail[8:]
    dots = jnp.concatenate([dots, jnp.zeros_like(dots)], axis=1)
    for k in range(zs):
        at = (z + k) % zs
        for target, i in ((keep, 2 * at + core), (give, 2 * at + 1 - core)):
            total = None
            for s in range(slots):
                panel = gathered[columns[i * slots + s], :cells]
                panel = jnp.where(s < counts[i], panel, jnp.zeros_like(panel))
                part = nt(panel, tiles[i, s])
                total = part if total is None else total + part
            target[k, :cells] = total
            target[k, cells:] = dots


def gather_sums(tile_sums, near, far1, far3, far2, scales, cells):
    total = tile_sums[0]
    for b in range(1, tile_sums.shape[0]):
        total = total + tile_sums[b]
    side = near[...] + far1[...] + far2[...] + far3[...]
    product = (total + side[:cells]) * scales[0:1, :]
    return product, side[cells:, :128]


def first_kernel(tile_sums, near, far1, far3, far2, scales, many, one, applied, dots0, residual):
    cells = applied.shape[0]
    product, side = gather_sums(tile_sums, near, far1, far3, far2, scales, cells)
    projection, _ = to_columns(side, cells)
    applied[...] = product
    dots0[...] = side
    finish(product, projection, scales, many, one, residual)


def finish(applied, projection, scales, many, one, residual):
    inv_root, leading = scales[0:1, :], scales[1:2, :]
    rest = applied - projection * leading
    residual[...] = rest
    norm = jnp.sum(rest * rest, axis=1, keepdims=True)
    dot = jnp.sum(rest * leading, axis=1, keepdims=True)
    pack(rest * inv_root, to_rows(norm, dot), many, one)


def next_applied(total_cells, product, side, applied0, dots0, cells):
    norm, dot = to_columns(side, cells)
    start_dot, _ = to_columns(dots0[...], cells)
    scale = (1.0 - RESTART) / jnp.sqrt(norm / total_cells + EPSILON)
    applied = scale * product + RESTART * applied0[...]
    return applied, scale * dot + RESTART * start_dot


def middle_kernel(
    total_cells, tile_sums, near, far1, far3, far2, scales, applied0, dots0, many, one, residual
):
    cells = applied0.shape[0]
    product, side = gather_sums(tile_sums, near, far1, far3, far2, scales, cells)
    applied, projection = next_applied(total_cells, product, side, applied0, dots0, cells)
    finish(applied, projection, scales, many, one, residual)


def last_kernel(
    total_cells, tile_sums, near, far1, far3, far2, scales, applied0, dots0, norms, residual
):
    cells = applied0.shape[0]
    product, side = gather_sums(tile_sums, near, far1, far3, far2, scales, cells)
    applied, projection = next_applied(total_cells, product, side, applied0, dots0, cells)
    rest = applied - projection * scales[1:2, :]
    residual[...] = rest
    norm = jnp.sum(rest * rest, axis=1, keepdims=True)
    norms[...] = jnp.broadcast_to(to_rows(norm, norm)[:1], norms.shape)


def blend_kernel(total_cells, norms, residual, start, embedding):
    cells = start.shape[0]
    row = jnp.sum(norms[...], axis=0, keepdims=True)
    norm, _ = to_columns(jnp.concatenate([row, jnp.zeros((7, 128), F32)], axis=0), cells)
    scaled = residual[...] / jnp.sqrt(norm / total_cells + EPSILON)
    embedding[...] = (1.0 - RESTART) * scaled + RESTART * start[...].astype(F32)


def local(tile_values, tile_cols, row_counts, start_basis):
    rows, cols = lax.axis_size("row"), lax.axis_size("col")
    panels, _, slots, tile, _ = tile_values.shape
    cells = start_basis.shape[0]
    zs = cols // 2
    total_cells = rows * cols * tile
    tiles = tile_values.reshape(panels, slots, tile, tile)
    columns = tile_cols.reshape(panels * slots)
    counts = row_counts.reshape(panels)
    place = jnp.stack([lax.axis_index("row"), lax.axis_index("col")]).astype(jnp.int32)
    shape = jax.ShapeDtypeStruct
    swap = [(i, i ^ 1) for i in range(cols)]
    shift = lambda k: [(i, (i + 2 * k) % cols) for i in range(cols)]
    tile_bytes = panels * slots * tile * tile * 2
    work = 2 * panels * slots * cells * tile * tile

    message, table = call(
        degree_kernel,
        (shape((rows, cols, tile + 128), F32), shape((2 * rows,), jnp.int32)),
        [SMEM, SMEM, SMEM, VMEM],
        (VMEM, SMEM),
        [
            pltpu.VMEM((panels, tile), F32),
            pltpu.VMEM((panels * slots, 8, tile), F32),
            pltpu.SMEM((rows,), jnp.int32),
        ],
        work / 4,
        tile_bytes,
    )(place, columns, counts, tiles)
    parts = lax.all_to_all(
        message.reshape(rows * cols, tile + 128), ("row", "col"), 0, 0, tiled=True
    )

    many_shape = shape((rows, cells + EXTRA, tile), BF16)
    one_shape = shape((cells, tile), BF16)
    full = shape((cells, tile), F32)
    degrees, scales, many, one = call(
        lambda *refs: start_kernel(total_cells, *refs),
        (shape((1, tile), F32), shape((8, tile), F32), many_shape, one_shape),
        [VMEM, VMEM],
    )(parts, start_basis)

    applied0 = dots0 = residual = None
    for step in range(STEPS):
        pair = lax.ppermute(one, "col", swap)
        both = jnp.stack([one, pair])
        near = [lax.ppermute(both, "col", shift(k)) for k in (1, 3, 2)]
        gathered = lax.all_to_all(many, "row", 0, 0, tiled=True)
        back = call(
            lambda *refs: backward_kernel(*refs[:9], refs[9:]),
            shape((rows, cells, tile), F32),
            [SMEM, SMEM, SMEM] + [VMEM] * 6,
            VMEM,
            [pltpu.VMEM((panels, cells, tile), BF16)],
            work,
            tile_bytes,
        )(place, table, counts, tiles, one, pair, *near)
        back = lax.all_to_all(back, "row", 0, 0, tiled=True)
        side_shape = shape((zs, cells + 8, tile), F32)
        keep, give = call(
            forward_kernel,
            (side_shape, side_shape),
            [SMEM, SMEM, SMEM, VMEM, VMEM],
            flops=work,
            moved=tile_bytes,
        )(place, columns, counts, tiles, gathered)
        given = lax.ppermute(give, "col", swap)
        sums = keep + given
        sides = [sums[0]] + [lax.ppermute(sums[k], "col", shift(k)) for k in (1, 3, 2)]
        arrived = (back, *sides, scales)
        if step == 0:
            many, one, applied0, dots0, residual = call(
                first_kernel,
                (many_shape, one_shape, full, shape((8, 128), F32), full),
                [VMEM] * 6,
            )(*arrived)
        elif step + 1 < STEPS:
            many, one, residual = call(
                lambda *refs: middle_kernel(total_cells, *refs),
                (many_shape, one_shape, full),
                [VMEM] * 8,
            )(*arrived, applied0, dots0)
        else:
            norms, residual = call(
                lambda *refs: last_kernel(total_cells, *refs),
                (shape((rows * cols, 128), F32), full),
                [VMEM] * 8,
            )(*arrived, applied0, dots0)
    norms = lax.all_to_all(norms, ("row", "col"), 0, 0, tiled=True)
    embedding = call(
        lambda *refs: blend_kernel(total_cells, *refs), full, [VMEM] * 3
    )(norms, residual, start_basis)
    return (embedding, degrees.reshape(tile))


def solution(mesh):
    placed = (
        P("row", "col", None, None, None),
        P("row", "col", None),
        P("row", "col"),
        P(None, ("row", "col")),
    )
    return jax.shard_map(
        local,
        mesh=mesh,
        in_specs=placed,
        out_specs=(P(None, ("row", "col")), P(("row", "col"))),
        check_vma=False,
    )
```

time: 664 us -> 174 us (0.26)
  blocking collectives: 462 us -> 38.9 us
  waiting for transfers between devices: 105 us -> 37 us
  starting transfers between devices: 21.1 us -> 58 us
  matrix products: 25.1 us -> 0 us
  Pallas kernels: 0 us -> 20.7 us
  between operations: 14.6 us -> 0.83 us
  other arithmetic: 12.4 us -> 0.21 us
    psum x7 -> x0, blocking collectives: 451 us -> none  [the longest x3 193 us: local(): lax.psum(jnp.sum(current.astype(jnp.float32) * leading[None, :], axis=1),...]
    all_to_all x4 -> x6, waiting for transfers between devices: 105 us -> 1.91 us  [the longest x3 1.9 us: local(): back = lax.all_to_all(back, 'row', 0, 0, tiled=True)]
    ppermute x0 -> x24, waiting for transfers between devices: none -> 35.1 us  [the longest x9 14.8 us: local(): lax.ppermute(sums[k], 'col', shift(k))]
    all_to_all x1 -> x2, blocking collectives: 11.2 us -> 38.9 us  [the longest x1 21.7 us: local(): lax.all_to_all(message.reshape(rows * cols, tile + 128), ('row', 'col'),...]
    dot_general x8 -> x0, matrix products: 25.1 us -> none  [the longest x3 10.7 us: local(): jnp.einsum('cskv,csuv->ku', picked, in_tiles, preferred_element_type=jnp....]
    ppermute x0 -> x24, starting transfers between devices: none -> 22.1 us  [the longest x9 6.17 us: local(): near = [lax.ppermute(both, 'col', shift(k)) for k in (1, 3, 2)]]
    pallas_call x0 -> x12, Pallas kernels: none -> 20.7 us  [the longest x3 7.24 us: local(): call(lambda *refs: backward_kernel(*refs[:9], refs[9:]), shape((rows, cel...]
    gather x6 -> x0, local copies, waits for them, and re-layouts: 16.8 us -> none  [the longest x3 8.4 us: local(): gathered[mirror_panel]]
  transfers between devices with their start and end apart: 7 -> 30, of which waited for: 4 -> 20; matrix products, arithmetic and copies ran while one was open for 2% -> 0% of each run, Pallas kernels for 0% -> 8%
where the time goes in v1:
time: 174 us; the launch traced here: 173 us
  starting transfers between devices  58 us (33%)
  blocking collectives  38.9 us (22%)
  waiting for transfers between devices  37 us (21%)
  Pallas kernels  20.7 us (12%)
  local copies, waits for them, and re-layouts  17.1 us (10%)
    all_to_all x1, blocking collectives, local(): lax.all_to_all(message.reshape(rows * cols, tile + 128), ('row', 'col'),...  21.7 us
    all_to_all x3, starting transfers between devices, local(): back = lax.all_to_all(back, 'row', 0, 0, tiled=True)  20.1 us
    all_to_all x1, blocking collectives, local(): norms = lax.all_to_all(norms, ('row', 'col'), 0, 0, tiled=True)  17.2 us
    unnamed x22, local copies, waits for them, and re-layouts  16.7 us
    all_to_all x3, starting transfers between devices, local(): gathered = lax.all_to_all(many, 'row', 0, 0, tiled=True)  15.7 us
    ppermute x9, waiting for transfers between devices, local(): lax.ppermute(sums[k], 'col', shift(k))  14.8 us
    ppermute x9, waiting for transfers between devices, local(): near = [lax.ppermute(both, 'col', shift(k)) for k in (1, 3, 2)]  14 us
    pallas_call x3, Pallas kernels, local(): call(lambda *refs: backward_kernel(*refs[:9], refs[9:]), shape((rows, cel...  7.24 us
  transfers between devices with their start and end apart: 30, of which 20 were waited for; matrix products, arithmetic and copies ran while one was open for 0% of the time, Pallas kernels for 8%

profile of v1, /device:TPU:1, one launch (start us, length us, event | category | flops | bytes accessed | tf_op | source)
XLA Modules:
  0.0 172.7 jit_solution(1848171153043258762)
XLA Ops:
  1.6 2.2 %copy-done = bf16[8,1,4,256,256]{4,3,2,1,0:T(8,128)(2,1)S(1)} copy-done((bf16[8,1,4,256,256]{4,3,2,1,0:T(8,128)(2,1)S(1)}, bf16[8,1,4,256,256]{4,3,2,1,0:T(8,128)(2,1)}, u32[]{:S(2)}) %copy-start) | copy-done | bytes 4194328
  4.4 2.9 %shard_map.59 = (f32[16,8,384]{2,1,0:T(8,128)S(1)}, s32[32]{0:T(128)S(1)}) custom-call(s32[2]{0:T(128)S(1)} %pad_add_fusion.place.refs_0_, s32[32]{0:T(128)S(1)} %reshape.22.columns, s32[8]{0:T(128)S(1)} %bitcast.62, bf16[8,4,256,256]{3,2,1,0:T(8,128)(2,1)S(1)} %bitcast.45), custom_call_target="tpu_custom_call" | custom-call | flops 67108864 | bytes 4194304 | tf_op jit(solution)/shard_map/pallas_call | solution.py:245
  7.6 21.7 %all_to_all.52 = f32[128,1,384]{2,1,0:T(1,128)S(1)} all-to-all(f32[128,1,384]{2,1,0:T(1,128)S(1)} %copy.9), channel_id=1, replica_groups=mesh['row'=16,'col'=8] {'row','col'}, dimensions={0} | all-to-all | bytes 393216 | tf_op jit(solution)/shard_map/all_to_all | solution.py:258
  30.4 3.6 %all-to-all-start.2 = ((bf16[16,80,256]{2,1,0:T(8,128)(2,1)}), bf16[16,80,256]{2,1,0:T(8,128)(2,1)S(1)}, u32[]{:S(2)}, u32[]{:S(2)}) async-start(bf16[16,80,256]{2,1,0:T(8,128)(2,1)} %get-tuple-element.25), calls=%async_computation.2 | async-start | bytes 1310720 | tf_op jit(solution)/shard_map/all_to_all | solution.py:276
  38.4 2.1 %collective-permute-done.3.refs_8_ = bf16[2,64,256]{2,1,0:T(8,128)(2,1)S(1)} collective-permute-done((bf16[2,64,256]{2,1,0:T(8,128)(2,1)S(1)}, bf16[2,64,256]{2,1,0:T(8,128)(2,1)S(1)}, u32[]{:S(2)}, u32[]{:S(2)}) %collective-permute-start.3) | collective-permute-done | bytes 65568 | tf_op jit(solution)/shard_map/ppermute | solution.py:275
  40.5 2.5 %collective-permute-done.1.refs_6_ = bf16[2,64,256]{2,1,0:T(8,128)(2,1)S(1)} collective-permute-done((bf16[2,64,256]{2,1,0:T(8,128)(2,1)S(1)}, bf16[2,64,256]{2,1,0:T(8,128)(2,1)S(1)}, u32[]{:S(2)}, u32[]{:S(2)}) %collective-permute-start.1) | collective-permute-done | bytes 65568 | tf_op jit(solution)/shard_map/ppermute | solution.py:275
  43.1 2.2 %copy-done.1 = bf16[8,1,4,256,256]{4,3,2,1,0:T(8,128)(2,1)S(1)} copy-done((bf16[8,1,4,256,256]{4,3,2,1,0:T(8,128)(2,1)S(1)}, bf16[8,1,4,256,256]{4,3,2,1,0:T(8,128)(2,1)}, u32[]{:S(2)}) %copy-start.1) | copy-done | bytes 4194328
  45.3 2.4 %shard_map.61 = f32[16,64,256]{2,1,0:T(8,128)} custom-call(s32[2]{0:T(128)S(1)} %pad_add_fusion.place.refs_0_, s32[32]{0:T(128)S(1)} %get-tuple-element.22.refs_1_, s32[8]{0:T(128)S(1)} %bitcast.63, bf16[8,4,256,256]{3,2,1,0:T(8,128)(2,1)S(1)} %bitcast.46, bf16[64,256]{1,0:T(8,128)(2,1)S(1)} %get-tuple-element.24.refs_4_, ...), custom_call_target="tpu_custom_call" | custom-call | flops 268435456 | bytes 4194304 | tf_op jit(solution)/shard_map/pallas_call | solution.py:277
  47.7 6.6 %all-to-all-start.1 = ((f32[16,64,256]{2,1,0:T(8,128)}), f32[16,64,256]{2,1,0:T(8,128)S(1)}, u32[]{:S(2)}, u32[]{:S(2)}) async-start(f32[16,64,256]{2,1,0:T(8,128)} %shard_map.61), calls=%async_computation.1 | async-start | bytes 2097152 | tf_op jit(solution)/shard_map/all_to_all | solution.py:286
  54.3 2.2 %copy-done.2 = bf16[8,1,4,256,256]{4,3,2,1,0:T(8,128)(2,1)S(1)} copy-done((bf16[8,1,4,256,256]{4,3,2,1,0:T(8,128)(2,1)S(1)}, bf16[8,1,4,256,256]{4,3,2,1,0:T(8,128)(2,1)}, u32[]{:S(2)}) %copy-start.2) | copy-done | bytes 4194328
  56.5 1.9 %shard_map.62 = (f32[4,72,256]{2,1,0:T(8,128)S(1)}, f32[4,72,256]{2,1,0:T(8,128)S(1)}) custom-call(s32[2]{0:T(128)S(1)} %pad_add_fusion.place.refs_0_, s32[32]{0:T(128)S(1)} %reshape.22.columns, s32[8]{0:T(128)S(1)} %bitcast.64, bf16[8,4,256,256]{3,2,1,0:T(8,128)(2,1)S(1)} %bitcast.47, bf16[16,80,256]{2,1,0:T(8,128)(2,1)S(1)} %all-to-all-done.2.gathered), custom_call_target="tpu_custom_call" | custom-call | flops 268435456 | bytes 4194304 | tf_op jit(solution)/shard_map/pallas_call | solution.py:288
  58.5 2.3 %collective-permute-start.4 = (f32[4,72,256]{2,1,0:T(8,128)S(1)}, f32[4,72,256]{2,1,0:T(8,128)S(1)}, u32[]{:S(2)}, u32[]{:S(2)}) collective-permute-start(f32[4,72,256]{2,1,0:T(8,128)S(1)} %get-tuple-element.27), channel_id=1, source_target_pairs={{0,1},{1,0},{2,3},{3,2},{4,5},{5,4},{6,7},{7,6},{8,9},{9,8},{10,11... | collective-permute-start | bytes 884744 | tf_op jit(solution)/shard_map/ppermute | solution.py:295
  63.7 3.5 %collective-permute-done.7.far2 = f32[72,256]{1,0:T(8,128)S(1)} collective-permute-done((f32[72,256]{1,0:T(8,128)S(1)}, f32[72,256]{1,0:T(8,128)S(1)}, u32[]{:S(2)}, u32[]{:S(2)}) %collective-permute-start.7) | collective-permute-done | bytes 73760 | tf_op jit(solution)/shard_map/ppermute | solution.py:297
  70.2 6.9 %all-to-all-start.4 = ((bf16[16,80,256]{2,1,0:T(8,128)(2,1)}), bf16[16,80,256]{2,1,0:T(8,128)(2,1)S(1)}, u32[]{:S(2)}, u32[]{:S(2)}) async-start(bf16[16,80,256]{2,1,0:T(8,128)(2,1)} %get-tuple-element.30), calls=%async_computation.4 | async-start | bytes 1310720 | tf_op jit(solution)/shard_map/all_to_all | solution.py:276
  81.0 3.0 %collective-permute-done.11.refs_8_ = bf16[2,64,256]{2,1,0:T(8,128)(2,1)S(1)} collective-permute-done((bf16[2,64,256]{2,1,0:T(8,128)(2,1)S(1)}, bf16[2,64,256]{2,1,0:T(8,128)(2,1)S(1)}, u32[]{:S(2)}, u32[]{:S(2)}) %collective-permute-start.11) | collective-permute-done | bytes 65568 | tf_op jit(solution)/shard_map/ppermute | solution.py:275
  85.8 2.2 %copy-done.3 = bf16[8,1,4,256,256]{4,3,2,1,0:T(8,128)(2,1)S(1)} copy-done((bf16[8,1,4,256,256]{4,3,2,1,0:T(8,128)(2,1)S(1)}, bf16[8,1,4,256,256]{4,3,2,1,0:T(8,128)(2,1)}, u32[]{:S(2)}) %copy-start.3) | copy-done | bytes 4194328
  87.9 2.4 %shard_map.64 = f32[16,64,256]{2,1,0:T(8,128)} custom-call(s32[2]{0:T(128)S(1)} %pad_add_fusion.place.refs_0_, s32[32]{0:T(128)S(1)} %get-tuple-element.22.refs_1_, s32[8]{0:T(128)S(1)} %bitcast.65, bf16[8,4,256,256]{3,2,1,0:T(8,128)(2,1)S(1)} %bitcast.48, bf16[64,256]{1,0:T(8,128)(2,1)S(1)} %get-tuple-element.29.refs_4_, ...), custom_call_target="tpu_custom_call" | custom-call | flops 268435456 | bytes 4194304 | tf_op jit(solution)/shard_map/pallas_call | solution.py:277
  90.4 6.9 %all-to-all-start.3 = ((f32[16,64,256]{2,1,0:T(8,128)}), f32[16,64,256]{2,1,0:T(8,128)S(1)}, u32[]{:S(2)}, u32[]{:S(2)}) async-start(f32[16,64,256]{2,1,0:T(8,128)} %shard_map.64), calls=%async_computation.3 | async-start | bytes 2097152 | tf_op jit(solution)/shard_map/all_to_all | solution.py:286
  97.2 2.2 %copy-done.4 = bf16[8,1,4,256,256]{4,3,2,1,0:T(8,128)(2,1)S(1)} copy-done((bf16[8,1,4,256,256]{4,3,2,1,0:T(8,128)(2,1)S(1)}, bf16[8,1,4,256,256]{4,3,2,1,0:T(8,128)(2,1)}, u32[]{:S(2)}) %copy-start.4) | copy-done | bytes 4194328
  99.4 1.9 %shard_map.65 = (f32[4,72,256]{2,1,0:T(8,128)S(1)}, f32[4,72,256]{2,1,0:T(8,128)S(1)}) custom-call(s32[2]{0:T(128)S(1)} %pad_add_fusion.place.refs_0_, s32[32]{0:T(128)S(1)} %reshape.22.columns, s32[8]{0:T(128)S(1)} %bitcast.66, bf16[8,4,256,256]{3,2,1,0:T(8,128)(2,1)S(1)} %bitcast.49, bf16[16,80,256]{2,1,0:T(8,128)(2,1)S(1)} %all-to-all-done.4.gathered), custom_call_target="tpu_custom_call" | custom-call | flops 268435456 | bytes 4194304 | tf_op jit(solution)/shard_map/pallas_call | solution.py:288
  106.4 2.8 %collective-permute-done.15.refs_4_ = f32[72,256]{1,0:T(8,128)S(1)} collective-permute-done((f32[72,256]{1,0:T(8,128)S(1)}, f32[72,256]{1,0:T(8,128)S(1)}, u32[]{:S(2)}, u32[]{:S(2)}) %collective-permute-start.15) | collective-permute-done | bytes 73760 | tf_op jit(solution)/shard_map/ppermute | solution.py:297
  113.7 5.2 %all-to-all-start.6 = ((bf16[16,80,256]{2,1,0:T(8,128)(2,1)}), bf16[16,80,256]{2,1,0:T(8,128)(2,1)S(1)}, u32[]{:S(2)}, u32[]{:S(2)}) async-start(bf16[16,80,256]{2,1,0:T(8,128)(2,1)} %get-tuple-element.36), calls=%async_computation.6 | async-start | bytes 1310720 | tf_op jit(solution)/shard_map/all_to_all | solution.py:276
  118.9 2.1 %collective-permute-start.16 = (bf16[64,256]{1,0:T(8,128)(2,1)S(1)}, bf16[64,256]{1,0:T(8,128)(2,1)S(1)}, u32[]{:S(2)}, u32[]{:S(2)}) collective-permute-start(bf16[64,256]{1,0:T(8,128)(2,1)S(1)} %get-tuple-element.35.refs_4_), channel_id=1, source_target_pairs={{0,1},{1,0},{2,3},{3,2},{4,5},{5,4},{6,7},{7,6},{8,9},{9,8},{10,11... | collective-permute-start | bytes 98312 | tf_op jit(solution)/shard_map/ppermute | solution.py:273
  123.7 2.8 %collective-permute-done.19.refs_8_ = bf16[2,64,256]{2,1,0:T(8,128)(2,1)S(1)} collective-permute-done((bf16[2,64,256]{2,1,0:T(8,128)(2,1)S(1)}, bf16[2,64,256]{2,1,0:T(8,128)(2,1)S(1)}, u32[]{:S(2)}, u32[]{:S(2)}) %collective-permute-start.19) | collective-permute-done | bytes 65568 | tf_op jit(solution)/shard_map/ppermute | solution.py:275
  128.4 2.2 %copy-done.5 = bf16[8,1,4,256,256]{4,3,2,1,0:T(8,128)(2,1)S(1)} copy-done((bf16[8,1,4,256,256]{4,3,2,1,0:T(8,128)(2,1)S(1)}, bf16[8,1,4,256,256]{4,3,2,1,0:T(8,128)(2,1)}, u32[]{:S(2)}) %copy-start.5) | copy-done | bytes 4194328
  130.6 2.4 %shard_map.67 = f32[16,64,256]{2,1,0:T(8,128)} custom-call(s32[2]{0:T(128)S(1)} %pad_add_fusion.place.refs_0_, s32[32]{0:T(128)S(1)} %get-tuple-element.22.refs_1_, s32[8]{0:T(128)S(1)} %bitcast.67, bf16[8,4,256,256]{3,2,1,0:T(8,128)(2,1)S(1)} %bitcast.50, bf16[64,256]{1,0:T(8,128)(2,1)S(1)} %get-tuple-element.35.refs_4_, ...), custom_call_target="tpu_custom_call" | custom-call | flops 268435456 | bytes 4194304 | tf_op jit(solution)/shard_map/pallas_call | solution.py:277
  133.0 6.6 %all-to-all-start.5 = ((f32[16,64,256]{2,1,0:T(8,128)}), f32[16,64,256]{2,1,0:T(8,128)S(1)}, u32[]{:S(2)}, u32[]{:S(2)}) async-start(f32[16,64,256]{2,1,0:T(8,128)} %shard_map.67), calls=%async_computation.5 | async-start | bytes 2097152 | tf_op jit(solution)/shard_map/all_to_all | solution.py:286
  139.6 2.2 %copy-done.6 = bf16[8,1,4,256,256]{4,3,2,1,0:T(8,128)(2,1)S(1)} copy-done((bf16[8,1,4,256,256]{4,3,2,1,0:T(8,128)(2,1)S(1)}, bf16[8,1,4,256,256]{4,3,2,1,0:T(8,128)(2,1)}, u32[]{:S(2)}) %copy-start.6) | copy-done | bytes 4194328
  141.8 1.9 %shard_map.68 = (f32[4,72,256]{2,1,0:T(8,128)S(1)}, f32[4,72,256]{2,1,0:T(8,128)S(1)}) custom-call(s32[2]{0:T(128)S(1)} %pad_add_fusion.place.refs_0_, s32[32]{0:T(128)S(1)} %reshape.22.columns, s32[8]{0:T(128)S(1)} %bitcast.68, bf16[8,4,256,256]{3,2,1,0:T(8,128)(2,1)S(1)} %bitcast.51, bf16[16,80,256]{2,1,0:T(8,128)(2,1)S(1)} %all-to-all-done.6.gathered), custom_call_target="tpu_custom_call" | custom-call | flops 268435456 | bytes 4194304 | tf_op jit(solution)/shard_map/pallas_call | solution.py:288
  143.7 2.3 %collective-permute-start.20 = (f32[4,72,256]{2,1,0:T(8,128)S(1)}, f32[4,72,256]{2,1,0:T(8,128)S(1)}, u32[]{:S(2)}, u32[]{:S(2)}) collective-permute-start(f32[4,72,256]{2,1,0:T(8,128)S(1)} %get-tuple-element.38), channel_id=1, source_target_pairs={{0,1},{1,0},{2,3},{3,2},{4,5},{5,4},{6,7},{7,6},{8,9},{9,8},{10,11... | collective-permute-start | bytes 884744 | tf_op jit(solution)/shard_map/ppermute | solution.py:295
  148.9 3.5 %collective-permute-done.23.refs_4_ = f32[72,256]{1,0:T(8,128)S(1)} collective-permute-done((f32[72,256]{1,0:T(8,128)S(1)}, f32[72,256]{1,0:T(8,128)S(1)}, u32[]{:S(2)}, u32[]{:S(2)}) %collective-permute-start.23) | collective-permute-done | bytes 73760 | tf_op jit(solution)/shard_map/ppermute | solution.py:297
  154.7 17.2 %all_to_all.53 = f32[128,1,128]{2,1,0:T(1,128)S(1)} all-to-all(f32[128,1,128]{2,1,0:T(1,128)S(1)} %bitcast.61), channel_id=1, replica_groups=mesh['row'=16,'col'=8] {'row','col'}, dimensions={0} | all-to-all | bytes 131072 | tf_op jit(solution)/shard_map/all_to_all | solution.py:317
  (76 shorter events, 39.1 us)
Async XLA Ops:
  0.6 42.4 %copy-start.9 = (s32[8,1]{0,1:T(1,128)S(1)}, s32[8,1]{0,1:T(1,128)}, u32[]{:S(2)}) copy-start(s32[8,1]{0,1:T(1,128)} %param.6) | copy-start | bytes 100
  4.4 24.9 %copy-start.7 = (bf16[64,256]{1,0:T(8,128)(2,1)S(1)}, bf16[64,256]{1,0:T(8,128)(2,1)}, u32[]{:S(2)}) copy-start(bf16[64,256]{1,0:T(8,128)(2,1)} %refs_2_.1) | copy-start | bytes 98308
  30.4 17.3 %all-to-all-start.2 = ((bf16[16,80,256]{2,1,0:T(8,128)(2,1)}), bf16[16,80,256]{2,1,0:T(8,128)(2,1)S(1)}, u32[]{:S(2)}, u32[]{:S(2)}) async-start(bf16[16,80,256]{2,1,0:T(8,128)(2,1)} %get-tuple-element.25), calls=%async_computation.2 | async-start | bytes 1310720 | tf_op jit(solution)/shard_map/all_to_all | solution.py:276
  34.0 1.9 %collective-permute-start = (bf16[64,256]{1,0:T(8,128)(2,1)S(1)}, bf16[64,256]{1,0:T(8,128)(2,1)S(1)}, u32[]{:S(2)}, u32[]{:S(2)}) collective-permute-start(bf16[64,256]{1,0:T(8,128)(2,1)S(1)} %get-tuple-element.24.refs_4_), channel_id=1, source_target_pairs={{0,1},{1,0},{2,3},{3,2},{4,5},{5,4},{6,7},{7,6},{8,9},{9,8},{10,11... | collective-permute-start | bytes 98312 | tf_op jit(solution)/shard_map/ppermute | solution.py:273
  35.9 4.7 %collective-permute-start.3 = (bf16[2,64,256]{2,1,0:T(8,128)(2,1)S(1)}, bf16[2,64,256]{2,1,0:T(8,128)(2,1)S(1)}, u32[]{:S(2)}, u32[]{:S(2)}) collective-permute-start(bf16[2,64,256]{2,1,0:T(8,128)(2,1)S(1)} %pad_maximum_fusion), channel_id=1, source_target_pairs={{0,4},{1,5},{2,6},{3,7},{4,0},{5,1},{6,2},{7,3},{8,12},{9,13},{10,... | collective-permute-start | bytes 196616 | tf_op jit(solution)/shard_map/ppermute | solution.py:275
  36.7 3.8 %collective-permute-start.2 = (bf16[2,64,256]{2,1,0:T(8,128)(2,1)S(1)}, bf16[2,64,256]{2,1,0:T(8,128)(2,1)S(1)}, u32[]{:S(2)}, u32[]{:S(2)}) collective-permute-start(bf16[2,64,256]{2,1,0:T(8,128)(2,1)S(1)} %pad_maximum_fusion), channel_id=1, source_target_pairs={{0,6},{1,7},{2,0},{3,1},{4,2},{5,3},{6,4},{7,5},{8,14},{9,15},{10,... | collective-permute-start | bytes 196616 | tf_op jit(solution)/shard_map/ppermute | solution.py:275
  38.4 4.6 %collective-permute-start.1 = (bf16[2,64,256]{2,1,0:T(8,128)(2,1)S(1)}, bf16[2,64,256]{2,1,0:T(8,128)(2,1)S(1)}, u32[]{:S(2)}, u32[]{:S(2)}) collective-permute-start(bf16[2,64,256]{2,1,0:T(8,128)(2,1)S(1)} %pad_maximum_fusion), channel_id=1, source_target_pairs={{0,2},{1,3},{2,4},{3,5},{4,6},{5,7},{6,0},{7,1},{8,10},{9,11},{10,... | collective-permute-start | bytes 196616 | tf_op jit(solution)/shard_map/ppermute | solution.py:275
  47.7 21.3 %all-to-all-start.1 = ((f32[16,64,256]{2,1,0:T(8,128)}), f32[16,64,256]{2,1,0:T(8,128)S(1)}, u32[]{:S(2)}, u32[]{:S(2)}) async-start(f32[16,64,256]{2,1,0:T(8,128)} %shard_map.61), calls=%async_computation.1 | async-start | bytes 2097152 | tf_op jit(solution)/shard_map/all_to_all | solution.py:286
  58.5 3.5 %collective-permute-start.4 = (f32[4,72,256]{2,1,0:T(8,128)S(1)}, f32[4,72,256]{2,1,0:T(8,128)S(1)}, u32[]{:S(2)}, u32[]{:S(2)}) collective-permute-start(f32[4,72,256]{2,1,0:T(8,128)S(1)} %get-tuple-element.27), channel_id=1, source_target_pairs={{0,1},{1,0},{2,3},{3,2},{4,5},{5,4},{6,7},{7,6},{8,9},{9,8},{10,11... | collective-permute-start | bytes 884744 | tf_op jit(solution)/shard_map/ppermute | solution.py:295
  62.1 5.1 %collective-permute-start.7 = (f32[72,256]{1,0:T(8,128)S(1)}, f32[72,256]{1,0:T(8,128)S(1)}, u32[]{:S(2)}, u32[]{:S(2)}) collective-permute-start(f32[72,256]{1,0:T(8,128)S(1)} %get-tuple-element.50), channel_id=1, source_target_pairs={{0,4},{1,5},{2,6},{3,7},{4,0},{5,1},{6,2},{7,3},{8,12},{9,13},{10,... | collective-permute-start | bytes 221192 | tf_op jit(solution)/shard_map/ppermute | solution.py:297
  62.2 5.0 %collective-permute-start.6 = (f32[72,256]{1,0:T(8,128)S(1)}, f32[72,256]{1,0:T(8,128)S(1)}, u32[]{:S(2)}, u32[]{:S(2)}) collective-permute-start(f32[72,256]{1,0:T(8,128)S(1)} %get-tuple-element.51), channel_id=1, source_target_pairs={{0,6},{1,7},{2,0},{3,1},{4,2},{5,3},{6,4},{7,5},{8,14},{9,15},{10,... | collective-permute-start | bytes 221192 | tf_op jit(solution)/shard_map/ppermute | solution.py:297
  63.1 5.9 %collective-permute-start.5 = (f32[72,256]{1,0:T(8,128)S(1)}, f32[72,256]{1,0:T(8,128)S(1)}, u32[]{:S(2)}, u32[]{:S(2)}) collective-permute-start(f32[72,256]{1,0:T(8,128)S(1)} %get-tuple-element.52), channel_id=1, source_target_pairs={{0,2},{1,3},{2,4},{3,5},{4,6},{5,7},{6,0},{7,1},{8,10},{9,11},{10,... | collective-permute-start | bytes 221192 | tf_op jit(solution)/shard_map/ppermute | solution.py:297
  70.2 20.2 %all-to-all-start.4 = ((bf16[16,80,256]{2,1,0:T(8,128)(2,1)}), bf16[16,80,256]{2,1,0:T(8,128)(2,1)S(1)}, u32[]{:S(2)}, u32[]{:S(2)}) async-start(bf16[16,80,256]{2,1,0:T(8,128)(2,1)} %get-tuple-element.30), calls=%async_computation.4 | async-start | bytes 1310720 | tf_op jit(solution)/shard_map/all_to_all | solution.py:276
  77.1 2.1 %collective-permute-start.8 = (bf16[64,256]{1,0:T(8,128)(2,1)S(1)}, bf16[64,256]{1,0:T(8,128)(2,1)S(1)}, u32[]{:S(2)}, u32[]{:S(2)}) collective-permute-start(bf16[64,256]{1,0:T(8,128)(2,1)S(1)} %get-tuple-element.29.refs_4_), channel_id=1, source_target_pairs={{0,1},{1,0},{2,3},{3,2},{4,5},{5,4},{6,7},{7,6},{8,9},{9,8},{10,11... | collective-permute-start | bytes 98312 | tf_op jit(solution)/shard_map/ppermute | solution.py:273
  79.2 4.7 %collective-permute-start.11 = (bf16[2,64,256]{2,1,0:T(8,128)(2,1)S(1)}, bf16[2,64,256]{2,1,0:T(8,128)(2,1)S(1)}, u32[]{:S(2)}, u32[]{:S(2)}) collective-permute-start(bf16[2,64,256]{2,1,0:T(8,128)(2,1)S(1)} %pad_maximum_fusion.1), channel_id=1, source_target_pairs={{0,4},{1,5},{2,6},{3,7},{4,0},{5,1},{6,2},{7,3},{8,12},{9,13},{10,... | collective-permute-start | bytes 196616 | tf_op jit(solution)/shard_map/ppermute | solution.py:275
  79.5 4.5 %collective-permute-start.10 = (bf16[2,64,256]{2,1,0:T(8,128)(2,1)S(1)}, bf16[2,64,256]{2,1,0:T(8,128)(2,1)S(1)}, u32[]{:S(2)}, u32[]{:S(2)}) collective-permute-start(bf16[2,64,256]{2,1,0:T(8,128)(2,1)S(1)} %pad_maximum_fusion.1), channel_id=1, source_target_pairs={{0,6},{1,7},{2,0},{3,1},{4,2},{5,3},{6,4},{7,5},{8,14},{9,15},{10,... | collective-permute-start | bytes 196616 | tf_op jit(solution)/shard_map/ppermute | solution.py:275
  80.5 5.3 %collective-permute-start.9 = (bf16[2,64,256]{2,1,0:T(8,128)(2,1)S(1)}, bf16[2,64,256]{2,1,0:T(8,128)(2,1)S(1)}, u32[]{:S(2)}, u32[]{:S(2)}) collective-permute-start(bf16[2,64,256]{2,1,0:T(8,128)(2,1)S(1)} %pad_maximum_fusion.1), channel_id=1, source_target_pairs={{0,2},{1,3},{2,4},{3,5},{4,6},{5,7},{6,0},{7,1},{8,10},{9,11},{10,... | collective-permute-start | bytes 196616 | tf_op jit(solution)/shard_map/ppermute | solution.py:275
  90.4 22.1 %all-to-all-start.3 = ((f32[16,64,256]{2,1,0:T(8,128)}), f32[16,64,256]{2,1,0:T(8,128)S(1)}, u32[]{:S(2)}, u32[]{:S(2)}) async-start(f32[16,64,256]{2,1,0:T(8,128)} %shard_map.64), calls=%async_computation.3 | async-start | bytes 2097152 | tf_op jit(solution)/shard_map/all_to_all | solution.py:286
  101.4 2.7 %collective-permute-start.12 = (f32[4,72,256]{2,1,0:T(8,128)S(1)}, f32[4,72,256]{2,1,0:T(8,128)S(1)}, u32[]{:S(2)}, u32[]{:S(2)}) collective-permute-start(f32[4,72,256]{2,1,0:T(8,128)S(1)} %get-tuple-element.32), channel_id=1, source_target_pairs={{0,1},{1,0},{2,3},{3,2},{4,5},{5,4},{6,7},{7,6},{8,9},{9,8},{10,11... | collective-permute-start | bytes 884744 | tf_op jit(solution)/shard_map/ppermute | solution.py:295
  104.1 5.1 %collective-permute-start.15 = (f32[72,256]{1,0:T(8,128)S(1)}, f32[72,256]{1,0:T(8,128)S(1)}, u32[]{:S(2)}, u32[]{:S(2)}) collective-permute-start(f32[72,256]{1,0:T(8,128)S(1)} %get-tuple-element.46), channel_id=1, source_target_pairs={{0,4},{1,5},{2,6},{3,7},{4,0},{5,1},{6,2},{7,3},{8,12},{9,13},{10,... | collective-permute-start | bytes 221192 | tf_op jit(solution)/shard_map/ppermute | solution.py:297
  105.0 4.3 %collective-permute-start.14 = (f32[72,256]{1,0:T(8,128)S(1)}, f32[72,256]{1,0:T(8,128)S(1)}, u32[]{:S(2)}, u32[]{:S(2)}) collective-permute-start(f32[72,256]{1,0:T(8,128)S(1)} %get-tuple-element.47), channel_id=1, source_target_pairs={{0,6},{1,7},{2,0},{3,1},{4,2},{5,3},{6,4},{7,5},{8,14},{9,15},{10,... | collective-permute-start | bytes 221192 | tf_op jit(solution)/shard_map/ppermute | solution.py:297
  105.9 4.9 %collective-permute-start.13 = (f32[72,256]{1,0:T(8,128)S(1)}, f32[72,256]{1,0:T(8,128)S(1)}, u32[]{:S(2)}, u32[]{:S(2)}) collective-permute-start(f32[72,256]{1,0:T(8,128)S(1)} %get-tuple-element.48), channel_id=1, source_target_pairs={{0,2},{1,3},{2,4},{3,5},{4,6},{5,7},{6,0},{7,1},{8,10},{9,11},{10,... | collective-permute-start | bytes 221192 | tf_op jit(solution)/shard_map/ppermute | solution.py:297
  113.7 19.2 %all-to-all-start.6 = ((bf16[16,80,256]{2,1,0:T(8,128)(2,1)}), bf16[16,80,256]{2,1,0:T(8,128)(2,1)S(1)}, u32[]{:S(2)}, u32[]{:S(2)}) async-start(bf16[16,80,256]{2,1,0:T(8,128)(2,1)} %get-tuple-element.36), calls=%async_computation.6 | async-start | bytes 1310720 | tf_op jit(solution)/shard_map/all_to_all | solution.py:276
  118.9 2.9 %collective-permute-start.16 = (bf16[64,256]{1,0:T(8,128)(2,1)S(1)}, bf16[64,256]{1,0:T(8,128)(2,1)S(1)}, u32[]{:S(2)}, u32[]{:S(2)}) collective-permute-start(bf16[64,256]{1,0:T(8,128)(2,1)S(1)} %get-tuple-element.35.refs_4_), channel_id=1, source_target_pairs={{0,1},{1,0},{2,3},{3,2},{4,5},{5,4},{6,7},{7,6},{8,9},{9,8},{10,11... | collective-permute-start | bytes 98312 | tf_op jit(solution)/shard_map/ppermute | solution.py:273
  121.9 4.7 %collective-permute-start.19 = (bf16[2,64,256]{2,1,0:T(8,128)(2,1)S(1)}, bf16[2,64,256]{2,1,0:T(8,128)(2,1)S(1)}, u32[]{:S(2)}, u32[]{:S(2)}) collective-permute-start(bf16[2,64,256]{2,1,0:T(8,128)(2,1)S(1)} %pad_maximum_fusion.2), channel_id=1, source_target_pairs={{0,4},{1,5},{2,6},{3,7},{4,0},{5,1},{6,2},{7,3},{8,12},{9,13},{10,... | collective-permute-start | bytes 196616 | tf_op jit(solution)/shard_map/ppermute | solution.py:275
  122.3 4.3 %collective-permute-start.18 = (bf16[2,64,256]{2,1,0:T(8,128)(2,1)S(1)}, bf16[2,64,256]{2,1,0:T(8,128)(2,1)S(1)}, u32[]{:S(2)}, u32[]{:S(2)}) collective-permute-start(bf16[2,64,256]{2,1,0:T(8,128)(2,1)S(1)} %pad_maximum_fusion.2), channel_id=1, source_target_pairs={{0,6},{1,7},{2,0},{3,1},{4,2},{5,3},{6,4},{7,5},{8,14},{9,15},{10,... | collective-permute-start | bytes 196616 | tf_op jit(solution)/shard_map/ppermute | solution.py:275
  123.6 4.8 %collective-permute-start.17 = (bf16[2,64,256]{2,1,0:T(8,128)(2,1)S(1)}, bf16[2,64,256]{2,1,0:T(8,128)(2,1)S(1)}, u32[]{:S(2)}, u32[]{:S(2)}) collective-permute-start(bf16[2,64,256]{2,1,0:T(8,128)(2,1)S(1)} %pad_maximum_fusion.2), channel_id=1, source_target_pairs={{0,2},{1,3},{2,4},{3,5},{4,6},{5,7},{6,0},{7,1},{8,10},{9,11},{10,... | collective-permute-start | bytes 196616 | tf_op jit(solution)/shard_map/ppermute | solution.py:275
  133.0 21.3 %all-to-all-start.5 = ((f32[16,64,256]{2,1,0:T(8,128)}), f32[16,64,256]{2,1,0:T(8,128)S(1)}, u32[]{:S(2)}, u32[]{:S(2)}) async-start(f32[16,64,256]{2,1,0:T(8,128)} %shard_map.67), calls=%async_computation.5 | async-start | bytes 2097152 | tf_op jit(solution)/shard_map/all_to_all | solution.py:286
  143.7 3.5 %collective-permute-start.20 = (f32[4,72,256]{2,1,0:T(8,128)S(1)}, f32[4,72,256]{2,1,0:T(8,128)S(1)}, u32[]{:S(2)}, u32[]{:S(2)}) collective-permute-start(f32[4,72,256]{2,1,0:T(8,128)S(1)} %get-tuple-element.38), channel_id=1, source_target_pairs={{0,1},{1,0},{2,3},{3,2},{4,5},{5,4},{6,7},{7,6},{8,9},{9,8},{10,11... | collective-permute-start | bytes 884744 | tf_op jit(solution)/shard_map/ppermute | solution.py:295
  147.3 5.1 %collective-permute-start.23 = (f32[72,256]{1,0:T(8,128)S(1)}, f32[72,256]{1,0:T(8,128)S(1)}, u32[]{:S(2)}, u32[]{:S(2)}) collective-permute-start(f32[72,256]{1,0:T(8,128)S(1)} %get-tuple-element.42), channel_id=1, source_target_pairs={{0,4},{1,5},{2,6},{3,7},{4,0},{5,1},{6,2},{7,3},{8,12},{9,13},{10,... | collective-permute-start | bytes 221192 | tf_op jit(solution)/shard_map/ppermute | solution.py:297
  147.4 5.0 %collective-permute-start.22 = (f32[72,256]{1,0:T(8,128)S(1)}, f32[72,256]{1,0:T(8,128)S(1)}, u32[]{:S(2)}, u32[]{:S(2)}) collective-permute-start(f32[72,256]{1,0:T(8,128)S(1)} %get-tuple-element.43), channel_id=1, source_target_pairs={{0,6},{1,7},{2,0},{3,1},{4,2},{5,3},{6,4},{7,5},{8,14},{9,15},{10,... | collective-permute-start | bytes 221192 | tf_op jit(solution)/shard_map/ppermute | solution.py:297
  148.7 5.3 %collective-permute-start.21 = (f32[72,256]{1,0:T(8,128)S(1)}, f32[72,256]{1,0:T(8,128)S(1)}, u32[]{:S(2)}, u32[]{:S(2)}) collective-permute-start(f32[72,256]{1,0:T(8,128)S(1)} %get-tuple-element.44), channel_id=1, source_target_pairs={{0,2},{1,3},{2,4},{3,5},{4,6},{5,7},{6,0},{7,1},{8,10},{9,11},{10,... | collective-permute-start | bytes 221192 | tf_op jit(solution)/shard_map/ppermute | solution.py:297
  (8 other events, 16.0 us)

commit v2 on v1

--- a/solution.py
+++ b/solution.py
@@ -13,7 +13,11 @@
 BF16 = jnp.bfloat16
 VMEM = pl.BlockSpec(memory_space=pltpu.VMEM)
 SMEM = pl.BlockSpec(memory_space=pltpu.SMEM)
-PARAMS = pltpu.CompilerParams(vmem_limit_bytes=40 * 1024 * 1024)
+EMPTY = 1024
+COLUMNS = 8
+SLOTS_OF = 64
+META = 128
+BACK = BF16
 EXTRA = 16
 
 
@@ -25,14 +29,14 @@
     return lax.dot_general(a, b, (((1,), (1,)), ((), ())), preferred_element_type=F32)
 
 
-def call(kernel, outs, ins, out_specs=None, scratch=(), flops=1e6, moved=1e6):
+def call(kernel, outs, ins, out_specs=None, scratch=(), flops=1e6, moved=1e6, limit=16 * 1024 * 1024):
     return pl.pallas_call(
         kernel,
         out_shape=outs,
         in_specs=ins,
         out_specs=out_specs if out_specs is not None else jax.tree.map(lambda _: VMEM, outs),
         scratch_shapes=list(scratch),
-        compiler_params=PARAMS,
+        compiler_params=pltpu.CompilerParams(vmem_limit_bytes=limit),
         cost_estimate=pl.CostEstimate(
             flops=int(flops), bytes_accessed=int(moved), transcendentals=0
         ),
@@ -52,23 +56,28 @@
     return wide[:cells, 0:1], wide[:cells, 1:2]
 
 
-def degree_kernel(place, columns, counts, tiles, message, table, row_sums, col_sums, used):
+def degree_kernel(place, columns, counts, tiles, message, meta, row_sums, col_sums, used):
     panels, slots, tile = tiles.shape[0], tiles.shape[1], tiles.shape[2]
     row_devices = message.shape[0]
     mine_row, mine_col = place[0], place[1]
-
+    meta[0] = mine_row
+    meta[1] = mine_col
     for b in range(row_devices):
         used[b] = 0
-    for q in range(panels * slots):
-        b = columns[q]
-        table[2 * b + used[b]] = q
-        used[b] = used[b] + 1
+    for i in range(panels):
+        for s in range(slots):
+            q = i * slots + s
+            b = columns[i, 0, s]
+            dead = jnp.where(s < counts[i, 0], 0, EMPTY)
+            meta[COLUMNS + q] = b + dead
+            meta[SLOTS_OF + 2 * b + used[b]] = q + dead
+            used[b] = used[b] + 1
 
     ones = jnp.ones((16, tile), BF16)
     for i in range(panels):
         total = jnp.zeros((16, tile), F32)
         for s in range(slots):
-            live = s < counts[i]
+            live = s < counts[i, 0]
             weight = jnp.where(live, ones, jnp.zeros_like(ones))
             value = tiles[i, s]
             total = total + nt(weight, value)
@@ -77,7 +86,9 @@
     rows = row_sums[...]
     everything = jnp.sum(jnp.sum(rows, axis=1, keepdims=True), axis=0, keepdims=True)
     for b in range(row_devices):
-        part = col_sums[table[2 * b]] + col_sums[table[2 * b + 1]]
+        first = meta[SLOTS_OF + 2 * b] % EMPTY
+        second = meta[SLOTS_OF + 2 * b + 1] % EMPTY
+        part = col_sums[first] + col_sums[second]
         at = lax.broadcasted_iota(jnp.int32, part.shape, 0)
         part = jnp.where(at == mine_col, part, 0.0) + jnp.where(b == mine_row, rows, 0.0)
         message[b, :, :tile] = part
@@ -112,38 +123,13 @@
     pack(wide * inv_root, to_rows(dot, jnp.zeros_like(dot)), many, one)
 
 
-def backward_kernel(place, table, counts, tiles, own, pair, far1, far3, far2, out):
-    slots = tiles.shape[1]
-    zs = tiles.shape[0] // 2
-    mine_col = place[1]
-    z, core = mine_col // 2, mine_col % 2
-    panels = tiles.shape[0]
-    buffer = out[1]
-    result = out[0]
-    for k, source in ((0, None), (1, far1), (2, far2), (3, far3)):
-        at = (z + zs - k) % zs
-        same = own[...] if source is None else source[0]
-        other = pair[...] if source is None else source[1]
-        buffer[2 * at + core] = same
-        buffer[2 * at + 1 - core] = other
-    for b in range(result.shape[0]):
-        total = None
-        for m in range(2):
-            q = table[2 * b + m]
-            i = q // slots
-            s = q % slots
-            panel = buffer[i]
-            panel = jnp.where(s < counts[i], panel, jnp.zeros_like(panel))
-            part = nn(panel, tiles[i, s])
-            total = part if total is None else total + part
-        result[b] = total
-
-
-def forward_kernel(place, columns, counts, tiles, gathered, keep, give):
+def product_kernel(
+    meta, tiles, gathered, own, pair, far1, far3, far2, result, keep, give, buffer
+):
     panels, slots = tiles.shape[0], tiles.shape[1]
-    cells = gathered.shape[1] - EXTRA
+    cells = own.shape[0]
     zs = panels // 2
-    z, core = place[1] // 2, place[1] % 2
+    z, core = meta[1] // 2, meta[1] % 2
     dots = jnp.zeros((8, 128), F32)
     for b in range(gathered.shape[0]):
         tail = gathered[b, cells:, :128].astype(F32)
@@ -154,18 +140,35 @@
         for target, i in ((keep, 2 * at + core), (give, 2 * at + 1 - core)):
             total = None
             for s in range(slots):
-                panel = gathered[columns[i * slots + s], :cells]
-                panel = jnp.where(s < counts[i], panel, jnp.zeros_like(panel))
+                held = meta[COLUMNS + i * slots + s]
+                panel = gathered[held % EMPTY, :cells]
+                panel = jnp.where(held < EMPTY, panel, jnp.zeros_like(panel))
                 part = nt(panel, tiles[i, s])
                 total = part if total is None else total + part
             target[k, :cells] = total
             target[k, cells:] = dots
+    for k, source in ((0, None), (1, far1), (2, far2), (3, far3)):
+        at = (z + zs - k) % zs
+        same = own[...] if source is None else source[0]
+        other = pair[...] if source is None else source[1]
+        buffer[2 * at + core] = same
+        buffer[2 * at + 1 - core] = other
+    for b in range(result.shape[0]):
+        total = None
+        for m in range(2):
+            held = meta[SLOTS_OF + 2 * b + m]
+            q = held % EMPTY
+            panel = buffer[q // slots]
+            panel = jnp.where(held < EMPTY, panel, jnp.zeros_like(panel))
+            part = nn(panel, tiles[q // slots, q % slots])
+            total = part if total is None else total + part
+        result[b] = total.astype(result.dtype)
 
 
 def gather_sums(tile_sums, near, far1, far3, far2, scales, cells):
-    total = tile_sums[0]
+    total = tile_sums[0].astype(F32)
     for b in range(1, tile_sums.shape[0]):
-        total = total + tile_sums[b]
+        total = total + tile_sums[b].astype(F32)
     side = near[...] + far1[...] + far2[...] + far3[...]
     product = (total + side[:cells]) * scales[0:1, :]
     return product, side[cells:, :128]
@@ -233,8 +236,6 @@
     zs = cols // 2
     total_cells = rows * cols * tile
     tiles = tile_values.reshape(panels, slots, tile, tile)
-    columns = tile_cols.reshape(panels * slots)
-    counts = row_counts.reshape(panels)
     place = jnp.stack([lax.axis_index("row"), lax.axis_index("col")]).astype(jnp.int32)
     shape = jax.ShapeDtypeStruct
     swap = [(i, i ^ 1) for i in range(cols)]
@@ -242,9 +243,9 @@
     tile_bytes = panels * slots * tile * tile * 2
     work = 2 * panels * slots * cells * tile * tile
 
-    message, table = call(
+    message, meta = call(
         degree_kernel,
-        (shape((rows, cols, tile + 128), F32), shape((2 * rows,), jnp.int32)),
+        (shape((rows, cols, tile + 128), F32), shape((META,), jnp.int32)),
         [SMEM, SMEM, SMEM, VMEM],
         (VMEM, SMEM),
         [
@@ -254,7 +255,7 @@
         ],
         work / 4,
         tile_bytes,
-    )(place, columns, counts, tiles)
+    )(place, tile_cols, row_counts, tiles)
     parts = lax.all_to_all(
         message.reshape(rows * cols, tile + 128), ("row", "col"), 0, 0, tiled=True
     )
@@ -274,24 +275,16 @@
         both = jnp.stack([one, pair])
         near = [lax.ppermute(both, "col", shift(k)) for k in (1, 3, 2)]
         gathered = lax.all_to_all(many, "row", 0, 0, tiled=True)
-        back = call(
-            lambda *refs: backward_kernel(*refs[:9], refs[9:]),
-            shape((rows, cells, tile), F32),
-            [SMEM, SMEM, SMEM] + [VMEM] * 6,
-            VMEM,
-            [pltpu.VMEM((panels, cells, tile), BF16)],
-            work,
-            tile_bytes,
-        )(place, table, counts, tiles, one, pair, *near)
+        side_shape = shape((zs, cells + 8, tile), F32)
+        back, keep, give = call(
+            product_kernel,
+            (shape((rows, cells, tile), BACK), side_shape, side_shape),
+            [SMEM] + [VMEM] * 7,
+            scratch=[pltpu.VMEM((panels, cells, tile), BF16)],
+            flops=2 * work,
+            moved=tile_bytes,
+        )(meta, tiles, gathered, one, pair, *near)
         back = lax.all_to_all(back, "row", 0, 0, tiled=True)
-        side_shape = shape((zs, cells + 8, tile), F32)
-        keep, give = call(
-            forward_kernel,
-            (side_shape, side_shape),
-            [SMEM, SMEM, SMEM, VMEM, VMEM],
-            flops=work,
-            moved=tile_bytes,
-        )(place, columns, counts, tiles, gathered)
         given = lax.ppermute(give, "col", swap)
         sums = keep + given
         sides = [sums[0]] + [lax.ppermute(sums[k], "col", shift(k)) for k in (1, 3, 2)]

time: 174 us -> 163 us (0.937)
  waiting for transfers between devices: 37 us -> 48.2 us
  starting transfers between devices: 58 us -> 48 us
  local copies, waits for them, and re-layouts: 17.1 us -> 10.5 us
  blocking collectives: 38.9 us -> 35.9 us
  Pallas kernels: 20.7 us -> 18.3 us
    all_to_all x3, starting transfers between devices: 20.1 us -> 11.9 us  [local(): back = lax.all_to_all(back, 'row', 0, 0, tiled=True)]
    all_to_all x3, waiting for transfers between devices: 1.9 us -> 9.68 us  [local(): back = lax.all_to_all(back, 'row', 0, 0, tiled=True)]
    all_to_all x3, waiting for transfers between devices: 0.01 us -> 6.9 us  [local(): gathered = lax.all_to_all(many, 'row', 0, 0, tiled=True)]
    unnamed x22 -> x13, local copies, waits for them, and re-layouts: 16.7 us -> 10.3 us
    ppermute x3, waiting for transfers between devices: 3.63 us -> 0.01 us  [local(): given = lax.ppermute(give, 'col', swap)]
    all_to_all x3, starting transfers between devices: 15.7 us -> 12.4 us  [local(): gathered = lax.all_to_all(many, 'row', 0, 0, tiled=True)]
    all_to_all x1, blocking collectives: 17.2 us -> 14.2 us  [local(): norms = lax.all_to_all(norms, ('row', 'col'), 0, 0, tiled=True)]
    pallas_call x7 -> x4, Pallas kernels: 16 us -> 13.6 us  [the longest x3 10.4 us: local(): call(product_kernel, (shape((rows, cells, tile), BACK), side_shape, side_...]
  transfers between devices with their start and end apart: 30 -> 30, of which waited for: 20 -> 23; matrix products, arithmetic and copies ran while one was open for 0% -> 0% of each run, Pallas kernels for 8% -> 0%
where the time goes in v2:
time: 163 us; the launch traced here: 162 us
  waiting for transfers between devices  48.2 us (30%)
  starting transfers between devices  48 us (29%)
  blocking collectives  35.9 us (22%)
  Pallas kernels  18.3 us (11%)
  local copies, waits for them, and re-layouts  10.5 us (6%)
    all_to_all x1, blocking collectives, local(): lax.all_to_all(message.reshape(rows * cols, tile + 128), ('row', 'col'),...  21.7 us
    ppermute x9, waiting for transfers between devices, local(): lax.ppermute(sums[k], 'col', shift(k))  14.9 us
    all_to_all x1, blocking collectives, local(): norms = lax.all_to_all(norms, ('row', 'col'), 0, 0, tiled=True)  14.2 us
    ppermute x9, waiting for transfers between devices, local(): near = [lax.ppermute(both, 'col', shift(k)) for k in (1, 3, 2)]  14.2 us
    all_to_all x3, starting transfers between devices, local(): gathered = lax.all_to_all(many, 'row', 0, 0, tiled=True)  12.4 us
    all_to_all x3, starting transfers between devices, local(): back = lax.all_to_all(back, 'row', 0, 0, tiled=True)  11.9 us
    pallas_call x3, Pallas kernels, local(): call(product_kernel, (shape((rows, cells, tile), BACK), side_shape, side_...  10.4 us
    unnamed x13, local copies, waits for them, and re-layouts  10.3 us
  transfers between devices with their start and end apart: 30, of which 23 were waited for; matrix products, arithmetic and copies ran while one was open for 0% of the time, Pallas kernels for 0%

profile of v2, /device:TPU:1, one launch (start us, length us, event | category | flops | bytes accessed | tf_op | source)
XLA Modules:
  0.0 162.0 jit_solution(11997817059430299976)
XLA Ops:
  2.2 2.2 %copy-done = bf16[8,1,4,256,256]{4,3,2,1,0:T(8,128)(2,1)S(1)} copy-done((bf16[8,1,4,256,256]{4,3,2,1,0:T(8,128)(2,1)S(1)}, bf16[8,1,4,256,256]{4,3,2,1,0:T(8,128)(2,1)}, u32[]{:S(2)}) %copy-start) | copy-done | bytes 4194328
  4.4 3.1 %shard_map.59 = (f32[16,8,384]{2,1,0:T(8,128)S(1)}, s32[128]{0:T(128)S(1)}) custom-call(s32[2]{0:T(128)S(1)} %pad_add_fusion.place, s32[8,1,4]{2,1,0:T(1,128)S(1)} %copy.8.columns, s32[8,1]{1,0:T(8,128)S(1)} %copy.9.counts, bf16[8,4,256,256]{3,2,1,0:T(8,128)(2,1)S(1)} %bitcast.42), custom_call_target="tpu_custom_call" | custom-call | flops 67108864 | bytes 4194304 | tf_op jit(solution)/shard_map/pallas_call | solution.py:246
  7.7 21.7 %all_to_all.52 = f32[128,1,384]{2,1,0:T(1,128)S(1)} all-to-all(f32[128,1,384]{2,1,0:T(1,128)S(1)} %copy.10), channel_id=1, replica_groups=mesh['row'=16,'col'=8] {'row','col'}, dimensions={0} | all-to-all | bytes 393216 | tf_op jit(solution)/shard_map/all_to_all | solution.py:259
  30.6 3.6 %all-to-all-start.1 = ((bf16[16,80,256]{2,1,0:T(8,128)(2,1)}), bf16[16,80,256]{2,1,0:T(8,128)(2,1)S(1)}, u32[]{:S(2)}, u32[]{:S(2)}) async-start(bf16[16,80,256]{2,1,0:T(8,128)(2,1)} %get-tuple-element.27), calls=%async_computation.1 | async-start | bytes 1310720 | tf_op jit(solution)/shard_map/all_to_all | solution.py:277
  38.6 2.1 %collective-permute-done.3.far2 = bf16[2,64,256]{2,1,0:T(8,128)(2,1)S(1)} collective-permute-done((bf16[2,64,256]{2,1,0:T(8,128)(2,1)S(1)}, bf16[2,64,256]{2,1,0:T(8,128)(2,1)S(1)}, u32[]{:S(2)}, u32[]{:S(2)}) %collective-permute-start.3) | collective-permute-done | bytes 65568 | tf_op jit(solution)/shard_map/ppermute | solution.py:276
  40.7 2.5 %collective-permute-done.1.far1 = bf16[2,64,256]{2,1,0:T(8,128)(2,1)S(1)} collective-permute-done((bf16[2,64,256]{2,1,0:T(8,128)(2,1)S(1)}, bf16[2,64,256]{2,1,0:T(8,128)(2,1)S(1)}, u32[]{:S(2)}, u32[]{:S(2)}) %collective-permute-start.1) | collective-permute-done | bytes 65568 | tf_op jit(solution)/shard_map/ppermute | solution.py:276
  43.3 2.5 %all-to-all-done.1.gathered = bf16[16,80,256]{2,1,0:T(8,128)(2,1)S(1)} async-done(((bf16[16,80,256]{2,1,0:T(8,128)(2,1)}), bf16[16,80,256]{2,1,0:T(8,128)(2,1)S(1)}, u32[]{:S(2)}, u32[]{:S(2)}) %all-to-all-start.1) | async-done | bytes 655392 | tf_op jit(solution)/shard_map/all_to_all | solution.py:277
  45.7 2.2 %copy-done.1 = bf16[8,1,4,256,256]{4,3,2,1,0:T(8,128)(2,1)S(1)} copy-done((bf16[8,1,4,256,256]{4,3,2,1,0:T(8,128)(2,1)S(1)}, bf16[8,1,4,256,256]{4,3,2,1,0:T(8,128)(2,1)}, u32[]{:S(2)}) %copy-start.1) | copy-done | bytes 4194328
  47.9 3.5 %shard_map.61 = (bf16[16,64,256]{2,1,0:T(8,128)(2,1)}, f32[4,72,256]{2,1,0:T(8,128)S(1)}, f32[4,72,256]{2,1,0:T(8,128)S(1)}) custom-call(s32[128]{0:T(128)S(1)} %get-tuple-element.25.meta, bf16[8,4,256,256]{3,2,1,0:T(8,128)(2,1)S(1)} %bitcast.43, bf16[16,80,256]{2,1,0:T(8,128)(2,1)S(1)} %all-to-all-done.1.gathered, ...), custom_call_target="tpu_custom_call" | custom-call | flops 536870912 | bytes 4194304 | tf_op jit(solution)/shard_map/pallas_call | solution.py:279
  51.4 2.3 %collective-permute-start.4 = (f32[4,72,256]{2,1,0:T(8,128)S(1)}, f32[4,72,256]{2,1,0:T(8,128)S(1)}, u32[]{:S(2)}, u32[]{:S(2)}) collective-permute-start(f32[4,72,256]{2,1,0:T(8,128)S(1)} %get-tuple-element.31), channel_id=1, source_target_pairs={{0,1},{1,0},{2,3},{3,2},{4,5},{5,4},{6,7},{7,6},{8,9},{9,8},{10,11... | collective-permute-start | bytes 884744 | tf_op jit(solution)/shard_map/ppermute | solution.py:288
  53.6 3.9 %all-to-all-start.2 = ((bf16[16,64,256]{2,1,0:T(8,128)(2,1)}), bf16[16,64,256]{2,1,0:T(8,128)(2,1)S(1)}, u32[]{:S(2)}, u32[]{:S(2)}) async-start(bf16[16,64,256]{2,1,0:T(8,128)(2,1)} %get-tuple-element.29), calls=%async_computation.2 | async-start | bytes 1048576 | tf_op jit(solution)/shard_map/all_to_all | solution.py:287
  60.3 2.5 %collective-permute-done.7.far2 = f32[72,256]{1,0:T(8,128)S(1)} collective-permute-done((f32[72,256]{1,0:T(8,128)S(1)}, f32[72,256]{1,0:T(8,128)S(1)}, u32[]{:S(2)}, u32[]{:S(2)}) %collective-permute-start.7) | collective-permute-done | bytes 73760 | tf_op jit(solution)/shard_map/ppermute | solution.py:290
  65.0 2.7 %all-to-all-done.2.tile_sums = bf16[16,64,256]{2,1,0:T(8,128)(2,1)S(1)} async-done(((bf16[16,64,256]{2,1,0:T(8,128)(2,1)}), bf16[16,64,256]{2,1,0:T(8,128)(2,1)S(1)}, u32[]{:S(2)}, u32[]{:S(2)}) %all-to-all-start.2) | async-done | bytes 524320 | tf_op jit(solution)/shard_map/all_to_all | solution.py:287
  68.8 4.4 %all-to-all-start.3 = ((bf16[16,80,256]{2,1,0:T(8,128)(2,1)}), bf16[16,80,256]{2,1,0:T(8,128)(2,1)S(1)}, u32[]{:S(2)}, u32[]{:S(2)}) async-start(bf16[16,80,256]{2,1,0:T(8,128)(2,1)} %get-tuple-element.33), calls=%async_computation.3 | async-start | bytes 1310720 | tf_op jit(solution)/shard_map/all_to_all | solution.py:277
  78.3 2.1 %collective-permute-done.11.far2 = bf16[2,64,256]{2,1,0:T(8,128)(2,1)S(1)} collective-permute-done((bf16[2,64,256]{2,1,0:T(8,128)(2,1)S(1)}, bf16[2,64,256]{2,1,0:T(8,128)(2,1)S(1)}, u32[]{:S(2)}, u32[]{:S(2)}) %collective-permute-start.11) | collective-permute-done | bytes 65568 | tf_op jit(solution)/shard_map/ppermute | solution.py:276
  80.5 2.4 %collective-permute-done.9.far1 = bf16[2,64,256]{2,1,0:T(8,128)(2,1)S(1)} collective-permute-done((bf16[2,64,256]{2,1,0:T(8,128)(2,1)S(1)}, bf16[2,64,256]{2,1,0:T(8,128)(2,1)S(1)}, u32[]{:S(2)}, u32[]{:S(2)}) %collective-permute-start.9) | collective-permute-done | bytes 65568 | tf_op jit(solution)/shard_map/ppermute | solution.py:276
  84.8 2.2 %copy-done.2 = bf16[8,1,4,256,256]{4,3,2,1,0:T(8,128)(2,1)S(1)} copy-done((bf16[8,1,4,256,256]{4,3,2,1,0:T(8,128)(2,1)S(1)}, bf16[8,1,4,256,256]{4,3,2,1,0:T(8,128)(2,1)}, u32[]{:S(2)}) %copy-start.2) | copy-done | bytes 4194328
  86.9 3.5 %shard_map.63 = (bf16[16,64,256]{2,1,0:T(8,128)(2,1)}, f32[4,72,256]{2,1,0:T(8,128)S(1)}, f32[4,72,256]{2,1,0:T(8,128)S(1)}) custom-call(s32[128]{0:T(128)S(1)} %get-tuple-element.25.meta, bf16[8,4,256,256]{3,2,1,0:T(8,128)(2,1)S(1)} %bitcast.44, bf16[16,80,256]{2,1,0:T(8,128)(2,1)S(1)} %all-to-all-done.3.gathered, ...), custom_call_target="tpu_custom_call" | custom-call | flops 536870912 | bytes 4194304 | tf_op jit(solution)/shard_map/pallas_call | solution.py:279
  90.4 2.3 %collective-permute-start.12 = (f32[4,72,256]{2,1,0:T(8,128)S(1)}, f32[4,72,256]{2,1,0:T(8,128)S(1)}, u32[]{:S(2)}, u32[]{:S(2)}) collective-permute-start(f32[4,72,256]{2,1,0:T(8,128)S(1)} %get-tuple-element.37), channel_id=1, source_target_pairs={{0,1},{1,0},{2,3},{3,2},{4,5},{5,4},{6,7},{7,6},{8,9},{9,8},{10,11... | collective-permute-start | bytes 884744 | tf_op jit(solution)/shard_map/ppermute | solution.py:288
  92.8 4.4 %all-to-all-start.4 = ((bf16[16,64,256]{2,1,0:T(8,128)(2,1)}), bf16[16,64,256]{2,1,0:T(8,128)(2,1)S(1)}, u32[]{:S(2)}, u32[]{:S(2)}) async-start(bf16[16,64,256]{2,1,0:T(8,128)(2,1)} %get-tuple-element.35), calls=%async_computation.4 | async-start | bytes 1048576 | tf_op jit(solution)/shard_map/all_to_all | solution.py:287
  98.9 3.5 %collective-permute-done.15.refs_4_ = f32[72,256]{1,0:T(8,128)S(1)} collective-permute-done((f32[72,256]{1,0:T(8,128)S(1)}, f32[72,256]{1,0:T(8,128)S(1)}, u32[]{:S(2)}, u32[]{:S(2)}) %collective-permute-start.15) | collective-permute-done | bytes 73760 | tf_op jit(solution)/shard_map/ppermute | solution.py:290
  103.9 3.4 %all-to-all-done.4.refs_0_ = bf16[16,64,256]{2,1,0:T(8,128)(2,1)S(1)} async-done(((bf16[16,64,256]{2,1,0:T(8,128)(2,1)}), bf16[16,64,256]{2,1,0:T(8,128)(2,1)S(1)}, u32[]{:S(2)}, u32[]{:S(2)}) %all-to-all-start.4) | async-done | bytes 524320 | tf_op jit(solution)/shard_map/all_to_all | solution.py:287
  108.6 4.4 %all-to-all-start.5 = ((bf16[16,80,256]{2,1,0:T(8,128)(2,1)}), bf16[16,80,256]{2,1,0:T(8,128)(2,1)S(1)}, u32[]{:S(2)}, u32[]{:S(2)}) async-start(bf16[16,80,256]{2,1,0:T(8,128)(2,1)} %get-tuple-element.40), calls=%async_computation.5 | async-start | bytes 1310720 | tf_op jit(solution)/shard_map/all_to_all | solution.py:277
  117.0 3.1 %collective-permute-done.19.far2 = bf16[2,64,256]{2,1,0:T(8,128)(2,1)S(1)} collective-permute-done((bf16[2,64,256]{2,1,0:T(8,128)(2,1)S(1)}, bf16[2,64,256]{2,1,0:T(8,128)(2,1)S(1)}, u32[]{:S(2)}, u32[]{:S(2)}) %collective-permute-start.19) | collective-permute-done | bytes 65568 | tf_op jit(solution)/shard_map/ppermute | solution.py:276
  122.0 2.6 %all-to-all-done.5.gathered = bf16[16,80,256]{2,1,0:T(8,128)(2,1)S(1)} async-done(((bf16[16,80,256]{2,1,0:T(8,128)(2,1)}), bf16[16,80,256]{2,1,0:T(8,128)(2,1)S(1)}, u32[]{:S(2)}, u32[]{:S(2)}) %all-to-all-start.5) | async-done | bytes 655392 | tf_op jit(solution)/shard_map/all_to_all | solution.py:277
  124.6 2.2 %copy-done.3 = bf16[8,1,4,256,256]{4,3,2,1,0:T(8,128)(2,1)S(1)} copy-done((bf16[8,1,4,256,256]{4,3,2,1,0:T(8,128)(2,1)S(1)}, bf16[8,1,4,256,256]{4,3,2,1,0:T(8,128)(2,1)}, u32[]{:S(2)}) %copy-start.3) | copy-done | bytes 4194328
  126.7 3.5 %shard_map.65 = (bf16[16,64,256]{2,1,0:T(8,128)(2,1)}, f32[4,72,256]{2,1,0:T(8,128)S(1)}, f32[4,72,256]{2,1,0:T(8,128)S(1)}) custom-call(s32[128]{0:T(128)S(1)} %get-tuple-element.25.meta, bf16[8,4,256,256]{3,2,1,0:T(8,128)(2,1)S(1)} %bitcast.45, bf16[16,80,256]{2,1,0:T(8,128)(2,1)S(1)} %all-to-all-done.5.gathered, ...), custom_call_target="tpu_custom_call" | custom-call | flops 536870912 | bytes 4194304 | tf_op jit(solution)/shard_map/pallas_call | solution.py:279
  130.2 2.3 %collective-permute-start.20 = (f32[4,72,256]{2,1,0:T(8,128)S(1)}, f32[4,72,256]{2,1,0:T(8,128)S(1)}, u32[]{:S(2)}, u32[]{:S(2)}) collective-permute-start(f32[4,72,256]{2,1,0:T(8,128)S(1)} %get-tuple-element.44), channel_id=1, source_target_pairs={{0,1},{1,0},{2,3},{3,2},{4,5},{5,4},{6,7},{7,6},{8,9},{9,8},{10,11... | collective-permute-start | bytes 884744 | tf_op jit(solution)/shard_map/ppermute | solution.py:288
  132.5 3.6 %all-to-all-start.6 = ((bf16[16,64,256]{2,1,0:T(8,128)(2,1)}), bf16[16,64,256]{2,1,0:T(8,128)(2,1)S(1)}, u32[]{:S(2)}, u32[]{:S(2)}) async-start(bf16[16,64,256]{2,1,0:T(8,128)(2,1)} %get-tuple-element.42), calls=%async_computation.6 | async-start | bytes 1048576 | tf_op jit(solution)/shard_map/all_to_all | solution.py:287
  137.8 3.8 %collective-permute-done.23.refs_4_ = f32[72,256]{1,0:T(8,128)S(1)} collective-permute-done((f32[72,256]{1,0:T(8,128)S(1)}, f32[72,256]{1,0:T(8,128)S(1)}, u32[]{:S(2)}, u32[]{:S(2)}) %collective-permute-start.23) | collective-permute-done | bytes 73760 | tf_op jit(solution)/shard_map/ppermute | solution.py:290
  143.0 3.6 %all-to-all-done.6.refs_0_ = bf16[16,64,256]{2,1,0:T(8,128)(2,1)S(1)} async-done(((bf16[16,64,256]{2,1,0:T(8,128)(2,1)}), bf16[16,64,256]{2,1,0:T(8,128)(2,1)S(1)}, u32[]{:S(2)}, u32[]{:S(2)}) %all-to-all-start.6) | async-done | bytes 524320 | tf_op jit(solution)/shard_map/all_to_all | solution.py:287
  147.0 14.2 %all_to_all.53 = f32[128,1,128]{2,1,0:T(1,128)S(1)} all-to-all(f32[128,1,128]{2,1,0:T(1,128)S(1)} %bitcast.55), channel_id=1, replica_groups=mesh['row'=16,'col'=8] {'row','col'}, dimensions={0} | all-to-all | bytes 131072 | tf_op jit(solution)/shard_map/all_to_all | solution.py:310
  (63 shorter events, 35.1 us)
Async XLA Ops:
  4.4 25.1 %copy-start.4 = (bf16[64,256]{1,0:T(8,128)(2,1)S(1)}, bf16[64,256]{1,0:T(8,128)(2,1)}, u32[]{:S(2)}) copy-start(bf16[64,256]{1,0:T(8,128)(2,1)} %refs_2_.1) | copy-start | bytes 98308
  30.6 15.1 %all-to-all-start.1 = ((bf16[16,80,256]{2,1,0:T(8,128)(2,1)}), bf16[16,80,256]{2,1,0:T(8,128)(2,1)S(1)}, u32[]{:S(2)}, u32[]{:S(2)}) async-start(bf16[16,80,256]{2,1,0:T(8,128)(2,1)} %get-tuple-element.27), calls=%async_computation.1 | async-start | bytes 1310720 | tf_op jit(solution)/shard_map/all_to_all | solution.py:277
  34.2 1.9 %collective-permute-start = (bf16[64,256]{1,0:T(8,128)(2,1)S(1)}, bf16[64,256]{1,0:T(8,128)(2,1)S(1)}, u32[]{:S(2)}, u32[]{:S(2)}) collective-permute-start(bf16[64,256]{1,0:T(8,128)(2,1)S(1)} %get-tuple-element.28.own), channel_id=1, source_target_pairs={{0,1},{1,0},{2,3},{3,2},{4,5},{5,4},{6,7},{7,6},{8,9},{9,8},{10,11... | collective-permute-start | bytes 98312 | tf_op jit(solution)/shard_map/ppermute | solution.py:274
  36.0 4.7 %collective-permute-start.3 = (bf16[2,64,256]{2,1,0:T(8,128)(2,1)S(1)}, bf16[2,64,256]{2,1,0:T(8,128)(2,1)S(1)}, u32[]{:S(2)}, u32[]{:S(2)}) collective-permute-start(bf16[2,64,256]{2,1,0:T(8,128)(2,1)S(1)} %pad_maximum_fusion), channel_id=1, source_target_pairs={{0,4},{1,5},{2,6},{3,7},{4,0},{5,1},{6,2},{7,3},{8,12},{9,13},{10,... | collective-permute-start | bytes 196616 | tf_op jit(solution)/shard_map/ppermute | solution.py:276
  36.9 3.8 %collective-permute-start.2 = (bf16[2,64,256]{2,1,0:T(8,128)(2,1)S(1)}, bf16[2,64,256]{2,1,0:T(8,128)(2,1)S(1)}, u32[]{:S(2)}, u32[]{:S(2)}) collective-permute-start(bf16[2,64,256]{2,1,0:T(8,128)(2,1)S(1)} %pad_maximum_fusion), channel_id=1, source_target_pairs={{0,6},{1,7},{2,0},{3,1},{4,2},{5,3},{6,4},{7,5},{8,14},{9,15},{10,... | collective-permute-start | bytes 196616 | tf_op jit(solution)/shard_map/ppermute | solution.py:276
  38.6 4.6 %collective-permute-start.1 = (bf16[2,64,256]{2,1,0:T(8,128)(2,1)S(1)}, bf16[2,64,256]{2,1,0:T(8,128)(2,1)S(1)}, u32[]{:S(2)}, u32[]{:S(2)}) collective-permute-start(bf16[2,64,256]{2,1,0:T(8,128)(2,1)S(1)} %pad_maximum_fusion), channel_id=1, source_target_pairs={{0,2},{1,3},{2,4},{3,5},{4,6},{5,7},{6,0},{7,1},{8,10},{9,11},{10,... | collective-permute-start | bytes 196616 | tf_op jit(solution)/shard_map/ppermute | solution.py:276
  45.7 2.2 %copy-start.1 = (bf16[8,1,4,256,256]{4,3,2,1,0:T(8,128)(2,1)S(1)}, bf16[8,1,4,256,256]{4,3,2,1,0:T(8,128)(2,1)}, u32[]{:S(2)}) copy-start(bf16[8,1,4,256,256]{4,3,2,1,0:T(8,128)(2,1)} %param.4) | copy-start | bytes 12582916
  51.4 6.2 %collective-permute-start.4 = (f32[4,72,256]{2,1,0:T(8,128)S(1)}, f32[4,72,256]{2,1,0:T(8,128)S(1)}, u32[]{:S(2)}, u32[]{:S(2)}) collective-permute-start(f32[4,72,256]{2,1,0:T(8,128)S(1)} %get-tuple-element.31), channel_id=1, source_target_pairs={{0,1},{1,0},{2,3},{3,2},{4,5},{5,4},{6,7},{7,6},{8,9},{9,8},{10,11... | collective-permute-start | bytes 884744 | tf_op jit(solution)/shard_map/ppermute | solution.py:288
  53.6 14.0 %all-to-all-start.2 = ((bf16[16,64,256]{2,1,0:T(8,128)(2,1)}), bf16[16,64,256]{2,1,0:T(8,128)(2,1)S(1)}, u32[]{:S(2)}, u32[]{:S(2)}) async-start(bf16[16,64,256]{2,1,0:T(8,128)(2,1)} %get-tuple-element.29), calls=%async_computation.2 | async-start | bytes 1048576 | tf_op jit(solution)/shard_map/all_to_all | solution.py:287
  57.6 5.2 %collective-permute-start.7 = (f32[72,256]{1,0:T(8,128)S(1)}, f32[72,256]{1,0:T(8,128)S(1)}, u32[]{:S(2)}, u32[]{:S(2)}) collective-permute-start(f32[72,256]{1,0:T(8,128)S(1)} %get-tuple-element.56), channel_id=1, source_target_pairs={{0,4},{1,5},{2,6},{3,7},{4,0},{5,1},{6,2},{7,3},{8,12},{9,13},{10,... | collective-permute-start | bytes 221192 | tf_op jit(solution)/shard_map/ppermute | solution.py:290
  58.7 4.3 %collective-permute-start.6 = (f32[72,256]{1,0:T(8,128)S(1)}, f32[72,256]{1,0:T(8,128)S(1)}, u32[]{:S(2)}, u32[]{:S(2)}) collective-permute-start(f32[72,256]{1,0:T(8,128)S(1)} %get-tuple-element.57), channel_id=1, source_target_pairs={{0,6},{1,7},{2,0},{3,1},{4,2},{5,3},{6,4},{7,5},{8,14},{9,15},{10,... | collective-permute-start | bytes 221192 | tf_op jit(solution)/shard_map/ppermute | solution.py:290
  60.3 4.7 %collective-permute-start.5 = (f32[72,256]{1,0:T(8,128)S(1)}, f32[72,256]{1,0:T(8,128)S(1)}, u32[]{:S(2)}, u32[]{:S(2)}) collective-permute-start(f32[72,256]{1,0:T(8,128)S(1)} %get-tuple-element.58), channel_id=1, source_target_pairs={{0,2},{1,3},{2,4},{3,5},{4,6},{5,7},{6,0},{7,1},{8,10},{9,11},{10,... | collective-permute-start | bytes 221192 | tf_op jit(solution)/shard_map/ppermute | solution.py:290
  68.8 15.9 %all-to-all-start.3 = ((bf16[16,80,256]{2,1,0:T(8,128)(2,1)}), bf16[16,80,256]{2,1,0:T(8,128)(2,1)S(1)}, u32[]{:S(2)}, u32[]{:S(2)}) async-start(bf16[16,80,256]{2,1,0:T(8,128)(2,1)} %get-tuple-element.33), calls=%async_computation.3 | async-start | bytes 1310720 | tf_op jit(solution)/shard_map/all_to_all | solution.py:277
  73.2 2.5 %collective-permute-start.8 = (bf16[64,256]{1,0:T(8,128)(2,1)S(1)}, bf16[64,256]{1,0:T(8,128)(2,1)S(1)}, u32[]{:S(2)}, u32[]{:S(2)}) collective-permute-start(bf16[64,256]{1,0:T(8,128)(2,1)S(1)} %get-tuple-element.34.own), channel_id=1, source_target_pairs={{0,1},{1,0},{2,3},{3,2},{4,5},{5,4},{6,7},{7,6},{8,9},{9,8},{10,11... | collective-permute-start | bytes 98312 | tf_op jit(solution)/shard_map/ppermute | solution.py:274
  75.7 4.7 %collective-permute-start.11 = (bf16[2,64,256]{2,1,0:T(8,128)(2,1)S(1)}, bf16[2,64,256]{2,1,0:T(8,128)(2,1)S(1)}, u32[]{:S(2)}, u32[]{:S(2)}) collective-permute-start(bf16[2,64,256]{2,1,0:T(8,128)(2,1)S(1)} %pad_maximum_fusion.1), channel_id=1, source_target_pairs={{0,4},{1,5},{2,6},{3,7},{4,0},{5,1},{6,2},{7,3},{8,12},{9,13},{10,... | collective-permute-start | bytes 196616 | tf_op jit(solution)/shard_map/ppermute | solution.py:276
  76.7 3.8 %collective-permute-start.10 = (bf16[2,64,256]{2,1,0:T(8,128)(2,1)S(1)}, bf16[2,64,256]{2,1,0:T(8,128)(2,1)S(1)}, u32[]{:S(2)}, u32[]{:S(2)}) collective-permute-start(bf16[2,64,256]{2,1,0:T(8,128)(2,1)S(1)} %pad_maximum_fusion.1), channel_id=1, source_target_pairs={{0,6},{1,7},{2,0},{3,1},{4,2},{5,3},{6,4},{7,5},{8,14},{9,15},{10,... | collective-permute-start | bytes 196616 | tf_op jit(solution)/shard_map/ppermute | solution.py:276
  78.3 4.6 %collective-permute-start.9 = (bf16[2,64,256]{2,1,0:T(8,128)(2,1)S(1)}, bf16[2,64,256]{2,1,0:T(8,128)(2,1)S(1)}, u32[]{:S(2)}, u32[]{:S(2)}) collective-permute-start(bf16[2,64,256]{2,1,0:T(8,128)(2,1)S(1)} %pad_maximum_fusion.1), channel_id=1, source_target_pairs={{0,2},{1,3},{2,4},{3,5},{4,6},{5,7},{6,0},{7,1},{8,10},{9,11},{10,... | collective-permute-start | bytes 196616 | tf_op jit(solution)/shard_map/ppermute | solution.py:276
  90.4 6.8 %collective-permute-start.12 = (f32[4,72,256]{2,1,0:T(8,128)S(1)}, f32[4,72,256]{2,1,0:T(8,128)S(1)}, u32[]{:S(2)}, u32[]{:S(2)}) collective-permute-start(f32[4,72,256]{2,1,0:T(8,128)S(1)} %get-tuple-element.37), channel_id=1, source_target_pairs={{0,1},{1,0},{2,3},{3,2},{4,5},{5,4},{6,7},{7,6},{8,9},{9,8},{10,11... | collective-permute-start | bytes 884744 | tf_op jit(solution)/shard_map/ppermute | solution.py:288
  92.8 14.6 %all-to-all-start.4 = ((bf16[16,64,256]{2,1,0:T(8,128)(2,1)}), bf16[16,64,256]{2,1,0:T(8,128)(2,1)S(1)}, u32[]{:S(2)}, u32[]{:S(2)}) async-start(bf16[16,64,256]{2,1,0:T(8,128)(2,1)} %get-tuple-element.35), calls=%async_computation.4 | async-start | bytes 1048576 | tf_op jit(solution)/shard_map/all_to_all | solution.py:287
  97.3 5.2 %collective-permute-start.15 = (f32[72,256]{1,0:T(8,128)S(1)}, f32[72,256]{1,0:T(8,128)S(1)}, u32[]{:S(2)}, u32[]{:S(2)}) collective-permute-start(f32[72,256]{1,0:T(8,128)S(1)} %get-tuple-element.52), channel_id=1, source_target_pairs={{0,4},{1,5},{2,6},{3,7},{4,0},{5,1},{6,2},{7,3},{8,12},{9,13},{10,... | collective-permute-start | bytes 221192 | tf_op jit(solution)/shard_map/ppermute | solution.py:290
  97.4 5.1 %collective-permute-start.14 = (f32[72,256]{1,0:T(8,128)S(1)}, f32[72,256]{1,0:T(8,128)S(1)}, u32[]{:S(2)}, u32[]{:S(2)}) collective-permute-start(f32[72,256]{1,0:T(8,128)S(1)} %get-tuple-element.53), channel_id=1, source_target_pairs={{0,6},{1,7},{2,0},{3,1},{4,2},{5,3},{6,4},{7,5},{8,14},{9,15},{10,... | collective-permute-start | bytes 221192 | tf_op jit(solution)/shard_map/ppermute | solution.py:290
  98.9 5.1 %collective-permute-start.13 = (f32[72,256]{1,0:T(8,128)S(1)}, f32[72,256]{1,0:T(8,128)S(1)}, u32[]{:S(2)}, u32[]{:S(2)}) collective-permute-start(f32[72,256]{1,0:T(8,128)S(1)} %get-tuple-element.54), channel_id=1, source_target_pairs={{0,2},{1,3},{2,4},{3,5},{4,6},{5,7},{6,0},{7,1},{8,10},{9,11},{10,... | collective-permute-start | bytes 221192 | tf_op jit(solution)/shard_map/ppermute | solution.py:290
  108.6 16.0 %all-to-all-start.5 = ((bf16[16,80,256]{2,1,0:T(8,128)(2,1)}), bf16[16,80,256]{2,1,0:T(8,128)(2,1)S(1)}, u32[]{:S(2)}, u32[]{:S(2)}) async-start(bf16[16,80,256]{2,1,0:T(8,128)(2,1)} %get-tuple-element.40), calls=%async_computation.5 | async-start | bytes 1310720 | tf_op jit(solution)/shard_map/all_to_all | solution.py:277
  113.0 2.5 %collective-permute-start.16 = (bf16[64,256]{1,0:T(8,128)(2,1)S(1)}, bf16[64,256]{1,0:T(8,128)(2,1)S(1)}, u32[]{:S(2)}, u32[]{:S(2)}) collective-permute-start(bf16[64,256]{1,0:T(8,128)(2,1)S(1)} %get-tuple-element.41.own), channel_id=1, source_target_pairs={{0,1},{1,0},{2,3},{3,2},{4,5},{5,4},{6,7},{7,6},{8,9},{9,8},{10,11... | collective-permute-start | bytes 98312 | tf_op jit(solution)/shard_map/ppermute | solution.py:274
  115.5 4.7 %collective-permute-start.19 = (bf16[2,64,256]{2,1,0:T(8,128)(2,1)S(1)}, bf16[2,64,256]{2,1,0:T(8,128)(2,1)S(1)}, u32[]{:S(2)}, u32[]{:S(2)}) collective-permute-start(bf16[2,64,256]{2,1,0:T(8,128)(2,1)S(1)} %pad_maximum_fusion.2), channel_id=1, source_target_pairs={{0,4},{1,5},{2,6},{3,7},{4,0},{5,1},{6,2},{7,3},{8,12},{9,13},{10,... | collective-permute-start | bytes 196616 | tf_op jit(solution)/shard_map/ppermute | solution.py:276
  115.5 4.6 %collective-permute-start.18 = (bf16[2,64,256]{2,1,0:T(8,128)(2,1)S(1)}, bf16[2,64,256]{2,1,0:T(8,128)(2,1)S(1)}, u32[]{:S(2)}, u32[]{:S(2)}) collective-permute-start(bf16[2,64,256]{2,1,0:T(8,128)(2,1)S(1)} %pad_maximum_fusion.2), channel_id=1, source_target_pairs={{0,6},{1,7},{2,0},{3,1},{4,2},{5,3},{6,4},{7,5},{8,14},{9,15},{10,... | collective-permute-start | bytes 196616 | tf_op jit(solution)/shard_map/ppermute | solution.py:276
  117.0 5.0 %collective-permute-start.17 = (bf16[2,64,256]{2,1,0:T(8,128)(2,1)S(1)}, bf16[2,64,256]{2,1,0:T(8,128)(2,1)S(1)}, u32[]{:S(2)}, u32[]{:S(2)}) collective-permute-start(bf16[2,64,256]{2,1,0:T(8,128)(2,1)S(1)} %pad_maximum_fusion.2), channel_id=1, source_target_pairs={{0,2},{1,3},{2,4},{3,5},{4,6},{5,7},{6,0},{7,1},{8,10},{9,11},{10,... | collective-permute-start | bytes 196616 | tf_op jit(solution)/shard_map/ppermute | solution.py:276
  130.2 5.9 %collective-permute-start.20 = (f32[4,72,256]{2,1,0:T(8,128)S(1)}, f32[4,72,256]{2,1,0:T(8,128)S(1)}, u32[]{:S(2)}, u32[]{:S(2)}) collective-permute-start(f32[4,72,256]{2,1,0:T(8,128)S(1)} %get-tuple-element.44), channel_id=1, source_target_pairs={{0,1},{1,0},{2,3},{3,2},{4,5},{5,4},{6,7},{7,6},{8,9},{9,8},{10,11... | collective-permute-start | bytes 884744 | tf_op jit(solution)/shard_map/ppermute | solution.py:288
  132.5 14.1 %all-to-all-start.6 = ((bf16[16,64,256]{2,1,0:T(8,128)(2,1)}), bf16[16,64,256]{2,1,0:T(8,128)(2,1)S(1)}, u32[]{:S(2)}, u32[]{:S(2)}) async-start(bf16[16,64,256]{2,1,0:T(8,128)(2,1)} %get-tuple-element.42), calls=%async_computation.6 | async-start | bytes 1048576 | tf_op jit(solution)/shard_map/all_to_all | solution.py:287
  136.2 5.4 %collective-permute-start.23 = (f32[72,256]{1,0:T(8,128)S(1)}, f32[72,256]{1,0:T(8,128)S(1)}, u32[]{:S(2)}, u32[]{:S(2)}) collective-permute-start(f32[72,256]{1,0:T(8,128)S(1)} %get-tuple-element.48), channel_id=1, source_target_pairs={{0,4},{1,5},{2,6},{3,7},{4,0},{5,1},{6,2},{7,3},{8,12},{9,13},{10,... | collective-permute-start | bytes 221192 | tf_op jit(solution)/shard_map/ppermute | solution.py:290
  136.3 5.3 %collective-permute-start.22 = (f32[72,256]{1,0:T(8,128)S(1)}, f32[72,256]{1,0:T(8,128)S(1)}, u32[]{:S(2)}, u32[]{:S(2)}) collective-permute-start(f32[72,256]{1,0:T(8,128)S(1)} %get-tuple-element.49), channel_id=1, source_target_pairs={{0,6},{1,7},{2,0},{3,1},{4,2},{5,3},{6,4},{7,5},{8,14},{9,15},{10,... | collective-permute-start | bytes 221192 | tf_op jit(solution)/shard_map/ppermute | solution.py:290
  137.6 5.4 %collective-permute-start.21 = (f32[72,256]{1,0:T(8,128)S(1)}, f32[72,256]{1,0:T(8,128)S(1)}, u32[]{:S(2)}, u32[]{:S(2)}) collective-permute-start(f32[72,256]{1,0:T(8,128)S(1)} %get-tuple-element.50), channel_id=1, source_target_pairs={{0,2},{1,3},{2,4},{3,5},{4,6},{5,7},{6,0},{7,1},{8,10},{9,11},{10,... | collective-permute-start | bytes 221192 | tf_op jit(solution)/shard_map/ppermute | solution.py:290
  (3 other events, 6.6 us)

commit v3 on v2

--- a/solution.py
+++ b/solution.py
@@ -18,6 +18,8 @@
 SLOTS_OF = 64
 META = 128
 BACK = BF16
+CHUNK = 2
+KEPT = 3
 EXTRA = 16
 
 
@@ -56,9 +58,13 @@
     return wide[:cells, 0:1], wide[:cells, 1:2]
 
 
-def degree_kernel(place, columns, counts, tiles, message, meta, row_sums, col_sums, used):
+def degree_kernel(
+    place, columns, counts, tiles, message, meta, near, row_sums, col_sums, used, done
+):
     panels, slots, tile = tiles.shape[0], tiles.shape[1], tiles.shape[2]
     row_devices = message.shape[0]
+    keeping = pltpu.make_async_copy(tiles.at[: near.shape[0]], near, done)
+    keeping.start()
     mine_row, mine_col = place[0], place[1]
     meta[0] = mine_row
     meta[1] = mine_col
@@ -81,18 +87,21 @@
             weight = jnp.where(live, ones, jnp.zeros_like(ones))
             value = tiles[i, s]
             total = total + nt(weight, value)
-            col_sums[i * slots + s] = nn(weight, value)[:8]
+            wide = jnp.sum(value.astype(F32).reshape(tile // 8, 8, tile), axis=0)
+            col_sums[i * slots + s] = jnp.where(live, wide, jnp.zeros_like(wide))
         row_sums[i : i + 1, :] = total[:1]
     rows = row_sums[...]
     everything = jnp.sum(jnp.sum(rows, axis=1, keepdims=True), axis=0, keepdims=True)
     for b in range(row_devices):
         first = meta[SLOTS_OF + 2 * b] % EMPTY
         second = meta[SLOTS_OF + 2 * b + 1] % EMPTY
-        part = col_sums[first] + col_sums[second]
+        part = jnp.sum(col_sums[first] + col_sums[second], axis=0, keepdims=True)
+        part = jnp.broadcast_to(part, rows.shape)
         at = lax.broadcasted_iota(jnp.int32, part.shape, 0)
         part = jnp.where(at == mine_col, part, 0.0) + jnp.where(b == mine_row, rows, 0.0)
         message[b, :, :tile] = part
         message[b, :, tile:] = jnp.broadcast_to(everything, (part.shape[0], 128))
+    keeping.wait()
 
 
 def pack(values, dots, many, one):
@@ -124,10 +133,21 @@
 
 
 def product_kernel(
-    meta, tiles, gathered, own, pair, far1, far3, far2, result, keep, give, buffer
+    meta, near_tiles, stored, gathered, own, pair, far1, far3, far2, result, keep, give,
+    buffer, parts, far_tiles, arrived,
 ):
-    panels, slots = tiles.shape[0], tiles.shape[1]
+    split, slots = near_tiles.shape[0], near_tiles.shape[1]
+    panels = stored.shape[0]
     cells = own.shape[0]
+    fetch = {}
+    for first in range(split, panels, CHUNK):
+        last = min(first + CHUNK, panels)
+        fetch[first] = pltpu.make_async_copy(
+            stored.at[first:last],
+            far_tiles.at[first - split : last - split],
+            arrived.at[(first - split) // CHUNK],
+        )
+        fetch[first].start()
     zs = panels // 2
     z, core = meta[1] // 2, meta[1] % 2
     dots = jnp.zeros((8, 128), F32)
@@ -135,32 +155,39 @@
         tail = gathered[b, cells:, :128].astype(F32)
         dots = dots + tail[:8] + tail[8:]
     dots = jnp.concatenate([dots, jnp.zeros_like(dots)], axis=1)
-    for k in range(zs):
-        at = (z + k) % zs
-        for target, i in ((keep, 2 * at + core), (give, 2 * at + 1 - core)):
-            total = None
-            for s in range(slots):
-                held = meta[COLUMNS + i * slots + s]
-                panel = gathered[held % EMPTY, :cells]
-                panel = jnp.where(held < EMPTY, panel, jnp.zeros_like(panel))
-                part = nt(panel, tiles[i, s])
-                total = part if total is None else total + part
-            target[k, :cells] = total
-            target[k, cells:] = dots
     for k, source in ((0, None), (1, far1), (2, far2), (3, far3)):
         at = (z + zs - k) % zs
         same = own[...] if source is None else source[0]
         other = pair[...] if source is None else source[1]
         buffer[2 * at + core] = same
         buffer[2 * at + 1 - core] = other
+    for at in range(zs):
+        k = (at + zs - z) % zs
+        totals = []
+        for i in (2 * at, 2 * at + 1):
+            if i in fetch:
+                fetch[i].wait()
+            tiles, row = (near_tiles, i) if i < split else (far_tiles, i - split)
+            mine = buffer[i]
+            total = None
+            for s in range(slots):
+                held = meta[COLUMNS + i * slots + s]
+                panel = gathered[held % EMPTY, :cells]
+                panel = jnp.where(held < EMPTY, panel, jnp.zeros_like(panel))
+                part = nt(panel, tiles[row, s])
+                total = part if total is None else total + part
+                parts[i * slots + s] = nn(mine, tiles[row, s])
+            totals.append(total)
+        keep[k, :cells] = jnp.where(core == 0, totals[0], totals[1])
+        give[k, :cells] = jnp.where(core == 0, totals[1], totals[0])
+        keep[k, cells:] = dots
+        give[k, cells:] = dots
     for b in range(result.shape[0]):
         total = None
         for m in range(2):
             held = meta[SLOTS_OF + 2 * b + m]
-            q = held % EMPTY
-            panel = buffer[q // slots]
-            panel = jnp.where(held < EMPTY, panel, jnp.zeros_like(panel))
-            part = nn(panel, tiles[q // slots, q % slots])
+            part = parts[held % EMPTY]
+            part = jnp.where(held < EMPTY, part, jnp.zeros_like(part))
             total = part if total is None else total + part
         result[b] = total.astype(result.dtype)
 
@@ -236,6 +263,7 @@
     zs = cols // 2
     total_cells = rows * cols * tile
     tiles = tile_values.reshape(panels, slots, tile, tile)
+    stored = pltpu.with_memory_space_constraint(tiles, pltpu.HBM)
     place = jnp.stack([lax.axis_index("row"), lax.axis_index("col")]).astype(jnp.int32)
     shape = jax.ShapeDtypeStruct
     swap = [(i, i ^ 1) for i in range(cols)]
@@ -243,15 +271,20 @@
     tile_bytes = panels * slots * tile * tile * 2
     work = 2 * panels * slots * cells * tile * tile
 
-    message, meta = call(
+    message, meta, near_tiles = call(
         degree_kernel,
-        (shape((rows, cols, tile + 128), F32), shape((META,), jnp.int32)),
+        (
+            shape((rows, cols, tile + 128), F32),
+            shape((META,), jnp.int32),
+            shape((KEPT, slots, tile, tile), BF16),
+        ),
         [SMEM, SMEM, SMEM, VMEM],
-        (VMEM, SMEM),
+        (VMEM, SMEM, VMEM),
         [
             pltpu.VMEM((panels, tile), F32),
             pltpu.VMEM((panels * slots, 8, tile), F32),
             pltpu.SMEM((rows,), jnp.int32),
+            pltpu.SemaphoreType.DMA,
         ],
         work / 4,
         tile_bytes,
@@ -279,11 +312,16 @@
         back, keep, give = call(
             product_kernel,
             (shape((rows, cells, tile), BACK), side_shape, side_shape),
-            [SMEM] + [VMEM] * 7,
-            scratch=[pltpu.VMEM((panels, cells, tile), BF16)],
+            [SMEM, VMEM, pl.BlockSpec(memory_space=pltpu.HBM)] + [VMEM] * 6,
+            scratch=[
+                pltpu.VMEM((panels, cells, tile), BF16),
+                pltpu.VMEM((panels * slots, cells, tile), F32),
+                pltpu.VMEM((panels - KEPT, slots, tile, tile), BF16),
+                pltpu.SemaphoreType.DMA((pl.cdiv(panels - KEPT, CHUNK),)),
+            ],
             flops=2 * work,
             moved=tile_bytes,
-        )(meta, tiles, gathered, one, pair, *near)
+        )(meta, near_tiles, stored, gathered, one, pair, *near)
         back = lax.all_to_all(back, "row", 0, 0, tiled=True)
         given = lax.ppermute(give, "col", swap)
         sums = keep + given

time: 163 us -> 161 us (0.988)
  local copies, waits for them, and re-layouts: 10.5 us -> 3.96 us
  Pallas kernels: 18.3 us -> 22.7 us
    unnamed x13 -> x7, local copies, waits for them, and re-layouts: 10.3 us -> 3.69 us
    pallas_call x3, Pallas kernels: 10.4 us -> 15.2 us  [local(): call(product_kernel, (shape((rows, cells, tile), BACK), side_shape, side_...]
where the time goes in v3:
time: 161 us; the launch traced here: 160 us
  starting transfers between devices  48.6 us (30%)
  waiting for transfers between devices  47.8 us (30%)
  blocking collectives  35.9 us (22%)
  Pallas kernels  22.7 us (14%)
  local copies, waits for them, and re-layouts  3.96 us (2%)
    all_to_all x1, blocking collectives, local(): lax.all_to_all(message.reshape(rows * cols, tile + 128), ('row', 'col'),...  21.7 us
    pallas_call x3, Pallas kernels, local(): call(product_kernel, (shape((rows, cells, tile), BACK), side_shape, side_...  15.2 us
    ppermute x9, waiting for transfers between devices, local(): lax.ppermute(sums[k], 'col', shift(k))  14.8 us
    all_to_all x1, blocking collectives, local(): norms = lax.all_to_all(norms, ('row', 'col'), 0, 0, tiled=True)  14.2 us
    ppermute x9, waiting for transfers between devices, local(): near = [lax.ppermute(both, 'col', shift(k)) for k in (1, 3, 2)]  14.2 us
    all_to_all x3, starting transfers between devices, local(): gathered = lax.all_to_all(many, 'row', 0, 0, tiled=True)  12.3 us
    all_to_all x3, starting transfers between devices, local(): back = lax.all_to_all(back, 'row', 0, 0, tiled=True)  11.9 us
    all_to_all x3, waiting for transfers between devices, local(): back = lax.all_to_all(back, 'row', 0, 0, tiled=True)  9.75 us
  transfers between devices with their start and end apart: 30, of which 23 were waited for; matrix products, arithmetic and copies ran while one was open for 0% of the time, Pallas kernels for 0%

profile of v3, /device:TPU:1, one launch (start us, length us, event | category | flops | bytes accessed | tf_op | source)
XLA Modules:
  0.0 160.0 jit_solution(2873054307715033626)
XLA Ops:
  2.2 2.2 %copy-done = bf16[8,1,4,256,256]{4,3,2,1,0:T(8,128)(2,1)S(1)} copy-done((bf16[8,1,4,256,256]{4,3,2,1,0:T(8,128)(2,1)S(1)}, bf16[8,1,4,256,256]{4,3,2,1,0:T(8,128)(2,1)}, u32[]{:S(2)}) %copy-start) | copy-done | bytes 4194328
  4.4 2.7 %shard_map.59 = (f32[16,8,384]{2,1,0:T(8,128)S(1)}, s32[128]{0:T(128)S(1)}, bf16[3,4,256,256]{3,2,1,0:T(8,128)(2,1)S(1)}) custom-call(s32[2]{0:T(128)S(1)} %pad_add_fusion.place, s32[8,1,4]{2,1,0:T(1,128)S(1)} %copy.8.columns, s32[8,1]{1,0:T(8,128)S(1)} %copy.9.counts, bf16[8,4,256,256]{3,2,1,0:T(8,128)(2,1)S(1)} %bitcast.45), custom_call_target="tpu_custom_call" | custom-call | flops 67108864 | bytes 4194304 | tf_op jit(solution)/shard_map/pallas_call | solution.py:274
  7.3 21.7 %all_to_all.52 = f32[128,1,384]{2,1,0:T(1,128)S(1)} all-to-all(f32[128,1,384]{2,1,0:T(1,128)S(1)} %copy.10), channel_id=1, replica_groups=mesh['row'=16,'col'=8] {'row','col'}, dimensions={0} | all-to-all | bytes 393216 | tf_op jit(solution)/shard_map/all_to_all | solution.py:292
  30.2 3.6 %all-to-all-start.1 = ((bf16[16,80,256]{2,1,0:T(8,128)(2,1)}), bf16[16,80,256]{2,1,0:T(8,128)(2,1)S(1)}, u32[]{:S(2)}, u32[]{:S(2)}) async-start(bf16[16,80,256]{2,1,0:T(8,128)(2,1)} %get-tuple-element.29), calls=%async_computation.1 | async-start | bytes 1310720 | tf_op jit(solution)/shard_map/all_to_all | solution.py:310
  36.5 1.8 %collective-permute-start.2 = (bf16[2,64,256]{2,1,0:T(8,128)(2,1)S(1)}, bf16[2,64,256]{2,1,0:T(8,128)(2,1)S(1)}, u32[]{:S(2)}, u32[]{:S(2)}) collective-permute-start(bf16[2,64,256]{2,1,0:T(8,128)(2,1)S(1)} %pad_maximum_fusion), channel_id=1, source_target_pairs={{0,6},{1,7},{2,0},{3,1},{4,2},{5,3},{6,4},{7,5},{8,14},{9,15},{10,... | collective-permute-start | bytes 196616 | tf_op jit(solution)/shard_map/ppermute | solution.py:309
  38.2 2.1 %collective-permute-done.3.far2 = bf16[2,64,256]{2,1,0:T(8,128)(2,1)S(1)} collective-permute-done((bf16[2,64,256]{2,1,0:T(8,128)(2,1)S(1)}, bf16[2,64,256]{2,1,0:T(8,128)(2,1)S(1)}, u32[]{:S(2)}, u32[]{:S(2)}) %collective-permute-start.3) | collective-permute-done | bytes 65568 | tf_op jit(solution)/shard_map/ppermute | solution.py:309
  40.3 2.5 %collective-permute-done.1.far1 = bf16[2,64,256]{2,1,0:T(8,128)(2,1)S(1)} collective-permute-done((bf16[2,64,256]{2,1,0:T(8,128)(2,1)S(1)}, bf16[2,64,256]{2,1,0:T(8,128)(2,1)S(1)}, u32[]{:S(2)}, u32[]{:S(2)}) %collective-permute-start.1) | collective-permute-done | bytes 65568 | tf_op jit(solution)/shard_map/ppermute | solution.py:309
  42.8 2.5 %all-to-all-done.1.gathered = bf16[16,80,256]{2,1,0:T(8,128)(2,1)S(1)} async-done(((bf16[16,80,256]{2,1,0:T(8,128)(2,1)}), bf16[16,80,256]{2,1,0:T(8,128)(2,1)S(1)}, u32[]{:S(2)}, u32[]{:S(2)}) %all-to-all-start.1) | async-done | bytes 655392 | tf_op jit(solution)/shard_map/all_to_all | solution.py:310
  45.3 5.1 %shard_map.61 = (bf16[16,64,256]{2,1,0:T(8,128)(2,1)}, f32[4,72,256]{2,1,0:T(8,128)S(1)}, f32[4,72,256]{2,1,0:T(8,128)S(1)}) custom-call(s32[128]{0:T(128)S(1)} %get-tuple-element.26.meta, bf16[3,4,256,256]{3,2,1,0:T(8,128)(2,1)S(1)} %get-tuple-element.27.near_tiles, bf16[8,4,256,256]{3,2,1,0:T(8,128)(2,1)} %bitcast.42, ...), custom_call_target="tpu_custom_call" | custom-call | flops 536870912 | bytes 4194304 | tf_op jit(solution)/shard_map/pallas_call | solution.py:312
  50.4 2.3 %collective-permute-start.4 = (f32[4,72,256]{2,1,0:T(8,128)S(1)}, f32[4,72,256]{2,1,0:T(8,128)S(1)}, u32[]{:S(2)}, u32[]{:S(2)}) collective-permute-start(f32[4,72,256]{2,1,0:T(8,128)S(1)} %get-tuple-element.33), channel_id=1, source_target_pairs={{0,1},{1,0},{2,3},{3,2},{4,5},{5,4},{6,7},{7,6},{8,9},{9,8},{10,11... | collective-permute-start | bytes 884744 | tf_op jit(solution)/shard_map/ppermute | solution.py:326
  52.7 3.9 %all-to-all-start.2 = ((bf16[16,64,256]{2,1,0:T(8,128)(2,1)}), bf16[16,64,256]{2,1,0:T(8,128)(2,1)S(1)}, u32[]{:S(2)}, u32[]{:S(2)}) async-start(bf16[16,64,256]{2,1,0:T(8,128)(2,1)} %get-tuple-element.31), calls=%async_computation.2 | async-start | bytes 1048576 | tf_op jit(solution)/shard_map/all_to_all | solution.py:325
  59.4 2.5 %collective-permute-done.7.far2 = f32[72,256]{1,0:T(8,128)S(1)} collective-permute-done((f32[72,256]{1,0:T(8,128)S(1)}, f32[72,256]{1,0:T(8,128)S(1)}, u32[]{:S(2)}, u32[]{:S(2)}) %collective-permute-start.7) | collective-permute-done | bytes 73760 | tf_op jit(solution)/shard_map/ppermute | solution.py:328
  62.1 2.0 %collective-permute-done.5.far1 = f32[72,256]{1,0:T(8,128)S(1)} collective-permute-done((f32[72,256]{1,0:T(8,128)S(1)}, f32[72,256]{1,0:T(8,128)S(1)}, u32[]{:S(2)}, u32[]{:S(2)}) %collective-permute-start.5) | collective-permute-done | bytes 73760 | tf_op jit(solution)/shard_map/ppermute | solution.py:328
  64.1 2.7 %all-to-all-done.2.tile_sums = bf16[16,64,256]{2,1,0:T(8,128)(2,1)S(1)} async-done(((bf16[16,64,256]{2,1,0:T(8,128)(2,1)}), bf16[16,64,256]{2,1,0:T(8,128)(2,1)S(1)}, u32[]{:S(2)}, u32[]{:S(2)}) %all-to-all-start.2) | async-done | bytes 524320 | tf_op jit(solution)/shard_map/all_to_all | solution.py:325
  67.9 4.3 %all-to-all-start.3 = ((bf16[16,80,256]{2,1,0:T(8,128)(2,1)}), bf16[16,80,256]{2,1,0:T(8,128)(2,1)S(1)}, u32[]{:S(2)}, u32[]{:S(2)}) async-start(bf16[16,80,256]{2,1,0:T(8,128)(2,1)} %get-tuple-element.35), calls=%async_computation.3 | async-start | bytes 1310720 | tf_op jit(solution)/shard_map/all_to_all | solution.py:310
  77.4 2.1 %collective-permute-done.11.far2 = bf16[2,64,256]{2,1,0:T(8,128)(2,1)S(1)} collective-permute-done((bf16[2,64,256]{2,1,0:T(8,128)(2,1)S(1)}, bf16[2,64,256]{2,1,0:T(8,128)(2,1)S(1)}, u32[]{:S(2)}, u32[]{:S(2)}) %collective-permute-start.11) | collective-permute-done | bytes 65568 | tf_op jit(solution)/shard_map/ppermute | solution.py:309
  79.6 2.4 %collective-permute-done.9.far1 = bf16[2,64,256]{2,1,0:T(8,128)(2,1)S(1)} collective-permute-done((bf16[2,64,256]{2,1,0:T(8,128)(2,1)S(1)}, bf16[2,64,256]{2,1,0:T(8,128)(2,1)S(1)}, u32[]{:S(2)}, u32[]{:S(2)}) %collective-permute-start.9) | collective-permute-done | bytes 65568 | tf_op jit(solution)/shard_map/ppermute | solution.py:309
  83.5 5.1 %shard_map.63 = (bf16[16,64,256]{2,1,0:T(8,128)(2,1)}, f32[4,72,256]{2,1,0:T(8,128)S(1)}, f32[4,72,256]{2,1,0:T(8,128)S(1)}) custom-call(s32[128]{0:T(128)S(1)} %get-tuple-element.26.meta, bf16[3,4,256,256]{3,2,1,0:T(8,128)(2,1)S(1)} %get-tuple-element.27.near_tiles, bf16[8,4,256,256]{3,2,1,0:T(8,128)(2,1)} %bitcast.43, ...), custom_call_target="tpu_custom_call" | custom-call | flops 536870912 | bytes 4194304 | tf_op jit(solution)/shard_map/pallas_call | solution.py:312
  88.6 2.7 %collective-permute-start.12 = (f32[4,72,256]{2,1,0:T(8,128)S(1)}, f32[4,72,256]{2,1,0:T(8,128)S(1)}, u32[]{:S(2)}, u32[]{:S(2)}) collective-permute-start(f32[4,72,256]{2,1,0:T(8,128)S(1)} %get-tuple-element.39), channel_id=1, source_target_pairs={{0,1},{1,0},{2,3},{3,2},{4,5},{5,4},{6,7},{7,6},{8,9},{9,8},{10,11... | collective-permute-start | bytes 884744 | tf_op jit(solution)/shard_map/ppermute | solution.py:326
  91.3 4.5 %all-to-all-start.4 = ((bf16[16,64,256]{2,1,0:T(8,128)(2,1)}), bf16[16,64,256]{2,1,0:T(8,128)(2,1)S(1)}, u32[]{:S(2)}, u32[]{:S(2)}) async-start(bf16[16,64,256]{2,1,0:T(8,128)(2,1)} %get-tuple-element.37), calls=%async_computation.4 | async-start | bytes 1048576 | tf_op jit(solution)/shard_map/all_to_all | solution.py:325
  97.5 3.5 %collective-permute-done.15.refs_4_ = f32[72,256]{1,0:T(8,128)S(1)} collective-permute-done((f32[72,256]{1,0:T(8,128)S(1)}, f32[72,256]{1,0:T(8,128)S(1)}, u32[]{:S(2)}, u32[]{:S(2)}) %collective-permute-start.15) | collective-permute-done | bytes 73760 | tf_op jit(solution)/shard_map/ppermute | solution.py:328
  102.5 3.4 %all-to-all-done.4.refs_0_ = bf16[16,64,256]{2,1,0:T(8,128)(2,1)S(1)} async-done(((bf16[16,64,256]{2,1,0:T(8,128)(2,1)}), bf16[16,64,256]{2,1,0:T(8,128)(2,1)S(1)}, u32[]{:S(2)}, u32[]{:S(2)}) %all-to-all-start.4) | async-done | bytes 524320 | tf_op jit(solution)/shard_map/all_to_all | solution.py:325
  107.1 4.3 %all-to-all-start.5 = ((bf16[16,80,256]{2,1,0:T(8,128)(2,1)}), bf16[16,80,256]{2,1,0:T(8,128)(2,1)S(1)}, u32[]{:S(2)}, u32[]{:S(2)}) async-start(bf16[16,80,256]{2,1,0:T(8,128)(2,1)} %get-tuple-element.42), calls=%async_computation.5 | async-start | bytes 1310720 | tf_op jit(solution)/shard_map/all_to_all | solution.py:310
  115.6 3.1 %collective-permute-done.19.far2 = bf16[2,64,256]{2,1,0:T(8,128)(2,1)S(1)} collective-permute-done((bf16[2,64,256]{2,1,0:T(8,128)(2,1)S(1)}, bf16[2,64,256]{2,1,0:T(8,128)(2,1)S(1)}, u32[]{:S(2)}, u32[]{:S(2)}) %collective-permute-start.19) | collective-permute-done | bytes 65568 | tf_op jit(solution)/shard_map/ppermute | solution.py:309
  118.7 1.8 %collective-permute-done.17.far1 = bf16[2,64,256]{2,1,0:T(8,128)(2,1)S(1)} collective-permute-done((bf16[2,64,256]{2,1,0:T(8,128)(2,1)S(1)}, bf16[2,64,256]{2,1,0:T(8,128)(2,1)S(1)}, u32[]{:S(2)}, u32[]{:S(2)}) %collective-permute-start.17) | collective-permute-done | bytes 65568 | tf_op jit(solution)/shard_map/ppermute | solution.py:309
  120.5 2.5 %all-to-all-done.5.gathered = bf16[16,80,256]{2,1,0:T(8,128)(2,1)S(1)} async-done(((bf16[16,80,256]{2,1,0:T(8,128)(2,1)}), bf16[16,80,256]{2,1,0:T(8,128)(2,1)S(1)}, u32[]{:S(2)}, u32[]{:S(2)}) %all-to-all-start.5) | async-done | bytes 655392 | tf_op jit(solution)/shard_map/all_to_all | solution.py:310
  123.0 5.1 %shard_map.65 = (bf16[16,64,256]{2,1,0:T(8,128)(2,1)}, f32[4,72,256]{2,1,0:T(8,128)S(1)}, f32[4,72,256]{2,1,0:T(8,128)S(1)}) custom-call(s32[128]{0:T(128)S(1)} %get-tuple-element.26.meta, bf16[3,4,256,256]{3,2,1,0:T(8,128)(2,1)S(1)} %get-tuple-element.27.near_tiles, bf16[8,4,256,256]{3,2,1,0:T(8,128)(2,1)} %bitcast.44, ...), custom_call_target="tpu_custom_call" | custom-call | flops 536870912 | bytes 4194304 | tf_op jit(solution)/shard_map/pallas_call | solution.py:312
  128.1 2.4 %collective-permute-start.20 = (f32[4,72,256]{2,1,0:T(8,128)S(1)}, f32[4,72,256]{2,1,0:T(8,128)S(1)}, u32[]{:S(2)}, u32[]{:S(2)}) collective-permute-start(f32[4,72,256]{2,1,0:T(8,128)S(1)} %get-tuple-element.46), channel_id=1, source_target_pairs={{0,1},{1,0},{2,3},{3,2},{4,5},{5,4},{6,7},{7,6},{8,9},{9,8},{10,11... | collective-permute-start | bytes 884744 | tf_op jit(solution)/shard_map/ppermute | solution.py:326
  130.5 3.6 %all-to-all-start.6 = ((bf16[16,64,256]{2,1,0:T(8,128)(2,1)}), bf16[16,64,256]{2,1,0:T(8,128)(2,1)S(1)}, u32[]{:S(2)}, u32[]{:S(2)}) async-start(bf16[16,64,256]{2,1,0:T(8,128)(2,1)} %get-tuple-element.44), calls=%async_computation.6 | async-start | bytes 1048576 | tf_op jit(solution)/shard_map/all_to_all | solution.py:325
  135.8 3.7 %collective-permute-done.23.refs_4_ = f32[72,256]{1,0:T(8,128)S(1)} collective-permute-done((f32[72,256]{1,0:T(8,128)S(1)}, f32[72,256]{1,0:T(8,128)S(1)}, u32[]{:S(2)}, u32[]{:S(2)}) %collective-permute-start.23) | collective-permute-done | bytes 73760 | tf_op jit(solution)/shard_map/ppermute | solution.py:328
  140.9 3.7 %all-to-all-done.6.refs_0_ = bf16[16,64,256]{2,1,0:T(8,128)(2,1)S(1)} async-done(((bf16[16,64,256]{2,1,0:T(8,128)(2,1)}), bf16[16,64,256]{2,1,0:T(8,128)(2,1)S(1)}, u32[]{:S(2)}, u32[]{:S(2)}) %all-to-all-start.6) | async-done | bytes 524320 | tf_op jit(solution)/shard_map/all_to_all | solution.py:325
  145.0 14.2 %all_to_all.53 = f32[128,1,128]{2,1,0:T(1,128)S(1)} all-to-all(f32[128,1,128]{2,1,0:T(1,128)S(1)} %bitcast.55), channel_id=1, replica_groups=mesh['row'=16,'col'=8] {'row','col'}, dimensions={0} | all-to-all | bytes 131072 | tf_op jit(solution)/shard_map/all_to_all | solution.py:348
  (57 shorter events, 29.3 us)
Async XLA Ops:
  2.2 2.2 %copy-start = (bf16[8,1,4,256,256]{4,3,2,1,0:T(8,128)(2,1)S(1)}, bf16[8,1,4,256,256]{4,3,2,1,0:T(8,128)(2,1)}, u32[]{:S(2)}) copy-start(bf16[8,1,4,256,256]{4,3,2,1,0:T(8,128)(2,1)} %param.4) | copy-start | bytes 12582916
  4.4 24.7 %copy-start.1 = (bf16[64,256]{1,0:T(8,128)(2,1)S(1)}, bf16[64,256]{1,0:T(8,128)(2,1)}, u32[]{:S(2)}) copy-start(bf16[64,256]{1,0:T(8,128)(2,1)} %refs_2_.1) | copy-start | bytes 98308
  30.2 15.1 %all-to-all-start.1 = ((bf16[16,80,256]{2,1,0:T(8,128)(2,1)}), bf16[16,80,256]{2,1,0:T(8,128)(2,1)S(1)}, u32[]{:S(2)}, u32[]{:S(2)}) async-start(bf16[16,80,256]{2,1,0:T(8,128)(2,1)} %get-tuple-element.29), calls=%async_computation.1 | async-start | bytes 1310720 | tf_op jit(solution)/shard_map/all_to_all | solution.py:310
  33.8 1.9 %collective-permute-start = (bf16[64,256]{1,0:T(8,128)(2,1)S(1)}, bf16[64,256]{1,0:T(8,128)(2,1)S(1)}, u32[]{:S(2)}, u32[]{:S(2)}) collective-permute-start(bf16[64,256]{1,0:T(8,128)(2,1)S(1)} %get-tuple-element.30.own), channel_id=1, source_target_pairs={{0,1},{1,0},{2,3},{3,2},{4,5},{5,4},{6,7},{7,6},{8,9},{9,8},{10,11... | collective-permute-start | bytes 98312 | tf_op jit(solution)/shard_map/ppermute | solution.py:307
  35.6 4.7 %collective-permute-start.3 = (bf16[2,64,256]{2,1,0:T(8,128)(2,1)S(1)}, bf16[2,64,256]{2,1,0:T(8,128)(2,1)S(1)}, u32[]{:S(2)}, u32[]{:S(2)}) collective-permute-start(bf16[2,64,256]{2,1,0:T(8,128)(2,1)S(1)} %pad_maximum_fusion), channel_id=1, source_target_pairs={{0,4},{1,5},{2,6},{3,7},{4,0},{5,1},{6,2},{7,3},{8,12},{9,13},{10,... | collective-permute-start | bytes 196616 | tf_op jit(solution)/shard_map/ppermute | solution.py:309
  36.5 3.8 %collective-permute-start.2 = (bf16[2,64,256]{2,1,0:T(8,128)(2,1)S(1)}, bf16[2,64,256]{2,1,0:T(8,128)(2,1)S(1)}, u32[]{:S(2)}, u32[]{:S(2)}) collective-permute-start(bf16[2,64,256]{2,1,0:T(8,128)(2,1)S(1)} %pad_maximum_fusion), channel_id=1, source_target_pairs={{0,6},{1,7},{2,0},{3,1},{4,2},{5,3},{6,4},{7,5},{8,14},{9,15},{10,... | collective-permute-start | bytes 196616 | tf_op jit(solution)/shard_map/ppermute | solution.py:309
  38.2 4.6 %collective-permute-start.1 = (bf16[2,64,256]{2,1,0:T(8,128)(2,1)S(1)}, bf16[2,64,256]{2,1,0:T(8,128)(2,1)S(1)}, u32[]{:S(2)}, u32[]{:S(2)}) collective-permute-start(bf16[2,64,256]{2,1,0:T(8,128)(2,1)S(1)} %pad_maximum_fusion), channel_id=1, source_target_pairs={{0,2},{1,3},{2,4},{3,5},{4,6},{5,7},{6,0},{7,1},{8,10},{9,11},{10,... | collective-permute-start | bytes 196616 | tf_op jit(solution)/shard_map/ppermute | solution.py:309
  50.4 6.2 %collective-permute-start.4 = (f32[4,72,256]{2,1,0:T(8,128)S(1)}, f32[4,72,256]{2,1,0:T(8,128)S(1)}, u32[]{:S(2)}, u32[]{:S(2)}) collective-permute-start(f32[4,72,256]{2,1,0:T(8,128)S(1)} %get-tuple-element.33), channel_id=1, source_target_pairs={{0,1},{1,0},{2,3},{3,2},{4,5},{5,4},{6,7},{7,6},{8,9},{9,8},{10,11... | collective-permute-start | bytes 884744 | tf_op jit(solution)/shard_map/ppermute | solution.py:326
  52.7 14.0 %all-to-all-start.2 = ((bf16[16,64,256]{2,1,0:T(8,128)(2,1)}), bf16[16,64,256]{2,1,0:T(8,128)(2,1)S(1)}, u32[]{:S(2)}, u32[]{:S(2)}) async-start(bf16[16,64,256]{2,1,0:T(8,128)(2,1)} %get-tuple-element.31), calls=%async_computation.2 | async-start | bytes 1048576 | tf_op jit(solution)/shard_map/all_to_all | solution.py:325
  56.7 5.1 %collective-permute-start.7 = (f32[72,256]{1,0:T(8,128)S(1)}, f32[72,256]{1,0:T(8,128)S(1)}, u32[]{:S(2)}, u32[]{:S(2)}) collective-permute-start(f32[72,256]{1,0:T(8,128)S(1)} %get-tuple-element.58), channel_id=1, source_target_pairs={{0,4},{1,5},{2,6},{3,7},{4,0},{5,1},{6,2},{7,3},{8,12},{9,13},{10,... | collective-permute-start | bytes 221192 | tf_op jit(solution)/shard_map/ppermute | solution.py:328
  57.8 4.2 %collective-permute-start.6 = (f32[72,256]{1,0:T(8,128)S(1)}, f32[72,256]{1,0:T(8,128)S(1)}, u32[]{:S(2)}, u32[]{:S(2)}) collective-permute-start(f32[72,256]{1,0:T(8,128)S(1)} %get-tuple-element.59), channel_id=1, source_target_pairs={{0,6},{1,7},{2,0},{3,1},{4,2},{5,3},{6,4},{7,5},{8,14},{9,15},{10,... | collective-permute-start | bytes 221192 | tf_op jit(solution)/shard_map/ppermute | solution.py:328
  59.4 4.7 %collective-permute-start.5 = (f32[72,256]{1,0:T(8,128)S(1)}, f32[72,256]{1,0:T(8,128)S(1)}, u32[]{:S(2)}, u32[]{:S(2)}) collective-permute-start(f32[72,256]{1,0:T(8,128)S(1)} %get-tuple-element.60), channel_id=1, source_target_pairs={{0,2},{1,3},{2,4},{3,5},{4,6},{5,7},{6,0},{7,1},{8,10},{9,11},{10,... | collective-permute-start | bytes 221192 | tf_op jit(solution)/shard_map/ppermute | solution.py:328
  67.9 15.6 %all-to-all-start.3 = ((bf16[16,80,256]{2,1,0:T(8,128)(2,1)}), bf16[16,80,256]{2,1,0:T(8,128)(2,1)S(1)}, u32[]{:S(2)}, u32[]{:S(2)}) async-start(bf16[16,80,256]{2,1,0:T(8,128)(2,1)} %get-tuple-element.35), calls=%async_computation.3 | async-start | bytes 1310720 | tf_op jit(solution)/shard_map/all_to_all | solution.py:310
  72.3 2.5 %collective-permute-start.8 = (bf16[64,256]{1,0:T(8,128)(2,1)S(1)}, bf16[64,256]{1,0:T(8,128)(2,1)S(1)}, u32[]{:S(2)}, u32[]{:S(2)}) collective-permute-start(bf16[64,256]{1,0:T(8,128)(2,1)S(1)} %get-tuple-element.36.own), channel_id=1, source_target_pairs={{0,1},{1,0},{2,3},{3,2},{4,5},{5,4},{6,7},{7,6},{8,9},{9,8},{10,11... | collective-permute-start | bytes 98312 | tf_op jit(solution)/shard_map/ppermute | solution.py:307
  74.8 4.7 %collective-permute-start.11 = (bf16[2,64,256]{2,1,0:T(8,128)(2,1)S(1)}, bf16[2,64,256]{2,1,0:T(8,128)(2,1)S(1)}, u32[]{:S(2)}, u32[]{:S(2)}) collective-permute-start(bf16[2,64,256]{2,1,0:T(8,128)(2,1)S(1)} %pad_maximum_fusion.1), channel_id=1, source_target_pairs={{0,4},{1,5},{2,6},{3,7},{4,0},{5,1},{6,2},{7,3},{8,12},{9,13},{10,... | collective-permute-start | bytes 196616 | tf_op jit(solution)/shard_map/ppermute | solution.py:309
  75.8 3.8 %collective-permute-start.10 = (bf16[2,64,256]{2,1,0:T(8,128)(2,1)S(1)}, bf16[2,64,256]{2,1,0:T(8,128)(2,1)S(1)}, u32[]{:S(2)}, u32[]{:S(2)}) collective-permute-start(bf16[2,64,256]{2,1,0:T(8,128)(2,1)S(1)} %pad_maximum_fusion.1), channel_id=1, source_target_pairs={{0,6},{1,7},{2,0},{3,1},{4,2},{5,3},{6,4},{7,5},{8,14},{9,15},{10,... | collective-permute-start | bytes 196616 | tf_op jit(solution)/shard_map/ppermute | solution.py:309
  77.4 4.6 %collective-permute-start.9 = (bf16[2,64,256]{2,1,0:T(8,128)(2,1)S(1)}, bf16[2,64,256]{2,1,0:T(8,128)(2,1)S(1)}, u32[]{:S(2)}, u32[]{:S(2)}) collective-permute-start(bf16[2,64,256]{2,1,0:T(8,128)(2,1)S(1)} %pad_maximum_fusion.1), channel_id=1, source_target_pairs={{0,2},{1,3},{2,4},{3,5},{4,6},{5,7},{6,0},{7,1},{8,10},{9,11},{10,... | collective-permute-start | bytes 196616 | tf_op jit(solution)/shard_map/ppermute | solution.py:309
  88.6 7.2 %collective-permute-start.12 = (f32[4,72,256]{2,1,0:T(8,128)S(1)}, f32[4,72,256]{2,1,0:T(8,128)S(1)}, u32[]{:S(2)}, u32[]{:S(2)}) collective-permute-start(f32[4,72,256]{2,1,0:T(8,128)S(1)} %get-tuple-element.39), channel_id=1, source_target_pairs={{0,1},{1,0},{2,3},{3,2},{4,5},{5,4},{6,7},{7,6},{8,9},{9,8},{10,11... | collective-permute-start | bytes 884744 | tf_op jit(solution)/shard_map/ppermute | solution.py:326
  91.3 14.6 %all-to-all-start.4 = ((bf16[16,64,256]{2,1,0:T(8,128)(2,1)}), bf16[16,64,256]{2,1,0:T(8,128)(2,1)S(1)}, u32[]{:S(2)}, u32[]{:S(2)}) async-start(bf16[16,64,256]{2,1,0:T(8,128)(2,1)} %get-tuple-element.37), calls=%async_computation.4 | async-start | bytes 1048576 | tf_op jit(solution)/shard_map/all_to_all | solution.py:325
  95.8 5.1 %collective-permute-start.15 = (f32[72,256]{1,0:T(8,128)S(1)}, f32[72,256]{1,0:T(8,128)S(1)}, u32[]{:S(2)}, u32[]{:S(2)}) collective-permute-start(f32[72,256]{1,0:T(8,128)S(1)} %get-tuple-element.54), channel_id=1, source_target_pairs={{0,4},{1,5},{2,6},{3,7},{4,0},{5,1},{6,2},{7,3},{8,12},{9,13},{10,... | collective-permute-start | bytes 221192 | tf_op jit(solution)/shard_map/ppermute | solution.py:328
  95.9 5.0 %collective-permute-start.14 = (f32[72,256]{1,0:T(8,128)S(1)}, f32[72,256]{1,0:T(8,128)S(1)}, u32[]{:S(2)}, u32[]{:S(2)}) collective-permute-start(f32[72,256]{1,0:T(8,128)S(1)} %get-tuple-element.55), channel_id=1, source_target_pairs={{0,6},{1,7},{2,0},{3,1},{4,2},{5,3},{6,4},{7,5},{8,14},{9,15},{10,... | collective-permute-start | bytes 221192 | tf_op jit(solution)/shard_map/ppermute | solution.py:328
  97.4 5.1 %collective-permute-start.13 = (f32[72,256]{1,0:T(8,128)S(1)}, f32[72,256]{1,0:T(8,128)S(1)}, u32[]{:S(2)}, u32[]{:S(2)}) collective-permute-start(f32[72,256]{1,0:T(8,128)S(1)} %get-tuple-element.56), channel_id=1, source_target_pairs={{0,2},{1,3},{2,4},{3,5},{4,6},{5,7},{6,0},{7,1},{8,10},{9,11},{10,... | collective-permute-start | bytes 221192 | tf_op jit(solution)/shard_map/ppermute | solution.py:328
  107.1 15.9 %all-to-all-start.5 = ((bf16[16,80,256]{2,1,0:T(8,128)(2,1)}), bf16[16,80,256]{2,1,0:T(8,128)(2,1)S(1)}, u32[]{:S(2)}, u32[]{:S(2)}) async-start(bf16[16,80,256]{2,1,0:T(8,128)(2,1)} %get-tuple-element.42), calls=%async_computation.5 | async-start | bytes 1310720 | tf_op jit(solution)/shard_map/all_to_all | solution.py:310
  111.5 2.5 %collective-permute-start.16 = (bf16[64,256]{1,0:T(8,128)(2,1)S(1)}, bf16[64,256]{1,0:T(8,128)(2,1)S(1)}, u32[]{:S(2)}, u32[]{:S(2)}) collective-permute-start(bf16[64,256]{1,0:T(8,128)(2,1)S(1)} %get-tuple-element.43.own), channel_id=1, source_target_pairs={{0,1},{1,0},{2,3},{3,2},{4,5},{5,4},{6,7},{7,6},{8,9},{9,8},{10,11... | collective-permute-start | bytes 98312 | tf_op jit(solution)/shard_map/ppermute | solution.py:307
  114.0 4.7 %collective-permute-start.19 = (bf16[2,64,256]{2,1,0:T(8,128)(2,1)S(1)}, bf16[2,64,256]{2,1,0:T(8,128)(2,1)S(1)}, u32[]{:S(2)}, u32[]{:S(2)}) collective-permute-start(bf16[2,64,256]{2,1,0:T(8,128)(2,1)S(1)} %pad_maximum_fusion.2), channel_id=1, source_target_pairs={{0,4},{1,5},{2,6},{3,7},{4,0},{5,1},{6,2},{7,3},{8,12},{9,13},{10,... | collective-permute-start | bytes 196616 | tf_op jit(solution)/shard_map/ppermute | solution.py:309
  114.1 4.6 %collective-permute-start.18 = (bf16[2,64,256]{2,1,0:T(8,128)(2,1)S(1)}, bf16[2,64,256]{2,1,0:T(8,128)(2,1)S(1)}, u32[]{:S(2)}, u32[]{:S(2)}) collective-permute-start(bf16[2,64,256]{2,1,0:T(8,128)(2,1)S(1)} %pad_maximum_fusion.2), channel_id=1, source_target_pairs={{0,6},{1,7},{2,0},{3,1},{4,2},{5,3},{6,4},{7,5},{8,14},{9,15},{10,... | collective-permute-start | bytes 196616 | tf_op jit(solution)/shard_map/ppermute | solution.py:309
  115.5 5.0 %collective-permute-start.17 = (bf16[2,64,256]{2,1,0:T(8,128)(2,1)S(1)}, bf16[2,64,256]{2,1,0:T(8,128)(2,1)S(1)}, u32[]{:S(2)}, u32[]{:S(2)}) collective-permute-start(bf16[2,64,256]{2,1,0:T(8,128)(2,1)S(1)} %pad_maximum_fusion.2), channel_id=1, source_target_pairs={{0,2},{1,3},{2,4},{3,5},{4,6},{5,7},{6,0},{7,1},{8,10},{9,11},{10,... | collective-permute-start | bytes 196616 | tf_op jit(solution)/shard_map/ppermute | solution.py:309
  128.1 6.0 %collective-permute-start.20 = (f32[4,72,256]{2,1,0:T(8,128)S(1)}, f32[4,72,256]{2,1,0:T(8,128)S(1)}, u32[]{:S(2)}, u32[]{:S(2)}) collective-permute-start(f32[4,72,256]{2,1,0:T(8,128)S(1)} %get-tuple-element.46), channel_id=1, source_target_pairs={{0,1},{1,0},{2,3},{3,2},{4,5},{5,4},{6,7},{7,6},{8,9},{9,8},{10,11... | collective-permute-start | bytes 884744 | tf_op jit(solution)/shard_map/ppermute | solution.py:326
  130.5 14.1 %all-to-all-start.6 = ((bf16[16,64,256]{2,1,0:T(8,128)(2,1)}), bf16[16,64,256]{2,1,0:T(8,128)(2,1)S(1)}, u32[]{:S(2)}, u32[]{:S(2)}) async-start(bf16[16,64,256]{2,1,0:T(8,128)(2,1)} %get-tuple-element.44), calls=%async_computation.6 | async-start | bytes 1048576 | tf_op jit(solution)/shard_map/all_to_all | solution.py:325
  134.2 5.3 %collective-permute-start.23 = (f32[72,256]{1,0:T(8,128)S(1)}, f32[72,256]{1,0:T(8,128)S(1)}, u32[]{:S(2)}, u32[]{:S(2)}) collective-permute-start(f32[72,256]{1,0:T(8,128)S(1)} %get-tuple-element.50), channel_id=1, source_target_pairs={{0,4},{1,5},{2,6},{3,7},{4,0},{5,1},{6,2},{7,3},{8,12},{9,13},{10,... | collective-permute-start | bytes 221192 | tf_op jit(solution)/shard_map/ppermute | solution.py:328
  134.3 5.2 %collective-permute-start.22 = (f32[72,256]{1,0:T(8,128)S(1)}, f32[72,256]{1,0:T(8,128)S(1)}, u32[]{:S(2)}, u32[]{:S(2)}) collective-permute-start(f32[72,256]{1,0:T(8,128)S(1)} %get-tuple-element.51), channel_id=1, source_target_pairs={{0,6},{1,7},{2,0},{3,1},{4,2},{5,3},{6,4},{7,5},{8,14},{9,15},{10,... | collective-permute-start | bytes 221192 | tf_op jit(solution)/shard_map/ppermute | solution.py:328
  135.8 5.1 %collective-permute-start.21 = (f32[72,256]{1,0:T(8,128)S(1)}, f32[72,256]{1,0:T(8,128)S(1)}, u32[]{:S(2)}, u32[]{:S(2)}) collective-permute-start(f32[72,256]{1,0:T(8,128)S(1)} %get-tuple-element.52), channel_id=1, source_target_pairs={{0,2},{1,3},{2,4},{3,5},{4,6},{5,7},{6,0},{7,1},{8,10},{9,11},{10,... | collective-permute-start | bytes 221192 | tf_op jit(solution)/shard_map/ppermute | solution.py:328

commit v4 on v3

--- a/solution.py
+++ b/solution.py
@@ -13,6 +13,7 @@
 BF16 = jnp.bfloat16
 VMEM = pl.BlockSpec(memory_space=pltpu.VMEM)
 SMEM = pl.BlockSpec(memory_space=pltpu.SMEM)
+HBM = pl.BlockSpec(memory_space=pltpu.HBM)
 EMPTY = 1024
 COLUMNS = 8
 SLOTS_OF = 64
@@ -20,7 +21,11 @@
 BACK = BF16
 CHUNK = 2
 KEPT = 3
-EXTRA = 16
+EXTRA = 8
+
+
+def in_hbm(x):
+    return pltpu.with_memory_space_constraint(x, pltpu.HBM)
 
 
 def nn(a, b):
@@ -59,12 +64,25 @@
 
 
 def degree_kernel(
-    place, columns, counts, tiles, message, meta, near, row_sums, col_sums, used, done
+    place, stored_columns, stored_counts, stored, message, meta, near,
+    far, columns, counts, row_sums, col_sums, used, few, arrived,
 ):
-    panels, slots, tile = tiles.shape[0], tiles.shape[1], tiles.shape[2]
+    panels, slots, tile = stored.shape[0], stored.shape[1], stored.shape[2]
     row_devices = message.shape[0]
-    keeping = pltpu.make_async_copy(tiles.at[: near.shape[0]], near, done)
-    keeping.start()
+    split = near.shape[0]
+    small = [
+        pltpu.make_async_copy(stored_columns, columns, few.at[0]),
+        pltpu.make_async_copy(stored_counts, counts, few.at[1]),
+    ]
+    for copy in small:
+        copy.start()
+    fetch = []
+    for i in range(panels):
+        held = near.at[i] if i < split else far.at[i - split]
+        fetch.append(pltpu.make_async_copy(stored.at[i], held, arrived.at[i]))
+        fetch[i].start()
+    for copy in small:
+        copy.wait()
     mine_row, mine_col = place[0], place[1]
     meta[0] = mine_row
     meta[1] = mine_col
@@ -73,19 +91,22 @@
     for i in range(panels):
         for s in range(slots):
             q = i * slots + s
-            b = columns[i, 0, s]
-            dead = jnp.where(s < counts[i, 0], 0, EMPTY)
+            b = columns[s, i]
+            dead = jnp.where(s < counts[0, i], 0, EMPTY)
             meta[COLUMNS + q] = b + dead
             meta[SLOTS_OF + 2 * b + used[b]] = q + dead
             used[b] = used[b] + 1
 
     ones = jnp.ones((16, tile), BF16)
     for i in range(panels):
+        if i % 2 == 0:
+            fetch[i].wait()
+            fetch[i + 1].wait()
         total = jnp.zeros((16, tile), F32)
         for s in range(slots):
-            live = s < counts[i, 0]
+            live = s < counts[0, i]
             weight = jnp.where(live, ones, jnp.zeros_like(ones))
-            value = tiles[i, s]
+            value = near[i, s] if i < split else far[i - split, s]
             total = total + nt(weight, value)
             wide = jnp.sum(value.astype(F32).reshape(tile // 8, 8, tile), axis=0)
             col_sums[i * slots + s] = jnp.where(live, wide, jnp.zeros_like(wide))
@@ -101,7 +122,6 @@
         part = jnp.where(at == mine_col, part, 0.0) + jnp.where(b == mine_row, rows, 0.0)
         message[b, :, :tile] = part
         message[b, :, tile:] = jnp.broadcast_to(everything, (part.shape[0], 128))
-    keeping.wait()
 
 
 def pack(values, dots, many, one):
@@ -109,8 +129,7 @@
     body = values.astype(BF16)
     high = dots.astype(BF16)
     low = (dots - high.astype(F32)).astype(BF16)
-    tail = jnp.concatenate([high, low], axis=0)
-    tail = jnp.concatenate([tail, jnp.zeros_like(tail)], axis=1)
+    tail = jnp.concatenate([high, low], axis=1)
     one[...] = body
     for b in range(many.shape[0]):
         many[b, :cells] = body
@@ -152,8 +171,8 @@
     z, core = meta[1] // 2, meta[1] % 2
     dots = jnp.zeros((8, 128), F32)
     for b in range(gathered.shape[0]):
-        tail = gathered[b, cells:, :128].astype(F32)
-        dots = dots + tail[:8] + tail[8:]
+        tail = gathered[b, cells:].astype(F32)
+        dots = dots + tail[:, :128] + tail[:, 128:]
     dots = jnp.concatenate([dots, jnp.zeros_like(dots)], axis=1)
     for k, source in ((0, None), (1, far1), (2, far2), (3, far3)):
         at = (z + zs - k) % zs
@@ -263,7 +282,7 @@
     zs = cols // 2
     total_cells = rows * cols * tile
     tiles = tile_values.reshape(panels, slots, tile, tile)
-    stored = pltpu.with_memory_space_constraint(tiles, pltpu.HBM)
+    stored = in_hbm(tiles)
     place = jnp.stack([lax.axis_index("row"), lax.axis_index("col")]).astype(jnp.int32)
     shape = jax.ShapeDtypeStruct
     swap = [(i, i ^ 1) for i in range(cols)]
@@ -278,17 +297,21 @@
             shape((META,), jnp.int32),
             shape((KEPT, slots, tile, tile), BF16),
         ),
-        [SMEM, SMEM, SMEM, VMEM],
+        [SMEM, HBM, HBM, HBM],
         (VMEM, SMEM, VMEM),
         [
+            pltpu.VMEM((panels - KEPT, slots, tile, tile), BF16),
+            pltpu.SMEM((slots, panels), jnp.int32),
+            pltpu.SMEM((1, panels), jnp.int32),
             pltpu.VMEM((panels, tile), F32),
             pltpu.VMEM((panels * slots, 8, tile), F32),
             pltpu.SMEM((rows,), jnp.int32),
-            pltpu.SemaphoreType.DMA,
+            pltpu.SemaphoreType.DMA((2,)),
+            pltpu.SemaphoreType.DMA((panels,)),
         ],
         work / 4,
         tile_bytes,
-    )(place, tile_cols, row_counts, tiles)
+    )(place, in_hbm(tile_cols[:, 0].T), in_hbm(row_counts.T), stored)
     parts = lax.all_to_all(
         message.reshape(rows * cols, tile + 128), ("row", "col"), 0, 0, tiled=True
     )
@@ -312,7 +335,7 @@
         back, keep, give = call(
             product_kernel,
             (shape((rows, cells, tile), BACK), side_shape, side_shape),
-            [SMEM, VMEM, pl.BlockSpec(memory_space=pltpu.HBM)] + [VMEM] * 6,
+            [SMEM, VMEM, HBM] + [VMEM] * 6,
             scratch=[
                 pltpu.VMEM((panels, cells, tile), BF16),
                 pltpu.VMEM((panels * slots, cells, tile), F32),

time: 161 us -> 158 us (0.981)
  local copies, waits for them, and re-layouts: 3.96 us -> 0.29 us
  waiting for transfers between devices: 47.8 us -> 45.6 us
    unnamed x7 -> x3, local copies, waits for them, and re-layouts: 3.69 us -> 0.02 us
    all_to_all x3, waiting for transfers between devices: 6.46 us -> 4.46 us  [local(): gathered = lax.all_to_all(many, 'row', 0, 0, tiled=True)]
  transfers between devices with their start and end apart: 30 -> 30, of which waited for: 23 -> 22; matrix products, arithmetic and copies ran while one was open for 0% -> 0% of each run, Pallas kernels for 0% -> 0%
where the time goes in v4:
time: 158 us; the launch traced here: 157 us
  starting transfers between devices  49.1 us (31%)
  waiting for transfers between devices  45.6 us (29%)
  blocking collectives  36.8 us (23%)
  Pallas kernels  23.8 us (15%)
    all_to_all x1, blocking collectives, local(): lax.all_to_all(message.reshape(rows * cols, tile + 128), ('row', 'col'),...  21.7 us
    pallas_call x3, Pallas kernels, local(): call(product_kernel, (shape((rows, cells, tile), BACK), side_shape, side_...  15.2 us
    all_to_all x1, blocking collectives, local(): norms = lax.all_to_all(norms, ('row', 'col'), 0, 0, tiled=True)  15.1 us
    ppermute x9, waiting for transfers between devices, local(): lax.ppermute(sums[k], 'col', shift(k))  14.6 us
    ppermute x9, waiting for transfers between devices, local(): near = [lax.ppermute(both, 'col', shift(k)) for k in (1, 3, 2)]  14.2 us
    all_to_all x3, starting transfers between devices, local(): back = lax.all_to_all(back, 'row', 0, 0, tiled=True)  12.8 us
    all_to_all x3, starting transfers between devices, local(): gathered = lax.all_to_all(many, 'row', 0, 0, tiled=True)  12.3 us
    all_to_all x3, waiting for transfers between devices, local(): back = lax.all_to_all(back, 'row', 0, 0, tiled=True)  9.8 us
  transfers between devices with their start and end apart: 30, of which 22 were waited for; matrix products, arithmetic and copies ran while one was open for 0% of the time, Pallas kernels for 0%

profile of v4, /device:TPU:1, one launch (start us, length us, event | category | flops | bytes accessed | tf_op | source)
XLA Modules:
  0.0 156.7 jit_solution(11938663881411288416)
XLA Ops:
  0.7 4.0 %shard_map.59 = (f32[16,8,384]{2,1,0:T(8,128)S(1)}, s32[128]{0:T(128)S(1)}, bf16[3,4,256,256]{3,2,1,0:T(8,128)(2,1)S(1)}) custom-call(s32[2]{0:T(128)S(1)} %pad_add_fusion.place, s32[4,8]{1,0:T(4,128)} %bitcast.60, s32[1,8]{1,0:T(1,128)} %bitcast.61, bf16[8,4,256,256]{3,2,1,0:T(8,128)(2,1)} %bitcast.56), custom_call_target="tpu_custom_call" | custom-call | flops 67108864 | bytes 4194304 | tf_op jit(solution)/shard_map/pallas_call | solution.py:293
  4.9 21.7 %all_to_all.52 = f32[128,1,384]{2,1,0:T(1,128)S(1)} all-to-all(f32[128,1,384]{2,1,0:T(1,128)S(1)} %copy.6), channel_id=1, replica_groups=mesh['row'=16,'col'=8] {'row','col'}, dimensions={0} | all-to-all | bytes 393216 | tf_op jit(solution)/shard_map/all_to_all | solution.py:315
  27.7 3.6 %all-to-all-start.1 = ((bf16[16,72,256]{2,1,0:T(8,128)(2,1)}), bf16[16,72,256]{2,1,0:T(8,128)(2,1)S(1)}, u32[]{:S(2)}, u32[]{:S(2)}) async-start(bf16[16,72,256]{2,1,0:T(8,128)(2,1)} %get-tuple-element.29), calls=%async_computation.1 | async-start | bytes 1179648 | tf_op jit(solution)/shard_map/all_to_all | solution.py:333
  34.0 1.8 %collective-permute-start.2 = (bf16[2,64,256]{2,1,0:T(8,128)(2,1)S(1)}, bf16[2,64,256]{2,1,0:T(8,128)(2,1)S(1)}, u32[]{:S(2)}, u32[]{:S(2)}) collective-permute-start(bf16[2,64,256]{2,1,0:T(8,128)(2,1)S(1)} %pad_maximum_fusion), channel_id=1, source_target_pairs={{0,6},{1,7},{2,0},{3,1},{4,2},{5,3},{6,4},{7,5},{8,14},{9,15},{10,... | collective-permute-start | bytes 196616 | tf_op jit(solution)/shard_map/ppermute | solution.py:332
  35.7 2.1 %collective-permute-done.3.far2 = bf16[2,64,256]{2,1,0:T(8,128)(2,1)S(1)} collective-permute-done((bf16[2,64,256]{2,1,0:T(8,128)(2,1)S(1)}, bf16[2,64,256]{2,1,0:T(8,128)(2,1)S(1)}, u32[]{:S(2)}, u32[]{:S(2)}) %collective-permute-start.3) | collective-permute-done | bytes 65568 | tf_op jit(solution)/shard_map/ppermute | solution.py:332
  37.8 2.5 %collective-permute-done.1.far1 = bf16[2,64,256]{2,1,0:T(8,128)(2,1)S(1)} collective-permute-done((bf16[2,64,256]{2,1,0:T(8,128)(2,1)S(1)}, bf16[2,64,256]{2,1,0:T(8,128)(2,1)S(1)}, u32[]{:S(2)}, u32[]{:S(2)}) %collective-permute-start.1) | collective-permute-done | bytes 65568 | tf_op jit(solution)/shard_map/ppermute | solution.py:332
  40.4 1.9 %all-to-all-done.1.gathered = bf16[16,72,256]{2,1,0:T(8,128)(2,1)S(1)} async-done(((bf16[16,72,256]{2,1,0:T(8,128)(2,1)}), bf16[16,72,256]{2,1,0:T(8,128)(2,1)S(1)}, u32[]{:S(2)}, u32[]{:S(2)}) %all-to-all-start.1) | async-done | bytes 589856 | tf_op jit(solution)/shard_map/all_to_all | solution.py:333
  42.2 5.1 %shard_map.61 = (bf16[16,64,256]{2,1,0:T(8,128)(2,1)}, f32[4,72,256]{2,1,0:T(8,128)S(1)}, f32[4,72,256]{2,1,0:T(8,128)S(1)}) custom-call(s32[128]{0:T(128)S(1)} %get-tuple-element.26.meta, bf16[3,4,256,256]{3,2,1,0:T(8,128)(2,1)S(1)} %get-tuple-element.27.near_tiles, bf16[8,4,256,256]{3,2,1,0:T(8,128)(2,1)} %bitcast.57, ...), custom_call_target="tpu_custom_call" | custom-call | flops 536870912 | bytes 4194304 | tf_op jit(solution)/shard_map/pallas_call | solution.py:335
  47.3 2.2 %collective-permute-start.4 = (f32[4,72,256]{2,1,0:T(8,128)S(1)}, f32[4,72,256]{2,1,0:T(8,128)S(1)}, u32[]{:S(2)}, u32[]{:S(2)}) collective-permute-start(f32[4,72,256]{2,1,0:T(8,128)S(1)} %get-tuple-element.33), channel_id=1, source_target_pairs={{0,1},{1,0},{2,3},{3,2},{4,5},{5,4},{6,7},{7,6},{8,9},{9,8},{10,11... | collective-permute-start | bytes 884744 | tf_op jit(solution)/shard_map/ppermute | solution.py:349
  49.5 4.6 %all-to-all-start.2 = ((bf16[16,64,256]{2,1,0:T(8,128)(2,1)}), bf16[16,64,256]{2,1,0:T(8,128)(2,1)S(1)}, u32[]{:S(2)}, u32[]{:S(2)}) async-start(bf16[16,64,256]{2,1,0:T(8,128)(2,1)} %get-tuple-element.31), calls=%async_computation.2 | async-start | bytes 1048576 | tf_op jit(solution)/shard_map/all_to_all | solution.py:348
  56.2 3.2 %collective-permute-done.7.far2 = f32[72,256]{1,0:T(8,128)S(1)} collective-permute-done((f32[72,256]{1,0:T(8,128)S(1)}, f32[72,256]{1,0:T(8,128)S(1)}, u32[]{:S(2)}, u32[]{:S(2)}) %collective-permute-start.7) | collective-permute-done | bytes 73760 | tf_op jit(solution)/shard_map/ppermute | solution.py:351
  61.0 3.3 %all-to-all-done.2.tile_sums = bf16[16,64,256]{2,1,0:T(8,128)(2,1)S(1)} async-done(((bf16[16,64,256]{2,1,0:T(8,128)(2,1)}), bf16[16,64,256]{2,1,0:T(8,128)(2,1)S(1)}, u32[]{:S(2)}, u32[]{:S(2)}) %all-to-all-start.2) | async-done | bytes 524320 | tf_op jit(solution)/shard_map/all_to_all | solution.py:348
  65.4 4.3 %all-to-all-start.3 = ((bf16[16,72,256]{2,1,0:T(8,128)(2,1)}), bf16[16,72,256]{2,1,0:T(8,128)(2,1)S(1)}, u32[]{:S(2)}, u32[]{:S(2)}) async-start(bf16[16,72,256]{2,1,0:T(8,128)(2,1)} %get-tuple-element.35), calls=%async_computation.3 | async-start | bytes 1179648 | tf_op jit(solution)/shard_map/all_to_all | solution.py:333
  69.7 1.6 %collective-permute-start.8 = (bf16[64,256]{1,0:T(8,128)(2,1)S(1)}, bf16[64,256]{1,0:T(8,128)(2,1)S(1)}, u32[]{:S(2)}, u32[]{:S(2)}) collective-permute-start(bf16[64,256]{1,0:T(8,128)(2,1)S(1)} %get-tuple-element.36.own), channel_id=1, source_target_pairs={{0,1},{1,0},{2,3},{3,2},{4,5},{5,4},{6,7},{7,6},{8,9},{9,8},{10,11... | collective-permute-start | bytes 98312 | tf_op jit(solution)/shard_map/ppermute | solution.py:330
  74.1 2.8 %collective-permute-done.11.far2 = bf16[2,64,256]{2,1,0:T(8,128)(2,1)S(1)} collective-permute-done((bf16[2,64,256]{2,1,0:T(8,128)(2,1)S(1)}, bf16[2,64,256]{2,1,0:T(8,128)(2,1)S(1)}, u32[]{:S(2)}, u32[]{:S(2)}) %collective-permute-start.11) | collective-permute-done | bytes 65568 | tf_op jit(solution)/shard_map/ppermute | solution.py:332
  76.9 1.9 %collective-permute-done.9.far1 = bf16[2,64,256]{2,1,0:T(8,128)(2,1)S(1)} collective-permute-done((bf16[2,64,256]{2,1,0:T(8,128)(2,1)S(1)}, bf16[2,64,256]{2,1,0:T(8,128)(2,1)S(1)}, u32[]{:S(2)}, u32[]{:S(2)}) %collective-permute-start.9) | collective-permute-done | bytes 65568 | tf_op jit(solution)/shard_map/ppermute | solution.py:332
  80.1 5.1 %shard_map.63 = (bf16[16,64,256]{2,1,0:T(8,128)(2,1)}, f32[4,72,256]{2,1,0:T(8,128)S(1)}, f32[4,72,256]{2,1,0:T(8,128)S(1)}) custom-call(s32[128]{0:T(128)S(1)} %get-tuple-element.26.meta, bf16[3,4,256,256]{3,2,1,0:T(8,128)(2,1)S(1)} %get-tuple-element.27.near_tiles, bf16[8,4,256,256]{3,2,1,0:T(8,128)(2,1)} %bitcast.58, ...), custom_call_target="tpu_custom_call" | custom-call | flops 536870912 | bytes 4194304 | tf_op jit(solution)/shard_map/pallas_call | solution.py:335
  85.1 2.9 %collective-permute-start.12 = (f32[4,72,256]{2,1,0:T(8,128)S(1)}, f32[4,72,256]{2,1,0:T(8,128)S(1)}, u32[]{:S(2)}, u32[]{:S(2)}) collective-permute-start(f32[4,72,256]{2,1,0:T(8,128)S(1)} %get-tuple-element.39), channel_id=1, source_target_pairs={{0,1},{1,0},{2,3},{3,2},{4,5},{5,4},{6,7},{7,6},{8,9},{9,8},{10,11... | collective-permute-start | bytes 884744 | tf_op jit(solution)/shard_map/ppermute | solution.py:349
  88.0 4.5 %all-to-all-start.4 = ((bf16[16,64,256]{2,1,0:T(8,128)(2,1)}), bf16[16,64,256]{2,1,0:T(8,128)(2,1)S(1)}, u32[]{:S(2)}, u32[]{:S(2)}) async-start(bf16[16,64,256]{2,1,0:T(8,128)(2,1)} %get-tuple-element.37), calls=%async_computation.4 | async-start | bytes 1048576 | tf_op jit(solution)/shard_map/all_to_all | solution.py:348
  94.4 3.3 %collective-permute-done.15.refs_4_ = f32[72,256]{1,0:T(8,128)S(1)} collective-permute-done((f32[72,256]{1,0:T(8,128)S(1)}, f32[72,256]{1,0:T(8,128)S(1)}, u32[]{:S(2)}, u32[]{:S(2)}) %collective-permute-start.15) | collective-permute-done | bytes 73760 | tf_op jit(solution)/shard_map/ppermute | solution.py:351
  97.7 1.8 %collective-permute-done.13.refs_2_ = f32[72,256]{1,0:T(8,128)S(1)} collective-permute-done((f32[72,256]{1,0:T(8,128)S(1)}, f32[72,256]{1,0:T(8,128)S(1)}, u32[]{:S(2)}, u32[]{:S(2)}) %collective-permute-start.13) | collective-permute-done | bytes 73760 | tf_op jit(solution)/shard_map/ppermute | solution.py:351
  99.5 3.1 %all-to-all-done.4.refs_0_ = bf16[16,64,256]{2,1,0:T(8,128)(2,1)S(1)} async-done(((bf16[16,64,256]{2,1,0:T(8,128)(2,1)}), bf16[16,64,256]{2,1,0:T(8,128)(2,1)S(1)}, u32[]{:S(2)}, u32[]{:S(2)}) %all-to-all-start.4) | async-done | bytes 524320 | tf_op jit(solution)/shard_map/all_to_all | solution.py:348
  103.9 4.3 %all-to-all-start.5 = ((bf16[16,72,256]{2,1,0:T(8,128)(2,1)}), bf16[16,72,256]{2,1,0:T(8,128)(2,1)S(1)}, u32[]{:S(2)}, u32[]{:S(2)}) async-start(bf16[16,72,256]{2,1,0:T(8,128)(2,1)} %get-tuple-element.42), calls=%async_computation.5 | async-start | bytes 1179648 | tf_op jit(solution)/shard_map/all_to_all | solution.py:333
  108.2 1.6 %collective-permute-start.16 = (bf16[64,256]{1,0:T(8,128)(2,1)S(1)}, bf16[64,256]{1,0:T(8,128)(2,1)S(1)}, u32[]{:S(2)}, u32[]{:S(2)}) collective-permute-start(bf16[64,256]{1,0:T(8,128)(2,1)S(1)} %get-tuple-element.43.own), channel_id=1, source_target_pairs={{0,1},{1,0},{2,3},{3,2},{4,5},{5,4},{6,7},{7,6},{8,9},{9,8},{10,11... | collective-permute-start | bytes 98312 | tf_op jit(solution)/shard_map/ppermute | solution.py:330
  112.3 3.1 %collective-permute-done.19.far2 = bf16[2,64,256]{2,1,0:T(8,128)(2,1)S(1)} collective-permute-done((bf16[2,64,256]{2,1,0:T(8,128)(2,1)S(1)}, bf16[2,64,256]{2,1,0:T(8,128)(2,1)S(1)}, u32[]{:S(2)}, u32[]{:S(2)}) %collective-permute-start.19) | collective-permute-done | bytes 65568 | tf_op jit(solution)/shard_map/ppermute | solution.py:332
  115.4 1.8 %collective-permute-done.17.far1 = bf16[2,64,256]{2,1,0:T(8,128)(2,1)S(1)} collective-permute-done((bf16[2,64,256]{2,1,0:T(8,128)(2,1)S(1)}, bf16[2,64,256]{2,1,0:T(8,128)(2,1)S(1)}, u32[]{:S(2)}, u32[]{:S(2)}) %collective-permute-start.17) | collective-permute-done | bytes 65568 | tf_op jit(solution)/shard_map/ppermute | solution.py:332
  118.5 5.1 %shard_map.65 = (bf16[16,64,256]{2,1,0:T(8,128)(2,1)}, f32[4,72,256]{2,1,0:T(8,128)S(1)}, f32[4,72,256]{2,1,0:T(8,128)S(1)}) custom-call(s32[128]{0:T(128)S(1)} %get-tuple-element.26.meta, bf16[3,4,256,256]{3,2,1,0:T(8,128)(2,1)S(1)} %get-tuple-element.27.near_tiles, bf16[8,4,256,256]{3,2,1,0:T(8,128)(2,1)} %bitcast.59, ...), custom_call_target="tpu_custom_call" | custom-call | flops 536870912 | bytes 4194304 | tf_op jit(solution)/shard_map/pallas_call | solution.py:335
  123.6 2.9 %collective-permute-start.20 = (f32[4,72,256]{2,1,0:T(8,128)S(1)}, f32[4,72,256]{2,1,0:T(8,128)S(1)}, u32[]{:S(2)}, u32[]{:S(2)}) collective-permute-start(f32[4,72,256]{2,1,0:T(8,128)S(1)} %get-tuple-element.46), channel_id=1, source_target_pairs={{0,1},{1,0},{2,3},{3,2},{4,5},{5,4},{6,7},{7,6},{8,9},{9,8},{10,11... | collective-permute-start | bytes 884744 | tf_op jit(solution)/shard_map/ppermute | solution.py:349
  126.5 3.7 %all-to-all-start.6 = ((bf16[16,64,256]{2,1,0:T(8,128)(2,1)}), bf16[16,64,256]{2,1,0:T(8,128)(2,1)S(1)}, u32[]{:S(2)}, u32[]{:S(2)}) async-start(bf16[16,64,256]{2,1,0:T(8,128)(2,1)} %get-tuple-element.44), calls=%async_computation.6 | async-start | bytes 1048576 | tf_op jit(solution)/shard_map/all_to_all | solution.py:348
  132.3 3.2 %collective-permute-done.23.refs_4_ = f32[72,256]{1,0:T(8,128)S(1)} collective-permute-done((f32[72,256]{1,0:T(8,128)S(1)}, f32[72,256]{1,0:T(8,128)S(1)}, u32[]{:S(2)}, u32[]{:S(2)}) %collective-permute-start.23) | collective-permute-done | bytes 73760 | tf_op jit(solution)/shard_map/ppermute | solution.py:351
  137.0 3.4 %all-to-all-done.6.refs_0_ = bf16[16,64,256]{2,1,0:T(8,128)(2,1)S(1)} async-done(((bf16[16,64,256]{2,1,0:T(8,128)(2,1)}), bf16[16,64,256]{2,1,0:T(8,128)(2,1)S(1)}, u32[]{:S(2)}, u32[]{:S(2)}) %all-to-all-start.6) | async-done | bytes 524320 | tf_op jit(solution)/shard_map/all_to_all | solution.py:348
  140.8 15.1 %all_to_all.53 = f32[128,1,128]{2,1,0:T(1,128)S(1)} all-to-all(f32[128,1,128]{2,1,0:T(1,128)S(1)} %bitcast.55), channel_id=1, replica_groups=mesh['row'=16,'col'=8] {'row','col'}, dimensions={0} | all-to-all | bytes 131072 | tf_op jit(solution)/shard_map/all_to_all | solution.py:371
  (53 shorter events, 24.5 us)
Async XLA Ops:
  0.6 26.0 %copy-start = (bf16[64,256]{1,0:T(8,128)(2,1)S(1)}, bf16[64,256]{1,0:T(8,128)(2,1)}, u32[]{:S(2)}) copy-start(bf16[64,256]{1,0:T(8,128)(2,1)} %refs_2_.1) | copy-start | bytes 98308
  27.7 14.5 %all-to-all-start.1 = ((bf16[16,72,256]{2,1,0:T(8,128)(2,1)}), bf16[16,72,256]{2,1,0:T(8,128)(2,1)S(1)}, u32[]{:S(2)}, u32[]{:S(2)}) async-start(bf16[16,72,256]{2,1,0:T(8,128)(2,1)} %get-tuple-element.29), calls=%async_computation.1 | async-start | bytes 1179648 | tf_op jit(solution)/shard_map/all_to_all | solution.py:333
  31.3 1.9 %collective-permute-start = (bf16[64,256]{1,0:T(8,128)(2,1)S(1)}, bf16[64,256]{1,0:T(8,128)(2,1)S(1)}, u32[]{:S(2)}, u32[]{:S(2)}) collective-permute-start(bf16[64,256]{1,0:T(8,128)(2,1)S(1)} %get-tuple-element.30.own), channel_id=1, source_target_pairs={{0,1},{1,0},{2,3},{3,2},{4,5},{5,4},{6,7},{7,6},{8,9},{9,8},{10,11... | collective-permute-start | bytes 98312 | tf_op jit(solution)/shard_map/ppermute | solution.py:330
  33.2 4.7 %collective-permute-start.3 = (bf16[2,64,256]{2,1,0:T(8,128)(2,1)S(1)}, bf16[2,64,256]{2,1,0:T(8,128)(2,1)S(1)}, u32[]{:S(2)}, u32[]{:S(2)}) collective-permute-start(bf16[2,64,256]{2,1,0:T(8,128)(2,1)S(1)} %pad_maximum_fusion), channel_id=1, source_target_pairs={{0,4},{1,5},{2,6},{3,7},{4,0},{5,1},{6,2},{7,3},{8,12},{9,13},{10,... | collective-permute-start | bytes 196616 | tf_op jit(solution)/shard_map/ppermute | solution.py:332
  34.0 3.8 %collective-permute-start.2 = (bf16[2,64,256]{2,1,0:T(8,128)(2,1)S(1)}, bf16[2,64,256]{2,1,0:T(8,128)(2,1)S(1)}, u32[]{:S(2)}, u32[]{:S(2)}) collective-permute-start(bf16[2,64,256]{2,1,0:T(8,128)(2,1)S(1)} %pad_maximum_fusion), channel_id=1, source_target_pairs={{0,6},{1,7},{2,0},{3,1},{4,2},{5,3},{6,4},{7,5},{8,14},{9,15},{10,... | collective-permute-start | bytes 196616 | tf_op jit(solution)/shard_map/ppermute | solution.py:332
  35.7 4.6 %collective-permute-start.1 = (bf16[2,64,256]{2,1,0:T(8,128)(2,1)S(1)}, bf16[2,64,256]{2,1,0:T(8,128)(2,1)S(1)}, u32[]{:S(2)}, u32[]{:S(2)}) collective-permute-start(bf16[2,64,256]{2,1,0:T(8,128)(2,1)S(1)} %pad_maximum_fusion), channel_id=1, source_target_pairs={{0,2},{1,3},{2,4},{3,5},{4,6},{5,7},{6,0},{7,1},{8,10},{9,11},{10,... | collective-permute-start | bytes 196616 | tf_op jit(solution)/shard_map/ppermute | solution.py:332
  47.3 6.8 %collective-permute-start.4 = (f32[4,72,256]{2,1,0:T(8,128)S(1)}, f32[4,72,256]{2,1,0:T(8,128)S(1)}, u32[]{:S(2)}, u32[]{:S(2)}) collective-permute-start(f32[4,72,256]{2,1,0:T(8,128)S(1)} %get-tuple-element.33), channel_id=1, source_target_pairs={{0,1},{1,0},{2,3},{3,2},{4,5},{5,4},{6,7},{7,6},{8,9},{9,8},{10,11... | collective-permute-start | bytes 884744 | tf_op jit(solution)/shard_map/ppermute | solution.py:349
  49.5 14.7 %all-to-all-start.2 = ((bf16[16,64,256]{2,1,0:T(8,128)(2,1)}), bf16[16,64,256]{2,1,0:T(8,128)(2,1)S(1)}, u32[]{:S(2)}, u32[]{:S(2)}) async-start(bf16[16,64,256]{2,1,0:T(8,128)(2,1)} %get-tuple-element.31), calls=%async_computation.2 | async-start | bytes 1048576 | tf_op jit(solution)/shard_map/all_to_all | solution.py:348
  54.2 5.1 %collective-permute-start.7 = (f32[72,256]{1,0:T(8,128)S(1)}, f32[72,256]{1,0:T(8,128)S(1)}, u32[]{:S(2)}, u32[]{:S(2)}) collective-permute-start(f32[72,256]{1,0:T(8,128)S(1)} %get-tuple-element.58), channel_id=1, source_target_pairs={{0,4},{1,5},{2,6},{3,7},{4,0},{5,1},{6,2},{7,3},{8,12},{9,13},{10,... | collective-permute-start | bytes 221192 | tf_op jit(solution)/shard_map/ppermute | solution.py:351
  54.6 4.8 %collective-permute-start.6 = (f32[72,256]{1,0:T(8,128)S(1)}, f32[72,256]{1,0:T(8,128)S(1)}, u32[]{:S(2)}, u32[]{:S(2)}) collective-permute-start(f32[72,256]{1,0:T(8,128)S(1)} %get-tuple-element.59), channel_id=1, source_target_pairs={{0,6},{1,7},{2,0},{3,1},{4,2},{5,3},{6,4},{7,5},{8,14},{9,15},{10,... | collective-permute-start | bytes 221192 | tf_op jit(solution)/shard_map/ppermute | solution.py:351
  56.2 4.8 %collective-permute-start.5 = (f32[72,256]{1,0:T(8,128)S(1)}, f32[72,256]{1,0:T(8,128)S(1)}, u32[]{:S(2)}, u32[]{:S(2)}) collective-permute-start(f32[72,256]{1,0:T(8,128)S(1)} %get-tuple-element.60), channel_id=1, source_target_pairs={{0,2},{1,3},{2,4},{3,5},{4,6},{5,7},{6,0},{7,1},{8,10},{9,11},{10,... | collective-permute-start | bytes 221192 | tf_op jit(solution)/shard_map/ppermute | solution.py:351
  65.4 14.7 %all-to-all-start.3 = ((bf16[16,72,256]{2,1,0:T(8,128)(2,1)}), bf16[16,72,256]{2,1,0:T(8,128)(2,1)S(1)}, u32[]{:S(2)}, u32[]{:S(2)}) async-start(bf16[16,72,256]{2,1,0:T(8,128)(2,1)} %get-tuple-element.35), calls=%async_computation.3 | async-start | bytes 1179648 | tf_op jit(solution)/shard_map/all_to_all | solution.py:333
  69.7 2.5 %collective-permute-start.8 = (bf16[64,256]{1,0:T(8,128)(2,1)S(1)}, bf16[64,256]{1,0:T(8,128)(2,1)S(1)}, u32[]{:S(2)}, u32[]{:S(2)}) collective-permute-start(bf16[64,256]{1,0:T(8,128)(2,1)S(1)} %get-tuple-element.36.own), channel_id=1, source_target_pairs={{0,1},{1,0},{2,3},{3,2},{4,5},{5,4},{6,7},{7,6},{8,9},{9,8},{10,11... | collective-permute-start | bytes 98312 | tf_op jit(solution)/shard_map/ppermute | solution.py:330
  72.2 4.7 %collective-permute-start.11 = (bf16[2,64,256]{2,1,0:T(8,128)(2,1)S(1)}, bf16[2,64,256]{2,1,0:T(8,128)(2,1)S(1)}, u32[]{:S(2)}, u32[]{:S(2)}) collective-permute-start(bf16[2,64,256]{2,1,0:T(8,128)(2,1)S(1)} %pad_maximum_fusion.1), channel_id=1, source_target_pairs={{0,4},{1,5},{2,6},{3,7},{4,0},{5,1},{6,2},{7,3},{8,12},{9,13},{10,... | collective-permute-start | bytes 196616 | tf_op jit(solution)/shard_map/ppermute | solution.py:332
  72.5 4.4 %collective-permute-start.10 = (bf16[2,64,256]{2,1,0:T(8,128)(2,1)S(1)}, bf16[2,64,256]{2,1,0:T(8,128)(2,1)S(1)}, u32[]{:S(2)}, u32[]{:S(2)}) collective-permute-start(bf16[2,64,256]{2,1,0:T(8,128)(2,1)S(1)} %pad_maximum_fusion.1), channel_id=1, source_target_pairs={{0,6},{1,7},{2,0},{3,1},{4,2},{5,3},{6,4},{7,5},{8,14},{9,15},{10,... | collective-permute-start | bytes 196616 | tf_op jit(solution)/shard_map/ppermute | solution.py:332
  74.1 4.7 %collective-permute-start.9 = (bf16[2,64,256]{2,1,0:T(8,128)(2,1)S(1)}, bf16[2,64,256]{2,1,0:T(8,128)(2,1)S(1)}, u32[]{:S(2)}, u32[]{:S(2)}) collective-permute-start(bf16[2,64,256]{2,1,0:T(8,128)(2,1)S(1)} %pad_maximum_fusion.1), channel_id=1, source_target_pairs={{0,2},{1,3},{2,4},{3,5},{4,6},{5,7},{6,0},{7,1},{8,10},{9,11},{10,... | collective-permute-start | bytes 196616 | tf_op jit(solution)/shard_map/ppermute | solution.py:332
  85.1 7.4 %collective-permute-start.12 = (f32[4,72,256]{2,1,0:T(8,128)S(1)}, f32[4,72,256]{2,1,0:T(8,128)S(1)}, u32[]{:S(2)}, u32[]{:S(2)}) collective-permute-start(f32[4,72,256]{2,1,0:T(8,128)S(1)} %get-tuple-element.39), channel_id=1, source_target_pairs={{0,1},{1,0},{2,3},{3,2},{4,5},{5,4},{6,7},{7,6},{8,9},{9,8},{10,11... | collective-permute-start | bytes 884744 | tf_op jit(solution)/shard_map/ppermute | solution.py:349
  88.0 14.6 %all-to-all-start.4 = ((bf16[16,64,256]{2,1,0:T(8,128)(2,1)}), bf16[16,64,256]{2,1,0:T(8,128)(2,1)S(1)}, u32[]{:S(2)}, u32[]{:S(2)}) async-start(bf16[16,64,256]{2,1,0:T(8,128)(2,1)} %get-tuple-element.37), calls=%async_computation.4 | async-start | bytes 1048576 | tf_op jit(solution)/shard_map/all_to_all | solution.py:348
  92.6 5.1 %collective-permute-start.15 = (f32[72,256]{1,0:T(8,128)S(1)}, f32[72,256]{1,0:T(8,128)S(1)}, u32[]{:S(2)}, u32[]{:S(2)}) collective-permute-start(f32[72,256]{1,0:T(8,128)S(1)} %get-tuple-element.54), channel_id=1, source_target_pairs={{0,4},{1,5},{2,6},{3,7},{4,0},{5,1},{6,2},{7,3},{8,12},{9,13},{10,... | collective-permute-start | bytes 221192 | tf_op jit(solution)/shard_map/ppermute | solution.py:351
  92.7 5.0 %collective-permute-start.14 = (f32[72,256]{1,0:T(8,128)S(1)}, f32[72,256]{1,0:T(8,128)S(1)}, u32[]{:S(2)}, u32[]{:S(2)}) collective-permute-start(f32[72,256]{1,0:T(8,128)S(1)} %get-tuple-element.55), channel_id=1, source_target_pairs={{0,6},{1,7},{2,0},{3,1},{4,2},{5,3},{6,4},{7,5},{8,14},{9,15},{10,... | collective-permute-start | bytes 221192 | tf_op jit(solution)/shard_map/ppermute | solution.py:351
  93.8 5.7 %collective-permute-start.13 = (f32[72,256]{1,0:T(8,128)S(1)}, f32[72,256]{1,0:T(8,128)S(1)}, u32[]{:S(2)}, u32[]{:S(2)}) collective-permute-start(f32[72,256]{1,0:T(8,128)S(1)} %get-tuple-element.56), channel_id=1, source_target_pairs={{0,2},{1,3},{2,4},{3,5},{4,6},{5,7},{6,0},{7,1},{8,10},{9,11},{10,... | collective-permute-start | bytes 221192 | tf_op jit(solution)/shard_map/ppermute | solution.py:351
  103.9 14.7 %all-to-all-start.5 = ((bf16[16,72,256]{2,1,0:T(8,128)(2,1)}), bf16[16,72,256]{2,1,0:T(8,128)(2,1)S(1)}, u32[]{:S(2)}, u32[]{:S(2)}) async-start(bf16[16,72,256]{2,1,0:T(8,128)(2,1)} %get-tuple-element.42), calls=%async_computation.5 | async-start | bytes 1179648 | tf_op jit(solution)/shard_map/all_to_all | solution.py:333
  108.2 2.5 %collective-permute-start.16 = (bf16[64,256]{1,0:T(8,128)(2,1)S(1)}, bf16[64,256]{1,0:T(8,128)(2,1)S(1)}, u32[]{:S(2)}, u32[]{:S(2)}) collective-permute-start(bf16[64,256]{1,0:T(8,128)(2,1)S(1)} %get-tuple-element.43.own), channel_id=1, source_target_pairs={{0,1},{1,0},{2,3},{3,2},{4,5},{5,4},{6,7},{7,6},{8,9},{9,8},{10,11... | collective-permute-start | bytes 98312 | tf_op jit(solution)/shard_map/ppermute | solution.py:330
  110.7 4.7 %collective-permute-start.19 = (bf16[2,64,256]{2,1,0:T(8,128)(2,1)S(1)}, bf16[2,64,256]{2,1,0:T(8,128)(2,1)S(1)}, u32[]{:S(2)}, u32[]{:S(2)}) collective-permute-start(bf16[2,64,256]{2,1,0:T(8,128)(2,1)S(1)} %pad_maximum_fusion.2), channel_id=1, source_target_pairs={{0,4},{1,5},{2,6},{3,7},{4,0},{5,1},{6,2},{7,3},{8,12},{9,13},{10,... | collective-permute-start | bytes 196616 | tf_op jit(solution)/shard_map/ppermute | solution.py:332
  110.8 4.6 %collective-permute-start.18 = (bf16[2,64,256]{2,1,0:T(8,128)(2,1)S(1)}, bf16[2,64,256]{2,1,0:T(8,128)(2,1)S(1)}, u32[]{:S(2)}, u32[]{:S(2)}) collective-permute-start(bf16[2,64,256]{2,1,0:T(8,128)(2,1)S(1)} %pad_maximum_fusion.2), channel_id=1, source_target_pairs={{0,6},{1,7},{2,0},{3,1},{4,2},{5,3},{6,4},{7,5},{8,14},{9,15},{10,... | collective-permute-start | bytes 196616 | tf_op jit(solution)/shard_map/ppermute | solution.py:332
  111.8 5.3 %collective-permute-start.17 = (bf16[2,64,256]{2,1,0:T(8,128)(2,1)S(1)}, bf16[2,64,256]{2,1,0:T(8,128)(2,1)S(1)}, u32[]{:S(2)}, u32[]{:S(2)}) collective-permute-start(bf16[2,64,256]{2,1,0:T(8,128)(2,1)S(1)} %pad_maximum_fusion.2), channel_id=1, source_target_pairs={{0,2},{1,3},{2,4},{3,5},{4,6},{5,7},{6,0},{7,1},{8,10},{9,11},{10,... | collective-permute-start | bytes 196616 | tf_op jit(solution)/shard_map/ppermute | solution.py:332
  123.6 6.6 %collective-permute-start.20 = (f32[4,72,256]{2,1,0:T(8,128)S(1)}, f32[4,72,256]{2,1,0:T(8,128)S(1)}, u32[]{:S(2)}, u32[]{:S(2)}) collective-permute-start(f32[4,72,256]{2,1,0:T(8,128)S(1)} %get-tuple-element.46), channel_id=1, source_target_pairs={{0,1},{1,0},{2,3},{3,2},{4,5},{5,4},{6,7},{7,6},{8,9},{9,8},{10,11... | collective-permute-start | bytes 884744 | tf_op jit(solution)/shard_map/ppermute | solution.py:349
  126.5 13.8 %all-to-all-start.6 = ((bf16[16,64,256]{2,1,0:T(8,128)(2,1)}), bf16[16,64,256]{2,1,0:T(8,128)(2,1)S(1)}, u32[]{:S(2)}, u32[]{:S(2)}) async-start(bf16[16,64,256]{2,1,0:T(8,128)(2,1)} %get-tuple-element.44), calls=%async_computation.6 | async-start | bytes 1048576 | tf_op jit(solution)/shard_map/all_to_all | solution.py:348
  130.3 5.1 %collective-permute-start.23 = (f32[72,256]{1,0:T(8,128)S(1)}, f32[72,256]{1,0:T(8,128)S(1)}, u32[]{:S(2)}, u32[]{:S(2)}) collective-permute-start(f32[72,256]{1,0:T(8,128)S(1)} %get-tuple-element.50), channel_id=1, source_target_pairs={{0,4},{1,5},{2,6},{3,7},{4,0},{5,1},{6,2},{7,3},{8,12},{9,13},{10,... | collective-permute-start | bytes 221192 | tf_op jit(solution)/shard_map/ppermute | solution.py:351
  130.8 4.8 %collective-permute-start.22 = (f32[72,256]{1,0:T(8,128)S(1)}, f32[72,256]{1,0:T(8,128)S(1)}, u32[]{:S(2)}, u32[]{:S(2)}) collective-permute-start(f32[72,256]{1,0:T(8,128)S(1)} %get-tuple-element.51), channel_id=1, source_target_pairs={{0,6},{1,7},{2,0},{3,1},{4,2},{5,3},{6,4},{7,5},{8,14},{9,15},{10,... | collective-permute-start | bytes 221192 | tf_op jit(solution)/shard_map/ppermute | solution.py:351
  131.8 5.2 %collective-permute-start.21 = (f32[72,256]{1,0:T(8,128)S(1)}, f32[72,256]{1,0:T(8,128)S(1)}, u32[]{:S(2)}, u32[]{:S(2)}) collective-permute-start(f32[72,256]{1,0:T(8,128)S(1)} %get-tuple-element.52), channel_id=1, source_target_pairs={{0,2},{1,3},{2,4},{3,5},{4,6},{5,7},{6,0},{7,1},{8,10},{9,11},{10,... | collective-permute-start | bytes 221192 | tf_op jit(solution)/shard_map/ppermute | solution.py:351

commit v5 on v4

--- a/solution.py
+++ b/solution.py
@@ -19,8 +19,9 @@
 SLOTS_OF = 64
 META = 128
 BACK = BF16
-CHUNK = 2
-KEPT = 3
+COUNTS = 40
+KEPT = 6
+FIRST = 2
 EXTRA = 8
 
 
@@ -69,7 +70,7 @@
 ):
     panels, slots, tile = stored.shape[0], stored.shape[1], stored.shape[2]
     row_devices = message.shape[0]
-    split = near.shape[0]
+    split, first = near.shape[0], near.shape[1]
     small = [
         pltpu.make_async_copy(stored_columns, columns, few.at[0]),
         pltpu.make_async_copy(stored_counts, counts, few.at[1]),
@@ -78,9 +79,11 @@
         copy.start()
     fetch = []
     for i in range(panels):
-        held = near.at[i] if i < split else far.at[i - split]
-        fetch.append(pltpu.make_async_copy(stored.at[i], held, arrived.at[i]))
-        fetch[i].start()
+        for h, part in enumerate((pl.ds(0, first), pl.ds(first, slots - first))):
+            held = near.at[i] if i < split and h == 0 else far.at[i, part]
+            fetch.append(pltpu.make_async_copy(stored.at[i, part], held, arrived.at[i, h]))
+    for copy in fetch:
+        copy.start()
     for copy in small:
         copy.wait()
     mine_row, mine_col = place[0], place[1]
@@ -89,6 +92,7 @@
     for b in range(row_devices):
         used[b] = 0
     for i in range(panels):
+        meta[COUNTS + i] = counts[0, i]
         for s in range(slots):
             q = i * slots + s
             b = columns[s, i]
@@ -100,13 +104,13 @@
     ones = jnp.ones((16, tile), BF16)
     for i in range(panels):
         if i % 2 == 0:
-            fetch[i].wait()
-            fetch[i + 1].wait()
+            for copy in fetch[2 * i : 2 * i + 4]:
+                copy.wait()
         total = jnp.zeros((16, tile), F32)
         for s in range(slots):
             live = s < counts[0, i]
             weight = jnp.where(live, ones, jnp.zeros_like(ones))
-            value = near[i, s] if i < split else far[i - split, s]
+            value = near[i, s] if i < split and s < first else far[i, s]
             total = total + nt(weight, value)
             wide = jnp.sum(value.astype(F32).reshape(tile // 8, 8, tile), axis=0)
             col_sums[i * slots + s] = jnp.where(live, wide, jnp.zeros_like(wide))
@@ -153,22 +157,29 @@
 
 def product_kernel(
     meta, near_tiles, stored, gathered, own, pair, far1, far3, far2, result, keep, give,
-    buffer, parts, far_tiles, arrived,
+    buffer, parts, totals, far_tiles, late_tiles, arrived, late,
 ):
-    split, slots = near_tiles.shape[0], near_tiles.shape[1]
-    panels = stored.shape[0]
+    split, first = near_tiles.shape[0], near_tiles.shape[1]
+    panels, slots = stored.shape[0], stored.shape[1]
     cells = own.shape[0]
-    fetch = {}
-    for first in range(split, panels, CHUNK):
-        last = min(first + CHUNK, panels)
-        fetch[first] = pltpu.make_async_copy(
-            stored.at[first:last],
-            far_tiles.at[first - split : last - split],
-            arrived.at[(first - split) // CHUNK],
-        )
-        fetch[first].start()
     zs = panels // 2
     z, core = meta[1] // 2, meta[1] % 2
+    fetch = []
+    for i in range(split, panels):
+        fetch.append(
+            pltpu.make_async_copy(
+                stored.at[i, pl.ds(0, first)], far_tiles.at[i - split], arrived.at[i - split]
+            )
+        )
+        fetch[-1].start()
+    later = []
+    for i in range(panels):
+        later.append(
+            pltpu.make_async_copy(
+                stored.at[i, pl.ds(first, slots - first)], late_tiles.at[i], late.at[i]
+            )
+        )
+        pl.when(meta[COUNTS + i] > first)(later[i].start)
     dots = jnp.zeros((8, 128), F32)
     for b in range(gathered.shape[0]):
         tail = gathered[b, cells:].astype(F32)
@@ -180,25 +191,39 @@
         other = pair[...] if source is None else source[1]
         buffer[2 * at + core] = same
         buffer[2 * at + 1 - core] = other
-    for at in range(zs):
-        k = (at + zs - z) % zs
-        totals = []
-        for i in (2 * at, 2 * at + 1):
-            if i in fetch:
-                fetch[i].wait()
-            tiles, row = (near_tiles, i) if i < split else (far_tiles, i - split)
-            mine = buffer[i]
-            total = None
-            for s in range(slots):
-                held = meta[COLUMNS + i * slots + s]
-                panel = gathered[held % EMPTY, :cells]
-                panel = jnp.where(held < EMPTY, panel, jnp.zeros_like(panel))
-                part = nt(panel, tiles[row, s])
-                total = part if total is None else total + part
-                parts[i * slots + s] = nn(mine, tiles[row, s])
-            totals.append(total)
-        keep[k, :cells] = jnp.where(core == 0, totals[0], totals[1])
-        give[k, :cells] = jnp.where(core == 0, totals[1], totals[0])
+
+    def multiply(i, s, value):
+        held = meta[COLUMNS + i * slots + s]
+        panel = gathered[held % EMPTY, :cells]
+        panel = jnp.where(held < EMPTY, panel, jnp.zeros_like(panel))
+        parts[i * slots + s] = nn(buffer[i], value)
+        return nt(panel, value)
+
+    for i in range(panels):
+        if i == split:
+            for copy in fetch:
+                copy.wait()
+        total = None
+        for s in range(first):
+            value = near_tiles[i, s] if i < split else far_tiles[i - split, s]
+            part = multiply(i, s, value)
+            total = part if total is None else total + part
+        totals[i] = total
+
+    for i in range(panels):
+
+        @pl.when(meta[COUNTS + i] > first)
+        def _():
+            later[i].wait()
+            total = totals[i]
+            for s in range(first, slots):
+                total = total + multiply(i, s, late_tiles[i, s - first])
+            totals[i] = total
+
+    for k in range(zs):
+        at = (z + k) % zs
+        keep[k, :cells] = totals[2 * at + core]
+        give[k, :cells] = totals[2 * at + 1 - core]
         keep[k, cells:] = dots
         give[k, cells:] = dots
     for b in range(result.shape[0]):
@@ -295,19 +320,19 @@
         (
             shape((rows, cols, tile + 128), F32),
             shape((META,), jnp.int32),
-            shape((KEPT, slots, tile, tile), BF16),
+            shape((KEPT, FIRST, tile, tile), BF16),
         ),
         [SMEM, HBM, HBM, HBM],
         (VMEM, SMEM, VMEM),
         [
-            pltpu.VMEM((panels - KEPT, slots, tile, tile), BF16),
+            pltpu.VMEM(tiles.shape, BF16),
             pltpu.SMEM((slots, panels), jnp.int32),
             pltpu.SMEM((1, panels), jnp.int32),
             pltpu.VMEM((panels, tile), F32),
             pltpu.VMEM((panels * slots, 8, tile), F32),
             pltpu.SMEM((rows,), jnp.int32),
             pltpu.SemaphoreType.DMA((2,)),
-            pltpu.SemaphoreType.DMA((panels,)),
+            pltpu.SemaphoreType.DMA((panels, 2)),
         ],
         work / 4,
         tile_bytes,
@@ -339,8 +364,11 @@
             scratch=[
                 pltpu.VMEM((panels, cells, tile), BF16),
                 pltpu.VMEM((panels * slots, cells, tile), F32),
-                pltpu.VMEM((panels - KEPT, slots, tile, tile), BF16),
-                pltpu.SemaphoreType.DMA((pl.cdiv(panels - KEPT, CHUNK),)),
+                pltpu.VMEM((panels, cells, tile), F32),
+                pltpu.VMEM((panels - KEPT, FIRST, tile, tile), BF16),
+                pltpu.VMEM((panels, slots - FIRST, tile, tile), BF16),
+                pltpu.SemaphoreType.DMA((panels - KEPT,)),
+                pltpu.SemaphoreType.DMA((panels,)),
             ],
             flops=2 * work,
             moved=tile_bytes,

time: 158 us -> 156 us (0.987)
  waiting for transfers between devices: 45.6 us -> 42.9 us
  starting transfers between devices: 49.1 us -> 51.3 us
    ppermute x9, waiting for transfers between devices: 14.6 us -> 13 us  [local(): lax.ppermute(sums[k], 'col', shift(k))]
  transfers between devices with their start and end apart: 30 -> 30, of which waited for: 22 -> 21; matrix products, arithmetic and copies ran while one was open for 0% -> 0% of each run, Pallas kernels for 0% -> 0%
where the time goes in v5:
time: 156 us; the launch traced here: 155 us
  starting transfers between devices  51.3 us (33%)
  waiting for transfers between devices  42.9 us (28%)
  blocking collectives  36.7 us (24%)
  Pallas kernels  22.7 us (15%)
    all_to_all x1, blocking collectives, local(): lax.all_to_all(message.reshape(rows * cols, tile + 128), ('row', 'col'),...  21.7 us
    all_to_all x1, blocking collectives, local(): norms = lax.all_to_all(norms, ('row', 'col'), 0, 0, tiled=True)  15 us
    pallas_call x3, Pallas kernels, local(): call(product_kernel, (shape((rows, cells, tile), BACK), side_shape, side_...  14 us
    all_to_all x3, starting transfers between devices, local(): back = lax.all_to_all(back, 'row', 0, 0, tiled=True)  13.2 us
    ppermute x9, waiting for transfers between devices, local(): near = [lax.ppermute(both, 'col', shift(k)) for k in (1, 3, 2)]  13 us
    ppermute x9, waiting for transfers between devices, local(): lax.ppermute(sums[k], 'col', shift(k))  13 us
    all_to_all x3, starting transfers between devices, local(): gathered = lax.all_to_all(many, 'row', 0, 0, tiled=True)  12.3 us
    all_to_all x3, waiting for transfers between devices, local(): back = lax.all_to_all(back, 'row', 0, 0, tiled=True)  9.93 us
  transfers between devices with their start and end apart: 30, of which 21 were waited for; matrix products, arithmetic and copies ran while one was open for 0% of the time, Pallas kernels for 0%

profile of v5, /device:TPU:1, one launch (start us, length us, event | category | flops | bytes accessed | tf_op | source)
XLA Modules:
  0.0 154.9 jit_solution(4969949820197524205)
XLA Ops:
  0.7 4.0 %shard_map.59 = (f32[16,8,384]{2,1,0:T(8,128)S(1)}, s32[128]{0:T(128)S(1)}, bf16[6,2,256,256]{3,2,1,0:T(8,128)(2,1)S(1)}) custom-call(s32[2]{0:T(128)S(1)} %pad_add_fusion.place, s32[4,8]{1,0:T(4,128)} %bitcast.60, s32[1,8]{1,0:T(1,128)} %bitcast.61, bf16[8,4,256,256]{3,2,1,0:T(8,128)(2,1)} %bitcast.56), custom_call_target="tpu_custom_call" | custom-call | flops 67108864 | bytes 4194304 | tf_op jit(solution)/shard_map/pallas_call | solution.py:318
  5.0 21.7 %all_to_all.52 = f32[128,1,384]{2,1,0:T(1,128)S(1)} all-to-all(f32[128,1,384]{2,1,0:T(1,128)S(1)} %copy.6), channel_id=1, replica_groups=mesh['row'=16,'col'=8] {'row','col'}, dimensions={0} | all-to-all | bytes 393216 | tf_op jit(solution)/shard_map/all_to_all | solution.py:340
  27.8 3.6 %all-to-all-start.1 = ((bf16[16,72,256]{2,1,0:T(8,128)(2,1)}), bf16[16,72,256]{2,1,0:T(8,128)(2,1)S(1)}, u32[]{:S(2)}, u32[]{:S(2)}) async-start(bf16[16,72,256]{2,1,0:T(8,128)(2,1)} %get-tuple-element.29), calls=%async_computation.1 | async-start | bytes 1179648 | tf_op jit(solution)/shard_map/all_to_all | solution.py:358
  34.1 1.8 %collective-permute-start.2 = (bf16[2,64,256]{2,1,0:T(8,128)(2,1)S(1)}, bf16[2,64,256]{2,1,0:T(8,128)(2,1)S(1)}, u32[]{:S(2)}, u32[]{:S(2)}) collective-permute-start(bf16[2,64,256]{2,1,0:T(8,128)(2,1)S(1)} %pad_maximum_fusion), channel_id=1, source_target_pairs={{0,6},{1,7},{2,0},{3,1},{4,2},{5,3},{6,4},{7,5},{8,14},{9,15},{10,... | collective-permute-start | bytes 196616 | tf_op jit(solution)/shard_map/ppermute | solution.py:357
  35.8 2.1 %collective-permute-done.3.far2 = bf16[2,64,256]{2,1,0:T(8,128)(2,1)S(1)} collective-permute-done((bf16[2,64,256]{2,1,0:T(8,128)(2,1)S(1)}, bf16[2,64,256]{2,1,0:T(8,128)(2,1)S(1)}, u32[]{:S(2)}, u32[]{:S(2)}) %collective-permute-start.3) | collective-permute-done | bytes 65568 | tf_op jit(solution)/shard_map/ppermute | solution.py:357
  37.9 2.5 %collective-permute-done.1.far1 = bf16[2,64,256]{2,1,0:T(8,128)(2,1)S(1)} collective-permute-done((bf16[2,64,256]{2,1,0:T(8,128)(2,1)S(1)}, bf16[2,64,256]{2,1,0:T(8,128)(2,1)S(1)}, u32[]{:S(2)}, u32[]{:S(2)}) %collective-permute-start.1) | collective-permute-done | bytes 65568 | tf_op jit(solution)/shard_map/ppermute | solution.py:357
  40.4 1.9 %all-to-all-done.1.gathered = bf16[16,72,256]{2,1,0:T(8,128)(2,1)S(1)} async-done(((bf16[16,72,256]{2,1,0:T(8,128)(2,1)}), bf16[16,72,256]{2,1,0:T(8,128)(2,1)S(1)}, u32[]{:S(2)}, u32[]{:S(2)}) %all-to-all-start.1) | async-done | bytes 589856 | tf_op jit(solution)/shard_map/all_to_all | solution.py:358
  42.3 4.7 %shard_map.61 = (bf16[16,64,256]{2,1,0:T(8,128)(2,1)}, f32[4,72,256]{2,1,0:T(8,128)S(1)}, f32[4,72,256]{2,1,0:T(8,128)S(1)}) custom-call(s32[128]{0:T(128)S(1)} %get-tuple-element.26.meta, bf16[6,2,256,256]{3,2,1,0:T(8,128)(2,1)S(1)} %get-tuple-element.27.near_tiles, bf16[8,4,256,256]{3,2,1,0:T(8,128)(2,1)} %bitcast.57, ...), custom_call_target="tpu_custom_call" | custom-call | flops 536870912 | bytes 4194304 | tf_op jit(solution)/shard_map/pallas_call | solution.py:360
  47.0 1.9 %collective-permute-start.4 = (f32[4,72,256]{2,1,0:T(8,128)S(1)}, f32[4,72,256]{2,1,0:T(8,128)S(1)}, u32[]{:S(2)}, u32[]{:S(2)}) collective-permute-start(f32[4,72,256]{2,1,0:T(8,128)S(1)} %get-tuple-element.33), channel_id=1, source_target_pairs={{0,1},{1,0},{2,3},{3,2},{4,5},{5,4},{6,7},{7,6},{8,9},{9,8},{10,11... | collective-permute-start | bytes 884744 | tf_op jit(solution)/shard_map/ppermute | solution.py:377
  48.9 4.5 %all-to-all-start.2 = ((bf16[16,64,256]{2,1,0:T(8,128)(2,1)}), bf16[16,64,256]{2,1,0:T(8,128)(2,1)S(1)}, u32[]{:S(2)}, u32[]{:S(2)}) async-start(bf16[16,64,256]{2,1,0:T(8,128)(2,1)} %get-tuple-element.31), calls=%async_computation.2 | async-start | bytes 1048576 | tf_op jit(solution)/shard_map/all_to_all | solution.py:376
  55.8 2.8 %collective-permute-done.7.far2 = f32[72,256]{1,0:T(8,128)S(1)} collective-permute-done((f32[72,256]{1,0:T(8,128)S(1)}, f32[72,256]{1,0:T(8,128)S(1)}, u32[]{:S(2)}, u32[]{:S(2)}) %collective-permute-start.7) | collective-permute-done | bytes 73760 | tf_op jit(solution)/shard_map/ppermute | solution.py:379
  60.1 3.4 %all-to-all-done.2.tile_sums = bf16[16,64,256]{2,1,0:T(8,128)(2,1)S(1)} async-done(((bf16[16,64,256]{2,1,0:T(8,128)(2,1)}), bf16[16,64,256]{2,1,0:T(8,128)(2,1)S(1)}, u32[]{:S(2)}, u32[]{:S(2)}) %all-to-all-start.2) | async-done | bytes 524320 | tf_op jit(solution)/shard_map/all_to_all | solution.py:376
  64.6 4.3 %all-to-all-start.3 = ((bf16[16,72,256]{2,1,0:T(8,128)(2,1)}), bf16[16,72,256]{2,1,0:T(8,128)(2,1)S(1)}, u32[]{:S(2)}, u32[]{:S(2)}) async-start(bf16[16,72,256]{2,1,0:T(8,128)(2,1)} %get-tuple-element.35), calls=%async_computation.3 | async-start | bytes 1179648 | tf_op jit(solution)/shard_map/all_to_all | solution.py:358
  69.0 1.6 %collective-permute-start.8 = (bf16[64,256]{1,0:T(8,128)(2,1)S(1)}, bf16[64,256]{1,0:T(8,128)(2,1)S(1)}, u32[]{:S(2)}, u32[]{:S(2)}) collective-permute-start(bf16[64,256]{1,0:T(8,128)(2,1)S(1)} %get-tuple-element.36.own), channel_id=1, source_target_pairs={{0,1},{1,0},{2,3},{3,2},{4,5},{5,4},{6,7},{7,6},{8,9},{9,8},{10,11... | collective-permute-start | bytes 98312 | tf_op jit(solution)/shard_map/ppermute | solution.py:355
  73.8 2.4 %collective-permute-done.11.far2 = bf16[2,64,256]{2,1,0:T(8,128)(2,1)S(1)} collective-permute-done((bf16[2,64,256]{2,1,0:T(8,128)(2,1)S(1)}, bf16[2,64,256]{2,1,0:T(8,128)(2,1)S(1)}, u32[]{:S(2)}, u32[]{:S(2)}) %collective-permute-start.11) | collective-permute-done | bytes 65568 | tf_op jit(solution)/shard_map/ppermute | solution.py:357
  76.1 1.8 %collective-permute-done.9.far1 = bf16[2,64,256]{2,1,0:T(8,128)(2,1)S(1)} collective-permute-done((bf16[2,64,256]{2,1,0:T(8,128)(2,1)S(1)}, bf16[2,64,256]{2,1,0:T(8,128)(2,1)S(1)}, u32[]{:S(2)}, u32[]{:S(2)}) %collective-permute-start.9) | collective-permute-done | bytes 65568 | tf_op jit(solution)/shard_map/ppermute | solution.py:357
  79.3 4.7 %shard_map.63 = (bf16[16,64,256]{2,1,0:T(8,128)(2,1)}, f32[4,72,256]{2,1,0:T(8,128)S(1)}, f32[4,72,256]{2,1,0:T(8,128)S(1)}) custom-call(s32[128]{0:T(128)S(1)} %get-tuple-element.26.meta, bf16[6,2,256,256]{3,2,1,0:T(8,128)(2,1)S(1)} %get-tuple-element.27.near_tiles, bf16[8,4,256,256]{3,2,1,0:T(8,128)(2,1)} %bitcast.58, ...), custom_call_target="tpu_custom_call" | custom-call | flops 536870912 | bytes 4194304 | tf_op jit(solution)/shard_map/pallas_call | solution.py:360
  84.0 2.6 %collective-permute-start.12 = (f32[4,72,256]{2,1,0:T(8,128)S(1)}, f32[4,72,256]{2,1,0:T(8,128)S(1)}, u32[]{:S(2)}, u32[]{:S(2)}) collective-permute-start(f32[4,72,256]{2,1,0:T(8,128)S(1)} %get-tuple-element.39), channel_id=1, source_target_pairs={{0,1},{1,0},{2,3},{3,2},{4,5},{5,4},{6,7},{7,6},{8,9},{9,8},{10,11... | collective-permute-start | bytes 884744 | tf_op jit(solution)/shard_map/ppermute | solution.py:377
  86.6 4.3 %all-to-all-start.4 = ((bf16[16,64,256]{2,1,0:T(8,128)(2,1)}), bf16[16,64,256]{2,1,0:T(8,128)(2,1)S(1)}, u32[]{:S(2)}, u32[]{:S(2)}) async-start(bf16[16,64,256]{2,1,0:T(8,128)(2,1)} %get-tuple-element.37), calls=%async_computation.4 | async-start | bytes 1048576 | tf_op jit(solution)/shard_map/all_to_all | solution.py:376
  93.4 2.7 %collective-permute-done.15.refs_4_ = f32[72,256]{1,0:T(8,128)S(1)} collective-permute-done((f32[72,256]{1,0:T(8,128)S(1)}, f32[72,256]{1,0:T(8,128)S(1)}, u32[]{:S(2)}, u32[]{:S(2)}) %collective-permute-start.15) | collective-permute-done | bytes 73760 | tf_op jit(solution)/shard_map/ppermute | solution.py:379
  96.1 1.6 %collective-permute-done.13.refs_2_ = f32[72,256]{1,0:T(8,128)S(1)} collective-permute-done((f32[72,256]{1,0:T(8,128)S(1)}, f32[72,256]{1,0:T(8,128)S(1)}, u32[]{:S(2)}, u32[]{:S(2)}) %collective-permute-start.13) | collective-permute-done | bytes 73760 | tf_op jit(solution)/shard_map/ppermute | solution.py:379
  97.7 3.3 %all-to-all-done.4.refs_0_ = bf16[16,64,256]{2,1,0:T(8,128)(2,1)S(1)} async-done(((bf16[16,64,256]{2,1,0:T(8,128)(2,1)}), bf16[16,64,256]{2,1,0:T(8,128)(2,1)S(1)}, u32[]{:S(2)}, u32[]{:S(2)}) %all-to-all-start.4) | async-done | bytes 524320 | tf_op jit(solution)/shard_map/all_to_all | solution.py:376
  102.2 4.3 %all-to-all-start.5 = ((bf16[16,72,256]{2,1,0:T(8,128)(2,1)}), bf16[16,72,256]{2,1,0:T(8,128)(2,1)S(1)}, u32[]{:S(2)}, u32[]{:S(2)}) async-start(bf16[16,72,256]{2,1,0:T(8,128)(2,1)} %get-tuple-element.42), calls=%async_computation.5 | async-start | bytes 1179648 | tf_op jit(solution)/shard_map/all_to_all | solution.py:358
  106.6 1.6 %collective-permute-start.16 = (bf16[64,256]{1,0:T(8,128)(2,1)S(1)}, bf16[64,256]{1,0:T(8,128)(2,1)S(1)}, u32[]{:S(2)}, u32[]{:S(2)}) collective-permute-start(bf16[64,256]{1,0:T(8,128)(2,1)S(1)} %get-tuple-element.43.own), channel_id=1, source_target_pairs={{0,1},{1,0},{2,3},{3,2},{4,5},{5,4},{6,7},{7,6},{8,9},{9,8},{10,11... | collective-permute-start | bytes 98312 | tf_op jit(solution)/shard_map/ppermute | solution.py:355
  111.5 2.2 %collective-permute-done.19.far2 = bf16[2,64,256]{2,1,0:T(8,128)(2,1)S(1)} collective-permute-done((bf16[2,64,256]{2,1,0:T(8,128)(2,1)S(1)}, bf16[2,64,256]{2,1,0:T(8,128)(2,1)S(1)}, u32[]{:S(2)}, u32[]{:S(2)}) %collective-permute-start.19) | collective-permute-done | bytes 65568 | tf_op jit(solution)/shard_map/ppermute | solution.py:357
  113.7 2.0 %collective-permute-done.17.far1 = bf16[2,64,256]{2,1,0:T(8,128)(2,1)S(1)} collective-permute-done((bf16[2,64,256]{2,1,0:T(8,128)(2,1)S(1)}, bf16[2,64,256]{2,1,0:T(8,128)(2,1)S(1)}, u32[]{:S(2)}, u32[]{:S(2)}) %collective-permute-start.17) | collective-permute-done | bytes 65568 | tf_op jit(solution)/shard_map/ppermute | solution.py:357
  116.9 4.7 %shard_map.65 = (bf16[16,64,256]{2,1,0:T(8,128)(2,1)}, f32[4,72,256]{2,1,0:T(8,128)S(1)}, f32[4,72,256]{2,1,0:T(8,128)S(1)}) custom-call(s32[128]{0:T(128)S(1)} %get-tuple-element.26.meta, bf16[6,2,256,256]{3,2,1,0:T(8,128)(2,1)S(1)} %get-tuple-element.27.near_tiles, bf16[8,4,256,256]{3,2,1,0:T(8,128)(2,1)} %bitcast.59, ...), custom_call_target="tpu_custom_call" | custom-call | flops 536870912 | bytes 4194304 | tf_op jit(solution)/shard_map/pallas_call | solution.py:360
  121.5 2.6 %collective-permute-start.20 = (f32[4,72,256]{2,1,0:T(8,128)S(1)}, f32[4,72,256]{2,1,0:T(8,128)S(1)}, u32[]{:S(2)}, u32[]{:S(2)}) collective-permute-start(f32[4,72,256]{2,1,0:T(8,128)S(1)} %get-tuple-element.46), channel_id=1, source_target_pairs={{0,1},{1,0},{2,3},{3,2},{4,5},{5,4},{6,7},{7,6},{8,9},{9,8},{10,11... | collective-permute-start | bytes 884744 | tf_op jit(solution)/shard_map/ppermute | solution.py:377
  124.1 4.5 %all-to-all-start.6 = ((bf16[16,64,256]{2,1,0:T(8,128)(2,1)}), bf16[16,64,256]{2,1,0:T(8,128)(2,1)S(1)}, u32[]{:S(2)}, u32[]{:S(2)}) async-start(bf16[16,64,256]{2,1,0:T(8,128)(2,1)} %get-tuple-element.44), calls=%async_computation.6 | async-start | bytes 1048576 | tf_op jit(solution)/shard_map/all_to_all | solution.py:376
  131.1 2.8 %collective-permute-done.23.refs_4_ = f32[72,256]{1,0:T(8,128)S(1)} collective-permute-done((f32[72,256]{1,0:T(8,128)S(1)}, f32[72,256]{1,0:T(8,128)S(1)}, u32[]{:S(2)}, u32[]{:S(2)}) %collective-permute-start.23) | collective-permute-done | bytes 73760 | tf_op jit(solution)/shard_map/ppermute | solution.py:379
  135.4 3.3 %all-to-all-done.6.refs_0_ = bf16[16,64,256]{2,1,0:T(8,128)(2,1)S(1)} async-done(((bf16[16,64,256]{2,1,0:T(8,128)(2,1)}), bf16[16,64,256]{2,1,0:T(8,128)(2,1)S(1)}, u32[]{:S(2)}, u32[]{:S(2)}) %all-to-all-start.6) | async-done | bytes 524320 | tf_op jit(solution)/shard_map/all_to_all | solution.py:376
  139.1 15.0 %all_to_all.53 = f32[128,1,128]{2,1,0:T(1,128)S(1)} all-to-all(f32[128,1,128]{2,1,0:T(1,128)S(1)} %bitcast.55), channel_id=1, replica_groups=mesh['row'=16,'col'=8] {'row','col'}, dimensions={0} | all-to-all | bytes 131072 | tf_op jit(solution)/shard_map/all_to_all | solution.py:399
  (53 shorter events, 27.1 us)
Async XLA Ops:
  0.6 26.0 %copy-start = (bf16[64,256]{1,0:T(8,128)(2,1)S(1)}, bf16[64,256]{1,0:T(8,128)(2,1)}, u32[]{:S(2)}) copy-start(bf16[64,256]{1,0:T(8,128)(2,1)} %refs_2_.1) | copy-start | bytes 98308
  27.8 14.5 %all-to-all-start.1 = ((bf16[16,72,256]{2,1,0:T(8,128)(2,1)}), bf16[16,72,256]{2,1,0:T(8,128)(2,1)S(1)}, u32[]{:S(2)}, u32[]{:S(2)}) async-start(bf16[16,72,256]{2,1,0:T(8,128)(2,1)} %get-tuple-element.29), calls=%async_computation.1 | async-start | bytes 1179648 | tf_op jit(solution)/shard_map/all_to_all | solution.py:358
  31.3 1.9 %collective-permute-start = (bf16[64,256]{1,0:T(8,128)(2,1)S(1)}, bf16[64,256]{1,0:T(8,128)(2,1)S(1)}, u32[]{:S(2)}, u32[]{:S(2)}) collective-permute-start(bf16[64,256]{1,0:T(8,128)(2,1)S(1)} %get-tuple-element.30.own), channel_id=1, source_target_pairs={{0,1},{1,0},{2,3},{3,2},{4,5},{5,4},{6,7},{7,6},{8,9},{9,8},{10,11... | collective-permute-start | bytes 98312 | tf_op jit(solution)/shard_map/ppermute | solution.py:355
  33.2 4.7 %collective-permute-start.3 = (bf16[2,64,256]{2,1,0:T(8,128)(2,1)S(1)}, bf16[2,64,256]{2,1,0:T(8,128)(2,1)S(1)}, u32[]{:S(2)}, u32[]{:S(2)}) collective-permute-start(bf16[2,64,256]{2,1,0:T(8,128)(2,1)S(1)} %pad_maximum_fusion), channel_id=1, source_target_pairs={{0,4},{1,5},{2,6},{3,7},{4,0},{5,1},{6,2},{7,3},{8,12},{9,13},{10,... | collective-permute-start | bytes 196616 | tf_op jit(solution)/shard_map/ppermute | solution.py:357
  34.1 3.8 %collective-permute-start.2 = (bf16[2,64,256]{2,1,0:T(8,128)(2,1)S(1)}, bf16[2,64,256]{2,1,0:T(8,128)(2,1)S(1)}, u32[]{:S(2)}, u32[]{:S(2)}) collective-permute-start(bf16[2,64,256]{2,1,0:T(8,128)(2,1)S(1)} %pad_maximum_fusion), channel_id=1, source_target_pairs={{0,6},{1,7},{2,0},{3,1},{4,2},{5,3},{6,4},{7,5},{8,14},{9,15},{10,... | collective-permute-start | bytes 196616 | tf_op jit(solution)/shard_map/ppermute | solution.py:357
  35.8 4.6 %collective-permute-start.1 = (bf16[2,64,256]{2,1,0:T(8,128)(2,1)S(1)}, bf16[2,64,256]{2,1,0:T(8,128)(2,1)S(1)}, u32[]{:S(2)}, u32[]{:S(2)}) collective-permute-start(bf16[2,64,256]{2,1,0:T(8,128)(2,1)S(1)} %pad_maximum_fusion), channel_id=1, source_target_pairs={{0,2},{1,3},{2,4},{3,5},{4,6},{5,7},{6,0},{7,1},{8,10},{9,11},{10,... | collective-permute-start | bytes 196616 | tf_op jit(solution)/shard_map/ppermute | solution.py:357
  47.0 6.4 %collective-permute-start.4 = (f32[4,72,256]{2,1,0:T(8,128)S(1)}, f32[4,72,256]{2,1,0:T(8,128)S(1)}, u32[]{:S(2)}, u32[]{:S(2)}) collective-permute-start(f32[4,72,256]{2,1,0:T(8,128)S(1)} %get-tuple-element.33), channel_id=1, source_target_pairs={{0,1},{1,0},{2,3},{3,2},{4,5},{5,4},{6,7},{7,6},{8,9},{9,8},{10,11... | collective-permute-start | bytes 884744 | tf_op jit(solution)/shard_map/ppermute | solution.py:377
  48.9 14.6 %all-to-all-start.2 = ((bf16[16,64,256]{2,1,0:T(8,128)(2,1)}), bf16[16,64,256]{2,1,0:T(8,128)(2,1)S(1)}, u32[]{:S(2)}, u32[]{:S(2)}) async-start(bf16[16,64,256]{2,1,0:T(8,128)(2,1)} %get-tuple-element.31), calls=%async_computation.2 | async-start | bytes 1048576 | tf_op jit(solution)/shard_map/all_to_all | solution.py:376
  53.5 5.1 %collective-permute-start.7 = (f32[72,256]{1,0:T(8,128)S(1)}, f32[72,256]{1,0:T(8,128)S(1)}, u32[]{:S(2)}, u32[]{:S(2)}) collective-permute-start(f32[72,256]{1,0:T(8,128)S(1)} %get-tuple-element.58), channel_id=1, source_target_pairs={{0,4},{1,5},{2,6},{3,7},{4,0},{5,1},{6,2},{7,3},{8,12},{9,13},{10,... | collective-permute-start | bytes 221192 | tf_op jit(solution)/shard_map/ppermute | solution.py:379
  54.3 4.3 %collective-permute-start.6 = (f32[72,256]{1,0:T(8,128)S(1)}, f32[72,256]{1,0:T(8,128)S(1)}, u32[]{:S(2)}, u32[]{:S(2)}) collective-permute-start(f32[72,256]{1,0:T(8,128)S(1)} %get-tuple-element.59), channel_id=1, source_target_pairs={{0,6},{1,7},{2,0},{3,1},{4,2},{5,3},{6,4},{7,5},{8,14},{9,15},{10,... | collective-permute-start | bytes 221192 | tf_op jit(solution)/shard_map/ppermute | solution.py:379
  55.3 4.8 %collective-permute-start.5 = (f32[72,256]{1,0:T(8,128)S(1)}, f32[72,256]{1,0:T(8,128)S(1)}, u32[]{:S(2)}, u32[]{:S(2)}) collective-permute-start(f32[72,256]{1,0:T(8,128)S(1)} %get-tuple-element.60), channel_id=1, source_target_pairs={{0,2},{1,3},{2,4},{3,5},{4,6},{5,7},{6,0},{7,1},{8,10},{9,11},{10,... | collective-permute-start | bytes 221192 | tf_op jit(solution)/shard_map/ppermute | solution.py:379
  64.6 14.7 %all-to-all-start.3 = ((bf16[16,72,256]{2,1,0:T(8,128)(2,1)}), bf16[16,72,256]{2,1,0:T(8,128)(2,1)S(1)}, u32[]{:S(2)}, u32[]{:S(2)}) async-start(bf16[16,72,256]{2,1,0:T(8,128)(2,1)} %get-tuple-element.35), calls=%async_computation.3 | async-start | bytes 1179648 | tf_op jit(solution)/shard_map/all_to_all | solution.py:358
  69.0 2.5 %collective-permute-start.8 = (bf16[64,256]{1,0:T(8,128)(2,1)S(1)}, bf16[64,256]{1,0:T(8,128)(2,1)S(1)}, u32[]{:S(2)}, u32[]{:S(2)}) collective-permute-start(bf16[64,256]{1,0:T(8,128)(2,1)S(1)} %get-tuple-element.36.own), channel_id=1, source_target_pairs={{0,1},{1,0},{2,3},{3,2},{4,5},{5,4},{6,7},{7,6},{8,9},{9,8},{10,11... | collective-permute-start | bytes 98312 | tf_op jit(solution)/shard_map/ppermute | solution.py:355
  71.5 4.7 %collective-permute-start.11 = (bf16[2,64,256]{2,1,0:T(8,128)(2,1)S(1)}, bf16[2,64,256]{2,1,0:T(8,128)(2,1)S(1)}, u32[]{:S(2)}, u32[]{:S(2)}) collective-permute-start(bf16[2,64,256]{2,1,0:T(8,128)(2,1)S(1)} %pad_maximum_fusion.1), channel_id=1, source_target_pairs={{0,4},{1,5},{2,6},{3,7},{4,0},{5,1},{6,2},{7,3},{8,12},{9,13},{10,... | collective-permute-start | bytes 196616 | tf_op jit(solution)/shard_map/ppermute | solution.py:357
  72.3 3.8 %collective-permute-start.10 = (bf16[2,64,256]{2,1,0:T(8,128)(2,1)S(1)}, bf16[2,64,256]{2,1,0:T(8,128)(2,1)S(1)}, u32[]{:S(2)}, u32[]{:S(2)}) collective-permute-start(bf16[2,64,256]{2,1,0:T(8,128)(2,1)S(1)} %pad_maximum_fusion.1), channel_id=1, source_target_pairs={{0,6},{1,7},{2,0},{3,1},{4,2},{5,3},{6,4},{7,5},{8,14},{9,15},{10,... | collective-permute-start | bytes 196616 | tf_op jit(solution)/shard_map/ppermute | solution.py:357
  73.3 4.7 %collective-permute-start.9 = (bf16[2,64,256]{2,1,0:T(8,128)(2,1)S(1)}, bf16[2,64,256]{2,1,0:T(8,128)(2,1)S(1)}, u32[]{:S(2)}, u32[]{:S(2)}) collective-permute-start(bf16[2,64,256]{2,1,0:T(8,128)(2,1)S(1)} %pad_maximum_fusion.1), channel_id=1, source_target_pairs={{0,2},{1,3},{2,4},{3,5},{4,6},{5,7},{6,0},{7,1},{8,10},{9,11},{10,... | collective-permute-start | bytes 196616 | tf_op jit(solution)/shard_map/ppermute | solution.py:357
  84.0 6.9 %collective-permute-start.12 = (f32[4,72,256]{2,1,0:T(8,128)S(1)}, f32[4,72,256]{2,1,0:T(8,128)S(1)}, u32[]{:S(2)}, u32[]{:S(2)}) collective-permute-start(f32[4,72,256]{2,1,0:T(8,128)S(1)} %get-tuple-element.39), channel_id=1, source_target_pairs={{0,1},{1,0},{2,3},{3,2},{4,5},{5,4},{6,7},{7,6},{8,9},{9,8},{10,11... | collective-permute-start | bytes 884744 | tf_op jit(solution)/shard_map/ppermute | solution.py:377
  86.6 14.4 %all-to-all-start.4 = ((bf16[16,64,256]{2,1,0:T(8,128)(2,1)}), bf16[16,64,256]{2,1,0:T(8,128)(2,1)S(1)}, u32[]{:S(2)}, u32[]{:S(2)}) async-start(bf16[16,64,256]{2,1,0:T(8,128)(2,1)} %get-tuple-element.37), calls=%async_computation.4 | async-start | bytes 1048576 | tf_op jit(solution)/shard_map/all_to_all | solution.py:376
  90.9 5.1 %collective-permute-start.15 = (f32[72,256]{1,0:T(8,128)S(1)}, f32[72,256]{1,0:T(8,128)S(1)}, u32[]{:S(2)}, u32[]{:S(2)}) collective-permute-start(f32[72,256]{1,0:T(8,128)S(1)} %get-tuple-element.54), channel_id=1, source_target_pairs={{0,4},{1,5},{2,6},{3,7},{4,0},{5,1},{6,2},{7,3},{8,12},{9,13},{10,... | collective-permute-start | bytes 221192 | tf_op jit(solution)/shard_map/ppermute | solution.py:379
  91.9 4.1 %collective-permute-start.14 = (f32[72,256]{1,0:T(8,128)S(1)}, f32[72,256]{1,0:T(8,128)S(1)}, u32[]{:S(2)}, u32[]{:S(2)}) collective-permute-start(f32[72,256]{1,0:T(8,128)S(1)} %get-tuple-element.55), channel_id=1, source_target_pairs={{0,6},{1,7},{2,0},{3,1},{4,2},{5,3},{6,4},{7,5},{8,14},{9,15},{10,... | collective-permute-start | bytes 221192 | tf_op jit(solution)/shard_map/ppermute | solution.py:379
  93.0 4.7 %collective-permute-start.13 = (f32[72,256]{1,0:T(8,128)S(1)}, f32[72,256]{1,0:T(8,128)S(1)}, u32[]{:S(2)}, u32[]{:S(2)}) collective-permute-start(f32[72,256]{1,0:T(8,128)S(1)} %get-tuple-element.56), channel_id=1, source_target_pairs={{0,2},{1,3},{2,4},{3,5},{4,6},{5,7},{6,0},{7,1},{8,10},{9,11},{10,... | collective-permute-start | bytes 221192 | tf_op jit(solution)/shard_map/ppermute | solution.py:379
  102.2 14.7 %all-to-all-start.5 = ((bf16[16,72,256]{2,1,0:T(8,128)(2,1)}), bf16[16,72,256]{2,1,0:T(8,128)(2,1)S(1)}, u32[]{:S(2)}, u32[]{:S(2)}) async-start(bf16[16,72,256]{2,1,0:T(8,128)(2,1)} %get-tuple-element.42), calls=%async_computation.5 | async-start | bytes 1179648 | tf_op jit(solution)/shard_map/all_to_all | solution.py:358
  106.6 2.5 %collective-permute-start.16 = (bf16[64,256]{1,0:T(8,128)(2,1)S(1)}, bf16[64,256]{1,0:T(8,128)(2,1)S(1)}, u32[]{:S(2)}, u32[]{:S(2)}) collective-permute-start(bf16[64,256]{1,0:T(8,128)(2,1)S(1)} %get-tuple-element.43.own), channel_id=1, source_target_pairs={{0,1},{1,0},{2,3},{3,2},{4,5},{5,4},{6,7},{7,6},{8,9},{9,8},{10,11... | collective-permute-start | bytes 98312 | tf_op jit(solution)/shard_map/ppermute | solution.py:355
  109.0 4.7 %collective-permute-start.19 = (bf16[2,64,256]{2,1,0:T(8,128)(2,1)S(1)}, bf16[2,64,256]{2,1,0:T(8,128)(2,1)S(1)}, u32[]{:S(2)}, u32[]{:S(2)}) collective-permute-start(bf16[2,64,256]{2,1,0:T(8,128)(2,1)S(1)} %pad_maximum_fusion.2), channel_id=1, source_target_pairs={{0,4},{1,5},{2,6},{3,7},{4,0},{5,1},{6,2},{7,3},{8,12},{9,13},{10,... | collective-permute-start | bytes 196616 | tf_op jit(solution)/shard_map/ppermute | solution.py:357
  110.0 3.7 %collective-permute-start.18 = (bf16[2,64,256]{2,1,0:T(8,128)(2,1)S(1)}, bf16[2,64,256]{2,1,0:T(8,128)(2,1)S(1)}, u32[]{:S(2)}, u32[]{:S(2)}) collective-permute-start(bf16[2,64,256]{2,1,0:T(8,128)(2,1)S(1)} %pad_maximum_fusion.2), channel_id=1, source_target_pairs={{0,6},{1,7},{2,0},{3,1},{4,2},{5,3},{6,4},{7,5},{8,14},{9,15},{10,... | collective-permute-start | bytes 196616 | tf_op jit(solution)/shard_map/ppermute | solution.py:357
  111.0 4.6 %collective-permute-start.17 = (bf16[2,64,256]{2,1,0:T(8,128)(2,1)S(1)}, bf16[2,64,256]{2,1,0:T(8,128)(2,1)S(1)}, u32[]{:S(2)}, u32[]{:S(2)}) collective-permute-start(bf16[2,64,256]{2,1,0:T(8,128)(2,1)S(1)} %pad_maximum_fusion.2), channel_id=1, source_target_pairs={{0,2},{1,3},{2,4},{3,5},{4,6},{5,7},{6,0},{7,1},{8,10},{9,11},{10,... | collective-permute-start | bytes 196616 | tf_op jit(solution)/shard_map/ppermute | solution.py:357
  121.5 7.1 %collective-permute-start.20 = (f32[4,72,256]{2,1,0:T(8,128)S(1)}, f32[4,72,256]{2,1,0:T(8,128)S(1)}, u32[]{:S(2)}, u32[]{:S(2)}) collective-permute-start(f32[4,72,256]{2,1,0:T(8,128)S(1)} %get-tuple-element.46), channel_id=1, source_target_pairs={{0,1},{1,0},{2,3},{3,2},{4,5},{5,4},{6,7},{7,6},{8,9},{9,8},{10,11... | collective-permute-start | bytes 884744 | tf_op jit(solution)/shard_map/ppermute | solution.py:377
  124.1 14.6 %all-to-all-start.6 = ((bf16[16,64,256]{2,1,0:T(8,128)(2,1)}), bf16[16,64,256]{2,1,0:T(8,128)(2,1)S(1)}, u32[]{:S(2)}, u32[]{:S(2)}) async-start(bf16[16,64,256]{2,1,0:T(8,128)(2,1)} %get-tuple-element.44), calls=%async_computation.6 | async-start | bytes 1048576 | tf_op jit(solution)/shard_map/all_to_all | solution.py:376
  128.7 5.1 %collective-permute-start.23 = (f32[72,256]{1,0:T(8,128)S(1)}, f32[72,256]{1,0:T(8,128)S(1)}, u32[]{:S(2)}, u32[]{:S(2)}) collective-permute-start(f32[72,256]{1,0:T(8,128)S(1)} %get-tuple-element.50), channel_id=1, source_target_pairs={{0,4},{1,5},{2,6},{3,7},{4,0},{5,1},{6,2},{7,3},{8,12},{9,13},{10,... | collective-permute-start | bytes 221192 | tf_op jit(solution)/shard_map/ppermute | solution.py:379
  129.6 4.2 %collective-permute-start.22 = (f32[72,256]{1,0:T(8,128)S(1)}, f32[72,256]{1,0:T(8,128)S(1)}, u32[]{:S(2)}, u32[]{:S(2)}) collective-permute-start(f32[72,256]{1,0:T(8,128)S(1)} %get-tuple-element.51), channel_id=1, source_target_pairs={{0,6},{1,7},{2,0},{3,1},{4,2},{5,3},{6,4},{7,5},{8,14},{9,15},{10,... | collective-permute-start | bytes 221192 | tf_op jit(solution)/shard_map/ppermute | solution.py:379
  130.6 4.8 %collective-permute-start.21 = (f32[72,256]{1,0:T(8,128)S(1)}, f32[72,256]{1,0:T(8,128)S(1)}, u32[]{:S(2)}, u32[]{:S(2)}) collective-permute-start(f32[72,256]{1,0:T(8,128)S(1)} %get-tuple-element.52), channel_id=1, source_target_pairs={{0,2},{1,3},{2,4},{3,5},{4,6},{5,7},{6,0},{7,1},{8,10},{9,11},{10,... | collective-permute-start | bytes 221192 | tf_op jit(solution)/shard_map/ppermute | solution.py:379

commit v6 on v5

--- a/solution.py
+++ b/solution.py
@@ -20,7 +20,7 @@
 META = 128
 BACK = BF16
 COUNTS = 40
-KEPT = 6
+KEPT = 7
 FIRST = 2
 EXTRA = 8
 

time: 156 us -> 157 us (level); the launches traced: 155 us -> 158 us
  starting transfers between devices: 51.3 us -> 53.7 us
  other arithmetic: 0.22 us -> 2.14 us
    all_to_all x3, starting transfers between devices: 13.2 us -> 17.8 us  [local(): back = lax.all_to_all(back, 'row', 0, 0, tiled=True)]
    all_to_all x3, waiting for transfers between devices: 9.93 us -> 7.27 us  [local(): back = lax.all_to_all(back, 'row', 0, 0, tiled=True)]
    ppermute x9, waiting for transfers between devices: 13 us -> 15.1 us  [local(): lax.ppermute(sums[k], 'col', shift(k))]
    add x3, other arithmetic: 0.12 us -> 2.04 us  [local(): sums = keep + given]
  transfers between devices with their start and end apart: 30 -> 30, of which waited for: 21 -> 21; matrix products, arithmetic and copies ran while one was open for 0% -> 1% of each run, Pallas kernels for 0% -> 0%
where the time goes in v6:
time: 157 us; the launch traced here: 158 us
  starting transfers between devices  53.7 us (34%)
  waiting for transfers between devices  43.2 us (28%)
  blocking collectives  36.2 us (23%)
  Pallas kernels  21.2 us (14%)
  other arithmetic  2.14 us (1%)
    all_to_all x1, blocking collectives, local(): lax.all_to_all(message.reshape(rows * cols, tile + 128), ('row', 'col'),...  21.7 us
    all_to_all x3, starting transfers between devices, local(): back = lax.all_to_all(back, 'row', 0, 0, tiled=True)  17.8 us
    ppermute x9, waiting for transfers between devices, local(): lax.ppermute(sums[k], 'col', shift(k))  15.1 us
    all_to_all x1, blocking collectives, local(): norms = lax.all_to_all(norms, ('row', 'col'), 0, 0, tiled=True)  14.6 us
    ppermute x9, waiting for transfers between devices, local(): near = [lax.ppermute(both, 'col', shift(k)) for k in (1, 3, 2)]  13.8 us
    pallas_call x3, Pallas kernels, local(): call(product_kernel, (shape((rows, cells, tile), BACK), side_shape, side_...  12.5 us
    all_to_all x3, starting transfers between devices, local(): gathered = lax.all_to_all(many, 'row', 0, 0, tiled=True)  12.3 us
    all_to_all x3, waiting for transfers between devices, local(): back = lax.all_to_all(back, 'row', 0, 0, tiled=True)  7.27 us
  transfers between devices with their start and end apart: 30, of which 21 were waited for; matrix products, arithmetic and copies ran while one was open for 1% of the time, Pallas kernels for 0%

profile of v6, /device:TPU:1, one launch (start us, length us, event | category | flops | bytes accessed | tf_op | source)
XLA Modules:
  0.0 157.6 jit_solution(8016846450227450545)
XLA Ops:
  0.7 4.0 %shard_map.59 = (f32[16,8,384]{2,1,0:T(8,128)S(1)}, s32[128]{0:T(128)S(1)}, bf16[7,2,256,256]{3,2,1,0:T(8,128)(2,1)S(1)}) custom-call(s32[2]{0:T(128)S(1)} %pad_add_fusion.place, s32[4,8]{1,0:T(4,128)} %bitcast.60, s32[1,8]{1,0:T(1,128)} %bitcast.61, bf16[8,4,256,256]{3,2,1,0:T(8,128)(2,1)} %bitcast.56), custom_call_target="tpu_custom_call" | custom-call | flops 67108864 | bytes 4194304 | tf_op jit(solution)/shard_map/pallas_call | solution.py:318
  5.0 21.7 %all_to_all.52 = f32[128,1,384]{2,1,0:T(1,128)S(1)} all-to-all(f32[128,1,384]{2,1,0:T(1,128)S(1)} %copy.6), channel_id=1, replica_groups=mesh['row'=16,'col'=8] {'row','col'}, dimensions={0} | all-to-all | bytes 393216 | tf_op jit(solution)/shard_map/all_to_all | solution.py:340
  27.8 3.6 %all-to-all-start.1 = ((bf16[16,72,256]{2,1,0:T(8,128)(2,1)}), bf16[16,72,256]{2,1,0:T(8,128)(2,1)S(1)}, u32[]{:S(2)}, u32[]{:S(2)}) async-start(bf16[16,72,256]{2,1,0:T(8,128)(2,1)} %get-tuple-element.29), calls=%async_computation.1 | async-start | bytes 1179648 | tf_op jit(solution)/shard_map/all_to_all | solution.py:358
  34.0 1.8 %collective-permute-start.2 = (bf16[2,64,256]{2,1,0:T(8,128)(2,1)S(1)}, bf16[2,64,256]{2,1,0:T(8,128)(2,1)S(1)}, u32[]{:S(2)}, u32[]{:S(2)}) collective-permute-start(bf16[2,64,256]{2,1,0:T(8,128)(2,1)S(1)} %pad_maximum_fusion), channel_id=1, source_target_pairs={{0,6},{1,7},{2,0},{3,1},{4,2},{5,3},{6,4},{7,5},{8,14},{9,15},{10,... | collective-permute-start | bytes 196616 | tf_op jit(solution)/shard_map/ppermute | solution.py:357
  35.8 2.1 %collective-permute-done.3.far2 = bf16[2,64,256]{2,1,0:T(8,128)(2,1)S(1)} collective-permute-done((bf16[2,64,256]{2,1,0:T(8,128)(2,1)S(1)}, bf16[2,64,256]{2,1,0:T(8,128)(2,1)S(1)}, u32[]{:S(2)}, u32[]{:S(2)}) %collective-permute-start.3) | collective-permute-done | bytes 65568 | tf_op jit(solution)/shard_map/ppermute | solution.py:357
  37.9 2.5 %collective-permute-done.1.far1 = bf16[2,64,256]{2,1,0:T(8,128)(2,1)S(1)} collective-permute-done((bf16[2,64,256]{2,1,0:T(8,128)(2,1)S(1)}, bf16[2,64,256]{2,1,0:T(8,128)(2,1)S(1)}, u32[]{:S(2)}, u32[]{:S(2)}) %collective-permute-start.1) | collective-permute-done | bytes 65568 | tf_op jit(solution)/shard_map/ppermute | solution.py:357
  40.4 1.9 %all-to-all-done.1.gathered = bf16[16,72,256]{2,1,0:T(8,128)(2,1)S(1)} async-done(((bf16[16,72,256]{2,1,0:T(8,128)(2,1)}), bf16[16,72,256]{2,1,0:T(8,128)(2,1)S(1)}, u32[]{:S(2)}, u32[]{:S(2)}) %all-to-all-start.1) | async-done | bytes 589856 | tf_op jit(solution)/shard_map/all_to_all | solution.py:358
  42.3 4.2 %shard_map.61 = (bf16[16,64,256]{2,1,0:T(8,128)(2,1)}, f32[4,72,256]{2,1,0:T(8,128)S(1)}, f32[4,72,256]{2,1,0:T(8,128)S(1)}) custom-call(s32[128]{0:T(128)S(1)} %get-tuple-element.26.meta, bf16[7,2,256,256]{3,2,1,0:T(8,128)(2,1)S(1)} %get-tuple-element.27.near_tiles, bf16[8,4,256,256]{3,2,1,0:T(8,128)(2,1)} %bitcast.57, ...), custom_call_target="tpu_custom_call" | custom-call | flops 536870912 | bytes 4194304 | tf_op jit(solution)/shard_map/pallas_call | solution.py:360
  46.5 1.9 %collective-permute-start.4 = (f32[4,72,256]{2,1,0:T(8,128)S(1)}, f32[4,72,256]{2,1,0:T(8,128)}, u32[]{:S(2)}, u32[]{:S(2)}) collective-permute-start(f32[4,72,256]{2,1,0:T(8,128)S(1)} %get-tuple-element.33), channel_id=1, source_target_pairs={{0,1},{1,0},{2,3},{3,2},{4,5},{5,4},{6,7},{7,6},{8,9},{9,8},{10,11... | collective-permute-start | bytes 884744 | tf_op jit(solution)/shard_map/ppermute | solution.py:377
  48.4 6.0 %all-to-all-start.2 = ((bf16[16,64,256]{2,1,0:T(8,128)(2,1)}), bf16[16,64,256]{2,1,0:T(8,128)(2,1)S(1)}, u32[]{:S(2)}, u32[]{:S(2)}) async-start(bf16[16,64,256]{2,1,0:T(8,128)(2,1)} %get-tuple-element.31), calls=%async_computation.2 | async-start | bytes 1048576 | tf_op jit(solution)/shard_map/all_to_all | solution.py:376
  57.2 3.3 %collective-permute-done.7.far2 = f32[72,256]{1,0:T(8,128)S(1)} collective-permute-done((f32[72,256]{1,0:T(8,128)S(1)}, f32[72,256]{1,0:T(8,128)S(1)}, u32[]{:S(2)}, u32[]{:S(2)}) %collective-permute-start.7) | collective-permute-done | bytes 73760 | tf_op jit(solution)/shard_map/ppermute | solution.py:379
  60.5 1.7 %collective-permute-done.5.far1 = f32[72,256]{1,0:T(8,128)S(1)} collective-permute-done((f32[72,256]{1,0:T(8,128)S(1)}, f32[72,256]{1,0:T(8,128)S(1)}, u32[]{:S(2)}, u32[]{:S(2)}) %collective-permute-start.5) | collective-permute-done | bytes 73760 | tf_op jit(solution)/shard_map/ppermute | solution.py:379
  62.2 2.3 %all-to-all-done.2.tile_sums = bf16[16,64,256]{2,1,0:T(8,128)(2,1)S(1)} async-done(((bf16[16,64,256]{2,1,0:T(8,128)(2,1)}), bf16[16,64,256]{2,1,0:T(8,128)(2,1)S(1)}, u32[]{:S(2)}, u32[]{:S(2)}) %all-to-all-start.2) | async-done | bytes 524320 | tf_op jit(solution)/shard_map/all_to_all | solution.py:376
  65.6 4.3 %all-to-all-start.3 = ((bf16[16,72,256]{2,1,0:T(8,128)(2,1)}), bf16[16,72,256]{2,1,0:T(8,128)(2,1)S(1)}, u32[]{:S(2)}, u32[]{:S(2)}) async-start(bf16[16,72,256]{2,1,0:T(8,128)(2,1)} %get-tuple-element.35), calls=%async_computation.3 | async-start | bytes 1179648 | tf_op jit(solution)/shard_map/all_to_all | solution.py:358
  74.3 2.8 %collective-permute-done.11.far2 = bf16[2,64,256]{2,1,0:T(8,128)(2,1)S(1)} collective-permute-done((bf16[2,64,256]{2,1,0:T(8,128)(2,1)S(1)}, bf16[2,64,256]{2,1,0:T(8,128)(2,1)S(1)}, u32[]{:S(2)}, u32[]{:S(2)}) %collective-permute-start.11) | collective-permute-done | bytes 65568 | tf_op jit(solution)/shard_map/ppermute | solution.py:357
  77.1 1.8 %collective-permute-done.9.far1 = bf16[2,64,256]{2,1,0:T(8,128)(2,1)S(1)} collective-permute-done((bf16[2,64,256]{2,1,0:T(8,128)(2,1)S(1)}, bf16[2,64,256]{2,1,0:T(8,128)(2,1)S(1)}, u32[]{:S(2)}, u32[]{:S(2)}) %collective-permute-start.9) | collective-permute-done | bytes 65568 | tf_op jit(solution)/shard_map/ppermute | solution.py:357
  80.3 4.2 %shard_map.63 = (bf16[16,64,256]{2,1,0:T(8,128)(2,1)}, f32[4,72,256]{2,1,0:T(8,128)S(1)}, f32[4,72,256]{2,1,0:T(8,128)S(1)}) custom-call(s32[128]{0:T(128)S(1)} %get-tuple-element.26.meta, bf16[7,2,256,256]{3,2,1,0:T(8,128)(2,1)S(1)} %get-tuple-element.27.near_tiles, bf16[8,4,256,256]{3,2,1,0:T(8,128)(2,1)} %bitcast.58, ...), custom_call_target="tpu_custom_call" | custom-call | flops 536870912 | bytes 4194304 | tf_op jit(solution)/shard_map/pallas_call | solution.py:360
  84.5 2.6 %collective-permute-start.12 = (f32[4,72,256]{2,1,0:T(8,128)S(1)}, f32[4,72,256]{2,1,0:T(8,128)}, u32[]{:S(2)}, u32[]{:S(2)}) collective-permute-start(f32[4,72,256]{2,1,0:T(8,128)S(1)} %get-tuple-element.39), channel_id=1, source_target_pairs={{0,1},{1,0},{2,3},{3,2},{4,5},{5,4},{6,7},{7,6},{8,9},{9,8},{10,11... | collective-permute-start | bytes 884744 | tf_op jit(solution)/shard_map/ppermute | solution.py:377
  87.0 5.7 %all-to-all-start.4 = ((bf16[16,64,256]{2,1,0:T(8,128)(2,1)}), bf16[16,64,256]{2,1,0:T(8,128)(2,1)S(1)}, u32[]{:S(2)}, u32[]{:S(2)}) async-start(bf16[16,64,256]{2,1,0:T(8,128)(2,1)} %get-tuple-element.37), calls=%async_computation.4 | async-start | bytes 1048576 | tf_op jit(solution)/shard_map/all_to_all | solution.py:376
  96.0 3.0 %collective-permute-done.15.refs_4_ = f32[72,256]{1,0:T(8,128)S(1)} collective-permute-done((f32[72,256]{1,0:T(8,128)S(1)}, f32[72,256]{1,0:T(8,128)S(1)}, u32[]{:S(2)}, u32[]{:S(2)}) %collective-permute-start.15) | collective-permute-done | bytes 73760 | tf_op jit(solution)/shard_map/ppermute | solution.py:379
  98.9 1.9 %collective-permute-done.13.refs_2_ = f32[72,256]{1,0:T(8,128)S(1)} collective-permute-done((f32[72,256]{1,0:T(8,128)S(1)}, f32[72,256]{1,0:T(8,128)S(1)}, u32[]{:S(2)}, u32[]{:S(2)}) %collective-permute-start.13) | collective-permute-done | bytes 73760 | tf_op jit(solution)/shard_map/ppermute | solution.py:379
  100.8 2.1 %all-to-all-done.4.refs_0_ = bf16[16,64,256]{2,1,0:T(8,128)(2,1)S(1)} async-done(((bf16[16,64,256]{2,1,0:T(8,128)(2,1)}), bf16[16,64,256]{2,1,0:T(8,128)(2,1)S(1)}, u32[]{:S(2)}, u32[]{:S(2)}) %all-to-all-start.4) | async-done | bytes 524320 | tf_op jit(solution)/shard_map/all_to_all | solution.py:376
  104.1 4.3 %all-to-all-start.5 = ((bf16[16,72,256]{2,1,0:T(8,128)(2,1)}), bf16[16,72,256]{2,1,0:T(8,128)(2,1)S(1)}, u32[]{:S(2)}, u32[]{:S(2)}) async-start(bf16[16,72,256]{2,1,0:T(8,128)(2,1)} %get-tuple-element.42), calls=%async_computation.5 | async-start | bytes 1179648 | tf_op jit(solution)/shard_map/all_to_all | solution.py:358
  113.1 2.5 %collective-permute-done.19.far2 = bf16[2,64,256]{2,1,0:T(8,128)(2,1)S(1)} collective-permute-done((bf16[2,64,256]{2,1,0:T(8,128)(2,1)S(1)}, bf16[2,64,256]{2,1,0:T(8,128)(2,1)S(1)}, u32[]{:S(2)}, u32[]{:S(2)}) %collective-permute-start.19) | collective-permute-done | bytes 65568 | tf_op jit(solution)/shard_map/ppermute | solution.py:357
  115.6 2.0 %collective-permute-done.17.far1 = bf16[2,64,256]{2,1,0:T(8,128)(2,1)S(1)} collective-permute-done((bf16[2,64,256]{2,1,0:T(8,128)(2,1)S(1)}, bf16[2,64,256]{2,1,0:T(8,128)(2,1)S(1)}, u32[]{:S(2)}, u32[]{:S(2)}) %collective-permute-start.17) | collective-permute-done | bytes 65568 | tf_op jit(solution)/shard_map/ppermute | solution.py:357
  118.8 4.2 %shard_map.65 = (bf16[16,64,256]{2,1,0:T(8,128)(2,1)}, f32[4,72,256]{2,1,0:T(8,128)S(1)}, f32[4,72,256]{2,1,0:T(8,128)S(1)}) custom-call(s32[128]{0:T(128)S(1)} %get-tuple-element.26.meta, bf16[7,2,256,256]{3,2,1,0:T(8,128)(2,1)S(1)} %get-tuple-element.27.near_tiles, bf16[8,4,256,256]{3,2,1,0:T(8,128)(2,1)} %bitcast.59, ...), custom_call_target="tpu_custom_call" | custom-call | flops 536870912 | bytes 4194304 | tf_op jit(solution)/shard_map/pallas_call | solution.py:360
  123.0 2.6 %collective-permute-start.20 = (f32[4,72,256]{2,1,0:T(8,128)S(1)}, f32[4,72,256]{2,1,0:T(8,128)S(1)}, u32[]{:S(2)}, u32[]{:S(2)}) collective-permute-start(f32[4,72,256]{2,1,0:T(8,128)S(1)} %get-tuple-element.46), channel_id=1, source_target_pairs={{0,1},{1,0},{2,3},{3,2},{4,5},{5,4},{6,7},{7,6},{8,9},{9,8},{10,11... | collective-permute-start | bytes 884744 | tf_op jit(solution)/shard_map/ppermute | solution.py:377
  125.6 6.1 %all-to-all-start.6 = ((bf16[16,64,256]{2,1,0:T(8,128)(2,1)}), bf16[16,64,256]{2,1,0:T(8,128)(2,1)S(1)}, u32[]{:S(2)}, u32[]{:S(2)}) async-start(bf16[16,64,256]{2,1,0:T(8,128)(2,1)} %get-tuple-element.44), calls=%async_computation.6 | async-start | bytes 1048576 | tf_op jit(solution)/shard_map/all_to_all | solution.py:376
  133.5 3.3 %collective-permute-done.23.refs_4_ = f32[72,256]{1,0:T(8,128)S(1)} collective-permute-done((f32[72,256]{1,0:T(8,128)S(1)}, f32[72,256]{1,0:T(8,128)S(1)}, u32[]{:S(2)}, u32[]{:S(2)}) %collective-permute-start.23) | collective-permute-done | bytes 73760 | tf_op jit(solution)/shard_map/ppermute | solution.py:379
  136.9 2.0 %collective-permute-done.21.refs_2_ = f32[72,256]{1,0:T(8,128)S(1)} collective-permute-done((f32[72,256]{1,0:T(8,128)S(1)}, f32[72,256]{1,0:T(8,128)S(1)}, u32[]{:S(2)}, u32[]{:S(2)}) %collective-permute-start.21) | collective-permute-done | bytes 73760 | tf_op jit(solution)/shard_map/ppermute | solution.py:379
  138.9 2.9 %all-to-all-done.6.refs_0_ = bf16[16,64,256]{2,1,0:T(8,128)(2,1)S(1)} async-done(((bf16[16,64,256]{2,1,0:T(8,128)(2,1)}), bf16[16,64,256]{2,1,0:T(8,128)(2,1)S(1)}, u32[]{:S(2)}, u32[]{:S(2)}) %all-to-all-start.6) | async-done | bytes 524320 | tf_op jit(solution)/shard_map/all_to_all | solution.py:376
  142.2 14.6 %all_to_all.53 = f32[128,1,128]{2,1,0:T(1,128)S(1)} all-to-all(f32[128,1,128]{2,1,0:T(1,128)S(1)} %bitcast.55), channel_id=1, replica_groups=mesh['row'=16,'col'=8] {'row','col'}, dimensions={0} | all-to-all | bytes 131072 | tf_op jit(solution)/shard_map/all_to_all | solution.py:399
  (53 shorter events, 26.9 us)
Async XLA Ops:
  0.6 26.0 %copy-start = (bf16[64,256]{1,0:T(8,128)(2,1)S(1)}, bf16[64,256]{1,0:T(8,128)(2,1)}, u32[]{:S(2)}) copy-start(bf16[64,256]{1,0:T(8,128)(2,1)} %refs_2_.1) | copy-start | bytes 98308
  27.8 14.5 %all-to-all-start.1 = ((bf16[16,72,256]{2,1,0:T(8,128)(2,1)}), bf16[16,72,256]{2,1,0:T(8,128)(2,1)S(1)}, u32[]{:S(2)}, u32[]{:S(2)}) async-start(bf16[16,72,256]{2,1,0:T(8,128)(2,1)} %get-tuple-element.29), calls=%async_computation.1 | async-start | bytes 1179648 | tf_op jit(solution)/shard_map/all_to_all | solution.py:358
  31.3 1.9 %collective-permute-start = (bf16[64,256]{1,0:T(8,128)(2,1)S(1)}, bf16[64,256]{1,0:T(8,128)(2,1)S(1)}, u32[]{:S(2)}, u32[]{:S(2)}) collective-permute-start(bf16[64,256]{1,0:T(8,128)(2,1)S(1)} %get-tuple-element.30.own), channel_id=1, source_target_pairs={{0,1},{1,0},{2,3},{3,2},{4,5},{5,4},{6,7},{7,6},{8,9},{9,8},{10,11... | collective-permute-start | bytes 98312 | tf_op jit(solution)/shard_map/ppermute | solution.py:355
  33.2 4.7 %collective-permute-start.3 = (bf16[2,64,256]{2,1,0:T(8,128)(2,1)S(1)}, bf16[2,64,256]{2,1,0:T(8,128)(2,1)S(1)}, u32[]{:S(2)}, u32[]{:S(2)}) collective-permute-start(bf16[2,64,256]{2,1,0:T(8,128)(2,1)S(1)} %pad_maximum_fusion), channel_id=1, source_target_pairs={{0,4},{1,5},{2,6},{3,7},{4,0},{5,1},{6,2},{7,3},{8,12},{9,13},{10,... | collective-permute-start | bytes 196616 | tf_op jit(solution)/shard_map/ppermute | solution.py:357
  34.0 3.8 %collective-permute-start.2 = (bf16[2,64,256]{2,1,0:T(8,128)(2,1)S(1)}, bf16[2,64,256]{2,1,0:T(8,128)(2,1)S(1)}, u32[]{:S(2)}, u32[]{:S(2)}) collective-permute-start(bf16[2,64,256]{2,1,0:T(8,128)(2,1)S(1)} %pad_maximum_fusion), channel_id=1, source_target_pairs={{0,6},{1,7},{2,0},{3,1},{4,2},{5,3},{6,4},{7,5},{8,14},{9,15},{10,... | collective-permute-start | bytes 196616 | tf_op jit(solution)/shard_map/ppermute | solution.py:357
  35.8 4.6 %collective-permute-start.1 = (bf16[2,64,256]{2,1,0:T(8,128)(2,1)S(1)}, bf16[2,64,256]{2,1,0:T(8,128)(2,1)S(1)}, u32[]{:S(2)}, u32[]{:S(2)}) collective-permute-start(bf16[2,64,256]{2,1,0:T(8,128)(2,1)S(1)} %pad_maximum_fusion), channel_id=1, source_target_pairs={{0,2},{1,3},{2,4},{3,5},{4,6},{5,7},{6,0},{7,1},{8,10},{9,11},{10,... | collective-permute-start | bytes 196616 | tf_op jit(solution)/shard_map/ppermute | solution.py:357
  46.5 7.9 %collective-permute-start.4 = (f32[4,72,256]{2,1,0:T(8,128)S(1)}, f32[4,72,256]{2,1,0:T(8,128)}, u32[]{:S(2)}, u32[]{:S(2)}) collective-permute-start(f32[4,72,256]{2,1,0:T(8,128)S(1)} %get-tuple-element.33), channel_id=1, source_target_pairs={{0,1},{1,0},{2,3},{3,2},{4,5},{5,4},{6,7},{7,6},{8,9},{9,8},{10,11... | collective-permute-start | bytes 884744 | tf_op jit(solution)/shard_map/ppermute | solution.py:377
  48.4 16.1 %all-to-all-start.2 = ((bf16[16,64,256]{2,1,0:T(8,128)(2,1)}), bf16[16,64,256]{2,1,0:T(8,128)(2,1)S(1)}, u32[]{:S(2)}, u32[]{:S(2)}) async-start(bf16[16,64,256]{2,1,0:T(8,128)(2,1)} %get-tuple-element.31), calls=%async_computation.2 | async-start | bytes 1048576 | tf_op jit(solution)/shard_map/all_to_all | solution.py:376
  55.4 5.1 %collective-permute-start.7 = (f32[72,256]{1,0:T(8,128)S(1)}, f32[72,256]{1,0:T(8,128)S(1)}, u32[]{:S(2)}, u32[]{:S(2)}) collective-permute-start(f32[72,256]{1,0:T(8,128)S(1)} %get-tuple-element.58), channel_id=1, source_target_pairs={{0,4},{1,5},{2,6},{3,7},{4,0},{5,1},{6,2},{7,3},{8,12},{9,13},{10,... | collective-permute-start | bytes 221192 | tf_op jit(solution)/shard_map/ppermute | solution.py:379
  55.7 4.8 %collective-permute-start.6 = (f32[72,256]{1,0:T(8,128)S(1)}, f32[72,256]{1,0:T(8,128)S(1)}, u32[]{:S(2)}, u32[]{:S(2)}) collective-permute-start(f32[72,256]{1,0:T(8,128)S(1)} %get-tuple-element.59), channel_id=1, source_target_pairs={{0,6},{1,7},{2,0},{3,1},{4,2},{5,3},{6,4},{7,5},{8,14},{9,15},{10,... | collective-permute-start | bytes 221192 | tf_op jit(solution)/shard_map/ppermute | solution.py:379
  56.6 5.6 %collective-permute-start.5 = (f32[72,256]{1,0:T(8,128)S(1)}, f32[72,256]{1,0:T(8,128)S(1)}, u32[]{:S(2)}, u32[]{:S(2)}) collective-permute-start(f32[72,256]{1,0:T(8,128)S(1)} %get-tuple-element.60), channel_id=1, source_target_pairs={{0,2},{1,3},{2,4},{3,5},{4,6},{5,7},{6,0},{7,1},{8,10},{9,11},{10,... | collective-permute-start | bytes 221192 | tf_op jit(solution)/shard_map/ppermute | solution.py:379
  65.6 14.7 %all-to-all-start.3 = ((bf16[16,72,256]{2,1,0:T(8,128)(2,1)}), bf16[16,72,256]{2,1,0:T(8,128)(2,1)S(1)}, u32[]{:S(2)}, u32[]{:S(2)}) async-start(bf16[16,72,256]{2,1,0:T(8,128)(2,1)} %get-tuple-element.35), calls=%async_computation.3 | async-start | bytes 1179648 | tf_op jit(solution)/shard_map/all_to_all | solution.py:358
  70.0 2.5 %collective-permute-start.8 = (bf16[64,256]{1,0:T(8,128)(2,1)S(1)}, bf16[64,256]{1,0:T(8,128)(2,1)S(1)}, u32[]{:S(2)}, u32[]{:S(2)}) collective-permute-start(bf16[64,256]{1,0:T(8,128)(2,1)S(1)} %get-tuple-element.36.own), channel_id=1, source_target_pairs={{0,1},{1,0},{2,3},{3,2},{4,5},{5,4},{6,7},{7,6},{8,9},{9,8},{10,11... | collective-permute-start | bytes 98312 | tf_op jit(solution)/shard_map/ppermute | solution.py:355
  72.5 4.7 %collective-permute-start.11 = (bf16[2,64,256]{2,1,0:T(8,128)(2,1)S(1)}, bf16[2,64,256]{2,1,0:T(8,128)(2,1)S(1)}, u32[]{:S(2)}, u32[]{:S(2)}) collective-permute-start(bf16[2,64,256]{2,1,0:T(8,128)(2,1)S(1)} %pad_maximum_fusion.1), channel_id=1, source_target_pairs={{0,4},{1,5},{2,6},{3,7},{4,0},{5,1},{6,2},{7,3},{8,12},{9,13},{10,... | collective-permute-start | bytes 196616 | tf_op jit(solution)/shard_map/ppermute | solution.py:357
  72.8 4.3 %collective-permute-start.10 = (bf16[2,64,256]{2,1,0:T(8,128)(2,1)S(1)}, bf16[2,64,256]{2,1,0:T(8,128)(2,1)S(1)}, u32[]{:S(2)}, u32[]{:S(2)}) collective-permute-start(bf16[2,64,256]{2,1,0:T(8,128)(2,1)S(1)} %pad_maximum_fusion.1), channel_id=1, source_target_pairs={{0,6},{1,7},{2,0},{3,1},{4,2},{5,3},{6,4},{7,5},{8,14},{9,15},{10,... | collective-permute-start | bytes 196616 | tf_op jit(solution)/shard_map/ppermute | solution.py:357
  74.2 4.8 %collective-permute-start.9 = (bf16[2,64,256]{2,1,0:T(8,128)(2,1)S(1)}, bf16[2,64,256]{2,1,0:T(8,128)(2,1)S(1)}, u32[]{:S(2)}, u32[]{:S(2)}) collective-permute-start(bf16[2,64,256]{2,1,0:T(8,128)(2,1)S(1)} %pad_maximum_fusion.1), channel_id=1, source_target_pairs={{0,2},{1,3},{2,4},{3,5},{4,6},{5,7},{6,0},{7,1},{8,10},{9,11},{10,... | collective-permute-start | bytes 196616 | tf_op jit(solution)/shard_map/ppermute | solution.py:357
  84.5 8.3 %collective-permute-start.12 = (f32[4,72,256]{2,1,0:T(8,128)S(1)}, f32[4,72,256]{2,1,0:T(8,128)}, u32[]{:S(2)}, u32[]{:S(2)}) collective-permute-start(f32[4,72,256]{2,1,0:T(8,128)S(1)} %get-tuple-element.39), channel_id=1, source_target_pairs={{0,1},{1,0},{2,3},{3,2},{4,5},{5,4},{6,7},{7,6},{8,9},{9,8},{10,11... | collective-permute-start | bytes 884744 | tf_op jit(solution)/shard_map/ppermute | solution.py:377
  87.0 15.9 %all-to-all-start.4 = ((bf16[16,64,256]{2,1,0:T(8,128)(2,1)}), bf16[16,64,256]{2,1,0:T(8,128)(2,1)S(1)}, u32[]{:S(2)}, u32[]{:S(2)}) async-start(bf16[16,64,256]{2,1,0:T(8,128)(2,1)} %get-tuple-element.37), calls=%async_computation.4 | async-start | bytes 1048576 | tf_op jit(solution)/shard_map/all_to_all | solution.py:376
  93.8 5.1 %collective-permute-start.15 = (f32[72,256]{1,0:T(8,128)S(1)}, f32[72,256]{1,0:T(8,128)S(1)}, u32[]{:S(2)}, u32[]{:S(2)}) collective-permute-start(f32[72,256]{1,0:T(8,128)S(1)} %get-tuple-element.54), channel_id=1, source_target_pairs={{0,4},{1,5},{2,6},{3,7},{4,0},{5,1},{6,2},{7,3},{8,12},{9,13},{10,... | collective-permute-start | bytes 221192 | tf_op jit(solution)/shard_map/ppermute | solution.py:379
  94.5 4.4 %collective-permute-start.14 = (f32[72,256]{1,0:T(8,128)S(1)}, f32[72,256]{1,0:T(8,128)S(1)}, u32[]{:S(2)}, u32[]{:S(2)}) collective-permute-start(f32[72,256]{1,0:T(8,128)S(1)} %get-tuple-element.55), channel_id=1, source_target_pairs={{0,6},{1,7},{2,0},{3,1},{4,2},{5,3},{6,4},{7,5},{8,14},{9,15},{10,... | collective-permute-start | bytes 221192 | tf_op jit(solution)/shard_map/ppermute | solution.py:379
  94.8 5.9 %collective-permute-start.13 = (f32[72,256]{1,0:T(8,128)S(1)}, f32[72,256]{1,0:T(8,128)S(1)}, u32[]{:S(2)}, u32[]{:S(2)}) collective-permute-start(f32[72,256]{1,0:T(8,128)S(1)} %get-tuple-element.56), channel_id=1, source_target_pairs={{0,2},{1,3},{2,4},{3,5},{4,6},{5,7},{6,0},{7,1},{8,10},{9,11},{10,... | collective-permute-start | bytes 221192 | tf_op jit(solution)/shard_map/ppermute | solution.py:379
  104.1 14.7 %all-to-all-start.5 = ((bf16[16,72,256]{2,1,0:T(8,128)(2,1)}), bf16[16,72,256]{2,1,0:T(8,128)(2,1)S(1)}, u32[]{:S(2)}, u32[]{:S(2)}) async-start(bf16[16,72,256]{2,1,0:T(8,128)(2,1)} %get-tuple-element.42), calls=%async_computation.5 | async-start | bytes 1179648 | tf_op jit(solution)/shard_map/all_to_all | solution.py:358
  108.5 2.5 %collective-permute-start.16 = (bf16[64,256]{1,0:T(8,128)(2,1)S(1)}, bf16[64,256]{1,0:T(8,128)(2,1)S(1)}, u32[]{:S(2)}, u32[]{:S(2)}) collective-permute-start(bf16[64,256]{1,0:T(8,128)(2,1)S(1)} %get-tuple-element.43.own), channel_id=1, source_target_pairs={{0,1},{1,0},{2,3},{3,2},{4,5},{5,4},{6,7},{7,6},{8,9},{9,8},{10,11... | collective-permute-start | bytes 98312 | tf_op jit(solution)/shard_map/ppermute | solution.py:355
  111.0 4.7 %collective-permute-start.19 = (bf16[2,64,256]{2,1,0:T(8,128)(2,1)S(1)}, bf16[2,64,256]{2,1,0:T(8,128)(2,1)S(1)}, u32[]{:S(2)}, u32[]{:S(2)}) collective-permute-start(bf16[2,64,256]{2,1,0:T(8,128)(2,1)S(1)} %pad_maximum_fusion.2), channel_id=1, source_target_pairs={{0,4},{1,5},{2,6},{3,7},{4,0},{5,1},{6,2},{7,3},{8,12},{9,13},{10,... | collective-permute-start | bytes 196616 | tf_op jit(solution)/shard_map/ppermute | solution.py:357
  111.6 4.0 %collective-permute-start.18 = (bf16[2,64,256]{2,1,0:T(8,128)(2,1)S(1)}, bf16[2,64,256]{2,1,0:T(8,128)(2,1)S(1)}, u32[]{:S(2)}, u32[]{:S(2)}) collective-permute-start(bf16[2,64,256]{2,1,0:T(8,128)(2,1)S(1)} %pad_maximum_fusion.2), channel_id=1, source_target_pairs={{0,6},{1,7},{2,0},{3,1},{4,2},{5,3},{6,4},{7,5},{8,14},{9,15},{10,... | collective-permute-start | bytes 196616 | tf_op jit(solution)/shard_map/ppermute | solution.py:357
  113.0 4.6 %collective-permute-start.17 = (bf16[2,64,256]{2,1,0:T(8,128)(2,1)S(1)}, bf16[2,64,256]{2,1,0:T(8,128)(2,1)S(1)}, u32[]{:S(2)}, u32[]{:S(2)}) collective-permute-start(bf16[2,64,256]{2,1,0:T(8,128)(2,1)S(1)} %pad_maximum_fusion.2), channel_id=1, source_target_pairs={{0,2},{1,3},{2,4},{3,5},{4,6},{5,7},{6,0},{7,1},{8,10},{9,11},{10,... | collective-permute-start | bytes 196616 | tf_op jit(solution)/shard_map/ppermute | solution.py:357
  123.0 8.7 %collective-permute-start.20 = (f32[4,72,256]{2,1,0:T(8,128)S(1)}, f32[4,72,256]{2,1,0:T(8,128)S(1)}, u32[]{:S(2)}, u32[]{:S(2)}) collective-permute-start(f32[4,72,256]{2,1,0:T(8,128)S(1)} %get-tuple-element.46), channel_id=1, source_target_pairs={{0,1},{1,0},{2,3},{3,2},{4,5},{5,4},{6,7},{7,6},{8,9},{9,8},{10,11... | collective-permute-start | bytes 884744 | tf_op jit(solution)/shard_map/ppermute | solution.py:377
  125.6 16.2 %all-to-all-start.6 = ((bf16[16,64,256]{2,1,0:T(8,128)(2,1)}), bf16[16,64,256]{2,1,0:T(8,128)(2,1)S(1)}, u32[]{:S(2)}, u32[]{:S(2)}) async-start(bf16[16,64,256]{2,1,0:T(8,128)(2,1)} %get-tuple-element.44), calls=%async_computation.6 | async-start | bytes 1048576 | tf_op jit(solution)/shard_map/all_to_all | solution.py:376
  131.7 5.1 %collective-permute-start.23 = (f32[72,256]{1,0:T(8,128)S(1)}, f32[72,256]{1,0:T(8,128)S(1)}, u32[]{:S(2)}, u32[]{:S(2)}) collective-permute-start(f32[72,256]{1,0:T(8,128)S(1)} %get-tuple-element.50), channel_id=1, source_target_pairs={{0,4},{1,5},{2,6},{3,7},{4,0},{5,1},{6,2},{7,3},{8,12},{9,13},{10,... | collective-permute-start | bytes 221192 | tf_op jit(solution)/shard_map/ppermute | solution.py:379
  132.1 4.8 %collective-permute-start.22 = (f32[72,256]{1,0:T(8,128)S(1)}, f32[72,256]{1,0:T(8,128)S(1)}, u32[]{:S(2)}, u32[]{:S(2)}) collective-permute-start(f32[72,256]{1,0:T(8,128)S(1)} %get-tuple-element.51), channel_id=1, source_target_pairs={{0,6},{1,7},{2,0},{3,1},{4,2},{5,3},{6,4},{7,5},{8,14},{9,15},{10,... | collective-permute-start | bytes 221192 | tf_op jit(solution)/shard_map/ppermute | solution.py:379
  132.7 6.2 %collective-permute-start.21 = (f32[72,256]{1,0:T(8,128)S(1)}, f32[72,256]{1,0:T(8,128)S(1)}, u32[]{:S(2)}, u32[]{:S(2)}) collective-permute-start(f32[72,256]{1,0:T(8,128)S(1)} %get-tuple-element.52), channel_id=1, source_target_pairs={{0,2},{1,3},{2,4},{3,5},{4,6},{5,7},{6,0},{7,1},{8,10},{9,11},{10,... | collective-permute-start | bytes 221192 | tf_op jit(solution)/shard_map/ppermute | solution.py:379
